TPU v7x, 512 devices: a whole 4x8x8 slice. The times are simulated.
512 devices in a mesh: dp: 64 (over x, y, z_hi), expert: 8 (over z_lo, core).
Axes of the slice: x: 4, y: 8, z: 8 (z_hi: 2, z_lo: 4; z = z_hi * 4 + z_lo), core: 2. Of those that a mesh axis runs over, the one named last changes fastest.
Arguments:
- attn_out: bfloat16 [8192, 6144], P('dp', 'expert'), may hold values from -6 to 6
- out_cols: bfloat16 [8192, 1024], P('dp', 'expert'), may hold values from -1.25 to 1.25
- error_in: bfloat16 [64, 6144, 1024], P('dp', None, 'expert'), may hold values from -6 to 6
- power_q: float32 [1024, 64], P('expert'), may hold values from -0.1875 to 0.1875
- tokens: bfloat16 [65536, 6144], P(('dp', 'expert')), may hold values from -24 to 24
- routes: int32 [65536, 2], P(('dp', 'expert')), may hold values from 0 to 7, all different within a row; in each aligned block of 128 rows (0 to 127, 128 to 255, ...) at most 64 rows name the same one
- route_logits: float32 [65536, 2], P(('dp', 'expert')), may hold values from -6 to 6
- pair_score: float32 [65536, 2], P(('dp', 'expert')), may hold values from -0.5 to 0.5
Outputs:
- approx: bfloat16 [6144, 1024], P('dp', 'expert')
- q_new: float32 [1024, 64], P('expert')
- error_out: bfloat16 [64, 6144, 1024], P('dp', None, 'expert')
- expert_grad: float32 [8, 6144], P('expert', 'dp')
Inputs may be any that keep to these rules, and one draw needn't show every extreme that they name: `routes`: within the 128 rows of one device, no expert is named by more than 64 pairs, a bound that some block reaches; the two experts of a token differ.
All inputs are finite; a program needn't handle non-finite values.
Results may differ from a plain program's by a relative error of at most 0.0027.
Values may be sent and summed in bfloat16 or wider, within the bound.
No kernel may reach another device: no remote copies, remote signals or barrier semaphores. Data moves between devices by JAX's collectives and lax.ppermute only.
A program may use at most 128 MiB of HBM per device.

v0:
```python
import jax
import jax.numpy as jnp
from jax import lax
from jax.sharding import PartitionSpec as P

HIGH = lax.Precision.HIGHEST


def orthonormal(whole):
    gram = jnp.dot(whole.T, whole, precision=HIGH)
    factor = jnp.linalg.cholesky(gram)
    return lax.linalg.triangular_solve(factor, whole, left_side=False, lower=True, transpose_a=True)


def expert_rows_of(route_logits, pair_score):
    first = 1.0 / (1.0 + jnp.exp(route_logits[:, 1] - route_logits[:, 0]))
    product = first * (1.0 - first) * (pair_score[:, 0] - pair_score[:, 1])
    return jnp.stack([product, -product], axis=-1).astype(jnp.bfloat16)


def local(attn_out, out_cols, error_in, power_q, tokens, routes, route_logits, pair_score):
    n_data = lax.axis_size("dp")
    n_groups = lax.axis_size("expert")
    width_d = tokens.shape[1]
    tok_count = tokens.shape[0]
    capacity = min(tok_count, 4 * tok_count // n_groups)
    rows_grad = expert_rows_of(route_logits, pair_score)
    labels = jnp.arange(n_groups, dtype=jnp.int32)
    pair_grad = rows_grad.reshape(tok_count * 2)
    flat_routes = routes.reshape(-1)
    onehot = (flat_routes[:, None] == labels[None, :]).astype(jnp.int32)
    before = jnp.cumsum(onehot, axis=0) - onehot
    slot_of = jnp.sum(before * onehot, axis=1)
    target = flat_routes * capacity + slot_of
    table = (
        jnp.full((n_groups * capacity,), -1, jnp.int32)
        .at[target]
        .set(jnp.arange(tok_count * 2, dtype=jnp.int32))
    )
    filled = table >= 0
    picked = jnp.maximum(table, 0)
    send_rows = jnp.where(
        filled[:, None], tokens[picked // 2], jnp.zeros((), jnp.bfloat16)
    ).reshape(n_groups, capacity, width_d)
    send_grads = jnp.where(filled, pair_grad[picked], jnp.zeros((), jnp.bfloat16)).reshape(
        n_groups, capacity
    )
    got_rows, got_grads = (
        lax.all_to_all(send_rows, "expert", split_axis=0, concat_axis=0, tiled=True),
        lax.all_to_all(send_grads, "expert", split_axis=0, concat_axis=0, tiled=True),
    )
    flat_rows = got_rows.reshape(-1, width_d)
    flat_grads = got_grads.reshape(-1)
    expert_shard = lax.psum_scatter(
        jnp.dot(flat_grads, flat_rows, preferred_element_type=jnp.float32),
        "dp",
        scatter_dimension=0,
        tiled=True,
    )
    expert_grad = expert_shard[None]
    grad_w = lax.dot_general(
        lax.all_gather(attn_out, "expert", axis=1, tiled=True),
        out_cols,
        (((0,), (0,)), ((), ())),
        preferred_element_type=jnp.float32,
    ) + error_in[0].astype(jnp.float32)
    local_p = jnp.dot(grad_w, power_q, precision=HIGH)
    summed = lax.psum(local_p, ("dp", "expert"))
    basis = orthonormal(summed / n_data)
    q_new = lax.psum(jnp.dot(grad_w.T, basis, precision=HIGH), "dp") / n_data
    approx_full = jnp.dot(basis, q_new.T, precision=HIGH)
    error_out = (grad_w - approx_full).astype(jnp.bfloat16)[None]
    rows_here = width_d // n_data
    approx_part = lax.dynamic_slice_in_dim(
        approx_full, lax.axis_index("dp") * rows_here, rows_here, 0
    ).astype(jnp.bfloat16)
    return (approx_part, q_new, error_out, expert_grad)


def solution(mesh):
    placed = (
        P("dp", "expert"),
        P("dp", "expert"),
        P("dp", None, "expert"),
        P("expert", None),
        P(("dp", "expert"), None),
        P(("dp", "expert"), None),
        P(("dp", "expert"), None),
        P(("dp", "expert"), None),
    )
    return jax.shard_map(
        local,
        mesh=mesh,
        in_specs=placed,
        out_specs=(
            P("dp", "expert"),
            P("expert", None),
            P("dp", None, "expert"),
            P("expert", "dp"),
        ),
        check_vma=False,
    )
```

profile of v0, /device:TPU:64, one launch (start us, length us, event | category | flops | bytes accessed | tf_op | source)
XLA Modules:
  0.0 894.4 jit_solution(8342830568355131961)
XLA Ops:
  7.2 0.0 copy-start
  7.2 0.9 copy.20
  8.1 0.1 eq.29
  8.2 0.1 eq.25
  8.4 0.7 broadcast_multiply_fusion.1
  9.1 0.6 reduce-window.6
  9.6 0.2 slice_reduce_fusion
  9.9 0.1 copy.19
  10.0 0.1 mul.35
  10.1 0.1 fusion.11
  10.3 1.4 scatter_custom_fusion
  11.7 0.8 fusion.21
  12.5 0.1 copy.22
  12.6 0.2 convert_element_type.30
  12.8 3.4 gather_fusion
  16.2 0.7 all_to_all.15
  16.8 8.2 all-to-all-start
  25.1 0.1 broadcast_in_dim.42
  25.2 6.0 gather_fusion.1
  31.2 5.9 broadcast_select_fusion
  37.1 0.0 all-to-all-done
  37.1 5.3 all-to-all-start.1
  42.4 0.7 all-gather.2.cloned.1.call-update
  43.1 0.0 copy-start.7
  43.1 0.2 all-reduce.4.cloned.1.call-start
  43.3 67.8 %all-gather.2.cloned.1.call-done = bf16[128,6144]{1,0:T(8,128)(2,1)} async-done(((bf16[128,768]{1,0:T(8,128)(2,1)}), bf16[128,6144]{1,0:T(8,128)(2,1)}) %all-gather.2.cloned.1.call-update) | async-done | bytes 1572880 | tf_op jit(solution)/shard_map/all_gather | solution.py:62
  111.2 2.0 convolution_add_fusion
  113.2 1.7 copy-done.1
  114.9 4.7 fusion.23
  119.5 0.0 all-reduce.4.cloned.1.call-update
  119.6 1.3 dynamic-slice
  121.5 299.2 %all-reduce.4.cloned.1.call-done = f32[6144,64]{0,1:T(8,128)} async-done(((f32[6144,64]{0,1:T(8,128)}), f32[6144,64]{0,1:T(8,128)}) %all-reduce.4.cloned.1.call-update) | async-done | bytes 1572880 | tf_op jit(solution)/shard_map/psum | solution.py:68
  420.7 3.4 fusion.3
  424.0 0.1 copy.18
  424.1 5.8 cholesky.16
  430.0 0.6 compare_reduce_fusion
  430.7 0.7 fusion.7
  431.3 4.9 custom-call.6
  436.2 0.0 copy-start.2
  436.2 3.1 fusion.1
  439.4 2.2 fusion.24
  441.6 0.0 all-to-all-done.1
  441.6 3.7 fusion.13
  445.3 434.5 %all-reduce.1 = (f32[128,64]{0,1:T(8,128)S(1)}, f32[6144]{0:T(1024)S(1)}) all-reduce(f32[128,64]{0,1:T(8,128)S(1)} %fusion.24, f32[6144]{0:T(1024)S(1)} %bitcast.42), channel_id=1, replica_groups=mesh['dp'=64,'expert'=8] {'dp'}, use_global_device_ids=true, to_apply=%region_3.4 | all-reduce | flops 14336 | bytes 114688 | tf_op jit(solution)/shard_map/psum | solution.py:70
  879.8 5.1 fusion.25
  884.9 1.4 fusion
  886.4 0.6 dynamic-slice_convert_fusion
  887.0 0.6 dynamic-slice_bitcast_fusion
  (26 shorter events, 0.2 us)
Async XLA Ops:
  7.2 18.0 %copy-start = (bf16[128,6144]{1,0:T(8,128)(2,1)S(1)}, bf16[128,6144]{1,0:T(8,128)(2,1)}, u32[]{:S(2)}) copy-start(bf16[128,6144]{1,0:T(8,128)(2,1)} %param.12) | copy-start | bytes 4718596
  16.8 20.3 %all-to-all-start = ((bf16[8,1,64]{2,1,0:T(2,128)(2,1)}), bf16[8,1,64]{2,1,0:T(2,128)(2,1)S(1)}, u32[]{:S(2)}, u32[]{:S(2)}) async-start(bf16[8,1,64]{2,1,0:T(2,128)(2,1)} %all_to_all.15), calls=%async_computation | async-start | bytes 8192 | tf_op jit(solution)/shard_map/all_to_all | solution.py:50
  37.1 74.1 %copy-start.4 = (bf16[1,6144,128]{2,1,0:T(8,128)(2,1)S(1)}, bf16[1,6144,128]{2,1,0:T(8,128)(2,1)}, u32[]{:S(2)}) copy-start(bf16[1,6144,128]{2,1,0:T(8,128)(2,1)} %param.10) | copy-start | bytes 4718596
  37.1 74.1 %copy-start.6 = (bf16[128,128]{1,0:T(8,128)(2,1)S(1)}, bf16[128,128]{1,0:T(8,128)(2,1)}, u32[]{:S(2)}) copy-start(bf16[128,128]{1,0:T(8,128)(2,1)} %param.9) | copy-start | bytes 98308
  37.1 404.5 %all-to-all-start.1 = ((bf16[8,64,6144]{2,1,0:T(8,128)(2,1)}), bf16[8,64,6144]{2,1,0:T(8,128)(2,1)}, u32[]{:S(2)}, u32[]{:S(2)}) async-start(bf16[8,64,6144]{2,1,0:T(8,128)(2,1)} %broadcast_select_fusion), calls=%async_computation.1 | async-start | bytes 12582912 | tf_op jit(solution)/shard_map/all_to_all | solution.py:49
  42.4 68.8 %all-gather.2.cloned.1.call-start = ((), (), s32[]{:S(2)}) async-start(), calls=%async_computation.2 | async-start | bytes 1769472 | tf_op jit(solution)/shard_map/all_gather | solution.py:62
  43.1 71.8 %copy-start.7 = (f32[128,64]{0,1:T(8,128)S(1)}, f32[128,64]{0,1:T(8,128)}, u32[]{:S(2)}) copy-start(f32[128,64]{0,1:T(8,128)} %param.11) | copy-start | bytes 98308
  43.1 377.6 %all-reduce.4.cloned.1.call-start = ((), (), s32[]{:S(2)}) async-start(), calls=%async_computation.3 | async-start | bytes 3145728 | tf_op jit(solution)/shard_map/psum | solution.py:68
  113.2 1.7 copy-start.1
  436.2 3.2 copy-start.2
  879.8 5.1 copy-start.5
  879.8 5.1 copy-start.3
Sparse Core Ops, SparseCore 0:
  45.3 65.8 all-gather.1
  119.7 300.9 all-reduce.3
where the time goes:
time: 895 us; the launch traced here: 894 us
  blocking collectives  434 us (48%)
  waiting for transfers between devices  368 us (41%)
  matrix products  24.2 us (3%)
  other arithmetic  21.7 us (2%)
  local copies, waits for them, and re-layouts  17.7 us (2%)
  between operations  14.9 us (2%)
  starting transfers between devices  13.7 us (2%)
    psum x1, blocking collectives, local(): q_new = lax.psum(jnp.dot(grad_w.T, basis, precision=HIGH), 'dp') / n_data  434 us
    psum x1, waiting for transfers between devices, local(): summed = lax.psum(local_p, ('dp', 'expert'))  299 us
    all_gather x1, waiting for transfers between devices, local(): lax.all_gather(attn_out, 'expert', axis=1, tiled=True)  67.8 us
  transfers between devices with their start and end apart: 4, of which 2 were waited for; matrix products, arithmetic and copies ran while one was open for 5% of the time, Pallas kernels for 0%

commit v1 on v0

v1 whole, which is shorter than its diff:
```python
import jax
import jax.numpy as jnp
from jax import lax
from jax.sharding import Mesh, PartitionSpec as P

HIGH = lax.Precision.HIGHEST
F16 = jnp.float16
RANK = 64
DP = ("x", "y", "h")
EXPERT = ("l", "c")
FLAT = ("x", "y", "h", "l")


def exchange(values, axes):
    return lax.all_to_all(values, axes, split_axis=0, concat_axis=0, tiled=True)


def swap_cores(values):
    return lax.ppermute(values, "c", [(0, 1), (1, 0)])


def scale_of(bound):
    safe = jnp.maximum(bound, 1e-30)
    return jnp.clip(jnp.ceil(jnp.log2(safe)) - 14.0, -110.0, 110.0)


def coded(values, exponent):
    small = (values * jnp.exp2(-exponent)).astype(F16)
    row = jnp.broadcast_to(exponent, small.shape[:-2] + (1, 128)).astype(F16)
    return jnp.concatenate([small, row], axis=-2)


def decoded(received):
    scale = jnp.exp2(received[..., 6:7, 0:1].astype(jnp.float32))
    return received[..., :6, :].astype(jnp.float32) * scale


def expert_partial(tokens, routes, route_logits, pair_score):
    first = 1.0 / (1.0 + jnp.exp(route_logits[:, 1] - route_logits[:, 0]))
    product = first * (1.0 - first) * (pair_score[:, 0] - pair_score[:, 1])
    rows = product.astype(jnp.bfloat16)[:, None]
    labels = jnp.arange(8, dtype=jnp.int32)[None, :]
    zero = jnp.zeros((), jnp.bfloat16)
    spread = jnp.where(routes[:, :1] == labels, rows, zero) + jnp.where(
        routes[:, 1:] == labels, -rows, zero
    )
    return lax.dot_general(
        spread, tokens, (((0,), (0,)), ((), ())), preferred_element_type=jnp.float32
    )


def local(attn_out, out_cols, error_in, power_q, tokens, routes, route_logits, pair_score):
    error = error_in[0]
    core = lax.axis_index("c")
    group = lax.axis_index("l") * 2 + core
    gathered = lax.all_gather(attn_out, EXPERT, axis=1, tiled=True)

    part = lax.dot_general(
        power_q, out_cols.astype(jnp.float32), (((0,), (1,)), ((), ())), precision=HIGH
    )
    cq = jnp.sum(exchange(jnp.broadcast_to(part, (8,) + part.shape), EXPERT), axis=0)

    from_error = lax.dot_general(
        power_q, error.astype(jnp.float32), (((0,), (1,)), ((), ())), precision=HIGH
    )
    from_attn = jnp.dot(cq, attn_out.astype(jnp.float32), precision=HIGH)
    bound = 256.0 * (
        jnp.max(jnp.abs(error)).astype(jnp.float32) * jnp.max(jnp.abs(power_q))
        + jnp.max(jnp.abs(attn_out)).astype(jnp.float32) * jnp.max(jnp.abs(cq))
    )
    here = (jnp.arange(8) == group)[None, :, None]
    share = from_error.reshape(RANK, 8, 768) + jnp.where(here, from_attn[:, None, :], 0.0)
    share = share.reshape(RANK, 4, 2, 768)
    kept = lax.dynamic_index_in_dim(share, core, 2, keepdims=False)
    given = lax.dynamic_index_in_dim(share, 1 - core, 2, keepdims=False)
    bounds = jnp.broadcast_to(bound, (1, 128))
    half = kept + swap_cores(given)
    exponent = scale_of(bound + swap_cores(bounds)[0, 0])
    summed = jnp.sum(
        decoded(exchange(coded(half.reshape(256, 6, 128), exponent), FLAT)), axis=0
    )

    piece = coded(summed, scale_of(jnp.max(jnp.abs(summed))))
    mine = exchange(jnp.broadcast_to(piece, (256, 7, 128)), FLAT)
    other = swap_cores(mine)
    first = decoded(jnp.where(core == 0, mine, other)).reshape(RANK, 4, 768)
    second = decoded(jnp.where(core == 0, other, mine)).reshape(RANK, 4, 768)
    p_t = jnp.stack([first, second], axis=2).reshape(RANK, 6144)

    grad_w = lax.dot_general(
        gathered, out_cols, (((0,), (0,)), ((), ())), preferred_element_type=jnp.float32
    ) + error.astype(jnp.float32)

    expert_sum = lax.psum_scatter(
        expert_partial(tokens, routes, route_logits, pair_score),
        EXPERT,
        scatter_dimension=0,
        tiled=True,
    )
    by_y = expert_sum.reshape(4, 8, 2, 96).transpose(1, 0, 2, 3).reshape(8, 6, 128)

    raw = jnp.dot(p_t, grad_w, precision=HIGH)
    over_y = jnp.sum(
        exchange(jnp.concatenate([jnp.broadcast_to(raw, (8, RANK, 128)), by_y], axis=1), "y"),
        axis=0,
    )
    rest = jnp.pad(over_y[RANK:].reshape(8, 1, 96), ((0, 0), (0, 0), (0, 32)))
    over_all = jnp.sum(
        exchange(
            jnp.concatenate([jnp.broadcast_to(over_y[:RANK], (8, RANK, 128)), rest], axis=1),
            ("x", "h"),
        ),
        axis=0,
    )
    expert_grad = over_all[RANK:, :96]

    gram = lax.dot_general(p_t, p_t, (((1,), (1,)), ((), ())), precision=HIGH)
    factor = jnp.linalg.cholesky(gram, symmetrize_input=False)
    inverse = lax.linalg.triangular_solve(
        factor, jnp.eye(RANK, dtype=jnp.float32), left_side=True, lower=True
    )
    q_t = jnp.dot(inverse, over_all[:RANK], precision=HIGH) / 64.0
    weights = jnp.dot(inverse.T, q_t, precision=HIGH)
    approx_full = lax.dot_general(p_t, weights, (((0,), (0,)), ((), ())), precision=HIGH)
    error_out = (grad_w - approx_full).astype(jnp.bfloat16)[None]
    index = (lax.axis_index("x") * 8 + lax.axis_index("y")) * 2 + lax.axis_index("h")
    approx = lax.dynamic_slice_in_dim(approx_full, index * 96, 96, 0).astype(jnp.bfloat16)
    return approx, q_t.T, error_out, expert_grad


def solution(mesh):
    fine = Mesh(mesh.devices.reshape(4, 8, 2, 4, 2), DP + EXPERT)
    everyone = P(DP + EXPERT, None)
    return jax.shard_map(
        local,
        mesh=fine,
        in_specs=(
            P(DP, EXPERT),
            P(DP, EXPERT),
            P(DP, None, EXPERT),
            P(EXPERT, None),
            everyone,
            everyone,
            everyone,
            everyone,
        ),
        out_specs=(P(DP, EXPERT), P(EXPERT, None), P(DP, None, EXPERT), P(EXPERT, DP)),
        check_vma=False,
    )
```

time: 895 us -> 246 us (0.27)
  the two profiles are of different devices: /device:TPU:64 before, /device:TPU:8 now
where the time goes in v1:
time: 246 us; the launch traced here: 245 us
  blocking collectives  70.4 us (29%)
  waiting for transfers between devices  58.5 us (24%)
  starting transfers between devices  28.8 us (12%)
  other arithmetic  27.8 us (11%)
  local copies, waits for them, and re-layouts  21.4 us (9%)
  matrix products  20.3 us (8%)
  between operations  17.9 us (7%)
    all_to_all x2, blocking collectives, exchange(): return lax.all_to_all(values, axes, split_axis=0, concat_axis=0, tiled=True)  70.4 us
    all_gather x1, waiting for transfers between devices, local(): gathered = lax.all_gather(attn_out, EXPERT, axis=1, tiled=True)  42.6 us
    all_to_all x3, starting transfers between devices, exchange(): return lax.all_to_all(values, axes, split_axis=0, concat_axis=0, tiled=True)  22.5 us
    all_to_all x3, waiting for transfers between devices, exchange(): return lax.all_to_all(values, axes, split_axis=0, concat_axis=0, tiled=True)  15.1 us
    another operation x3, other arithmetic, local(): factor = jnp.linalg.cholesky(gram, symmetrize_input=False)  6.51 us
    ppermute x3, starting transfers between devices, swap_cores(): return lax.ppermute(values, 'c', [(0, 1), (1, 0)])  6.23 us
    another operation x4, local copies, waits for them, and re-layouts, local(): p_t = jnp.stack([first, second], axis=2).reshape(RANK, 6144)  6.1 us
    another operation x2, other arithmetic, local(): lax.linalg.triangular_solve(factor, jnp.eye(RANK, dtype=jnp.float32), lef...  5.55 us
  transfers between devices with their start and end apart: 8, of which 5 were waited for; matrix products, arithmetic and copies ran while one was open for 13% of the time, Pallas kernels for 0%

profile of v1, /device:TPU:8, one launch (start us, length us, event | category | flops | bytes accessed | tf_op | source)
XLA Modules:
  0.0 245.0 jit_solution(16385996502659505332)
XLA Ops:
  7.2 1.1 fusion.31
  8.3 0.7 broadcast_in_dim.69
  9.0 7.3 %all-to-all-start = ((f32[8,64,128]{2,1,0:T(8,128)}), f32[8,64,128]{2,1,0:T(8,128)S(1)}, u32[]{:S(2)}, u32[]{:S(2)}) async-start(f32[8,64,128]{2,1,0:T(8,128)} %broadcast_in_dim.69), calls=%async_computation | async-start | bytes 524288 | tf_op jit(solution)/shard_map/all_to_all | solution.py:15
  16.4 0.8 slice_bitcast_fusion.1
  17.1 0.8 negate_bitcast_fusion
  17.9 8.1 %all-to-all-done = f32[8,64,128]{2,1,0:T(8,128)S(1)} async-done(((f32[8,64,128]{2,1,0:T(8,128)}), f32[8,64,128]{2,1,0:T(8,128)S(1)}, u32[]{:S(2)}, u32[]{:S(2)}) %all-to-all-start) | async-done | bytes 262176 | tf_op jit(solution)/shard_map/all_to_all | solution.py:15
  26.1 1.2 fusion.32
  27.3 1.8 select_add_fusion
  29.0 1.0 constant_dynamic-slice_fusion.1
  30.0 1.4 copy.55
  31.4 1.9 collective-permute-start
  33.4 1.1 fusion.16
  35.2 0.8 abs_reduce_fusion
  39.8 2.4 collective-permute-start.1
  42.3 0.8 collective-permute-done.1
  43.2 2.0 fusion.2
  45.2 1.0 convert_element_type.67
  46.2 1.2 concatenate.12
  47.4 40.8 %all_to_all.25 = f16[256,7,128]{2,1,0:T(8,128)(2,1)S(1)} all-to-all(f16[256,7,128]{2,1,0:T(8,128)(2,1)S(1)} %concatenate.12), channel_id=1, replica_groups=mesh['x'=4,'y'=8,'h'=2,'l'=4,'c'=2] {'x','y','h','l'}, dimensions={0} | all-to-all | bytes 917504 | tf_op jit(solution)/shard_map/all_to_all | solution.py:15
  88.1 1.0 fusion.9
  91.0 29.6 %all_to_all.26 = f16[256,7,128]{2,1,0:T(8,128)(2,1)} all-to-all(f16[256,7,128]{2,1,0:T(8,128)(2,1)S(1)} %broadcast_in_dim.73), channel_id=1, replica_groups=mesh['x'=4,'y'=8,'h'=2,'l'=4,'c'=2] {'x','y','h','l'}, dimensions={0} | all-to-all | bytes 917504 | tf_op jit(solution)/shard_map/all_to_all | solution.py:15
  120.6 1.9 collective-permute-start.2
  122.5 1.3 dynamic-slice
  123.8 1.6 dynamic-slice_reduce_fusion
  125.7 42.6 %all-gather.2.cloned.1.call-done = bf16[128,6144]{1,0:T(8,128)(2,1)} async-done(((bf16[128,768]{1,0:T(8,128)(2,1)}), bf16[128,6144]{1,0:T(8,128)(2,1)}) %all-gather.2.cloned.1.call-update) | async-done | bytes 1572880 | tf_op jit(solution)/shard_map/all_gather | solution.py:56
  168.2 3.7 %convolution_add_fusion = f32[6144,128]{1,0:T(8,128)} fusion(bf16[128,6144]{1,0:T(8,128)(2,1)} %all-gather.2.cloned.1.call-done, bf16[128,128]{1,0:T(8,128)(2,1)S(1)} %copy-done.7, bf16[1,6144,128]{2,1,0:T(8,128)(2,1)S(1)} %copy-done.2), kind=kOutput, calls=%fused_computation | convolution fusion | flops 202899456 | bytes 6324224 | tf_op jit(solution)/shard_map/dot_general | solution.py:90
  171.9 1.5 broadcast_select_fusion
  173.4 1.0 fusion.11
  174.5 1.0 fusion.10
  175.5 1.8 convert_multiply_fusion
  177.3 2.4 stack_reshape.7
  179.7 1.2 stack_reshape.6
  180.9 1.4 copy_dynamic-update-slice_fusion.1
  182.4 2.4 copy.38
  184.8 3.4 %reshape.49 = f32[64,6144]{1,0:T(8,128)} reshape(f32[64,4,2,768]{3,2,1,0:T(2,128)} %copy.38) | data formatting | bytes 3145728 | tf_op jit(solution)/shard_map/reshape | solution.py:88
  188.1 4.4 %fusion.33 = f32[64,128]{1,0:T(8,128)S(1)} fusion(f32[64,6144]{1,0:T(8,128)} %reshape.49, f32[6144,128]{1,0:T(8,128)} %convolution_add_fusion), kind=kOutput, calls=%fused_computation.74 | convolution fusion | flops 603979776 | bytes 4751360 | tf_op jit(solution)/shard_map/dot_general | solution.py:102
  192.6 0.7 pad_maximum_fusion
  193.3 7.3 %all-to-all-start.3 = ((f32[8,70,128]{2,1,0:T(8,128)}), f32[8,70,128]{2,1,0:T(8,128)S(1)}, u32[]{:S(2)}, u32[]{:S(2)}) async-start(f32[8,70,128]{2,1,0:T(8,128)} %pad_maximum_fusion), calls=%async_computation.3 | async-start | bytes 589824 | tf_op jit(solution)/shard_map/all_to_all | solution.py:15
  200.6 1.4 convolution_bitcast_fusion
  202.0 5.8 %cholesky.17 = f32[64,64]{1,0:T(8,128)S(1)} custom-call(f32[64,64]{1,0:T(8,128)S(1)} %convolution_bitcast_fusion), custom_call_target="Cholesky" | custom-call | tf_op jit(solution)/shard_map/jit(cholesky)/cholesky | solution.py:118
  207.9 2.0 all-to-all-done.3
  210.0 0.7 select_maximum_fusion
  210.7 8.0 %all-to-all-start.4 = ((f32[8,65,128]{2,1,0:T(8,128)}), f32[8,65,128]{2,1,0:T(8,128)S(1)}, u32[]{:S(2)}, u32[]{:S(2)}) async-start(f32[8,65,128]{2,1,0:T(8,128)} %select_maximum_fusion), calls=%async_computation.4 | async-start | bytes 589824 | tf_op jit(solution)/shard_map/all_to_all | solution.py:15
  219.3 0.7 fusion.14
  220.0 4.9 %custom-call.6 = f32[1,64,64]{1,2,0:T(8,128)S(1)} custom-call(f32[1,64,64]{2,1,0:T(8,128)S(1)} %fusion.14), custom_call_target="InvertDiagBlocksLowerTriangular" | custom-call | tf_op jit(solution)/shard_map/triangular_solve | solution.py:119
  225.1 4.9 %all-to-all-done.4 = f32[8,65,128]{2,1,0:T(8,128)S(1)} async-done(((f32[8,65,128]{2,1,0:T(8,128)}), f32[8,65,128]{2,1,0:T(8,128)S(1)}, u32[]{:S(2)}, u32[]{:S(2)}) %all-to-all-start.4) | async-done | bytes 266272 | tf_op jit(solution)/shard_map/all_to_all | solution.py:15
  231.0 5.1 %fusion.35 = f32[6144,128]{1,0:T(8,128)S(1)} fusion(f32[64,6144]{1,0:T(8,128)S(1)} %copy-done.3, f32[64,128]{1,0:T(8,128)S(1)} %fusion.34), kind=kOutput, calls=%fused_computation.76 | convolution fusion | flops 603979776 | bytes 4751360 | tf_op jit(solution)/shard_map/dot_general | solution.py:124
  236.1 1.4 fusion
  (54 shorter events, 6.0 us)
Async XLA Ops:
  7.2 26.2 %copy-start = (bf16[128,6144]{1,0:T(8,128)(2,1)S(1)}, bf16[128,6144]{1,0:T(8,128)(2,1)}, u32[]{:S(2)}) copy-start(bf16[128,6144]{1,0:T(8,128)(2,1)} %param.12) | copy-start | bytes 4718596
  7.2 20.1 %copy-start.6 = (f32[128,64]{0,1:T(8,128)S(1)}, f32[128,64]{0,1:T(8,128)}, u32[]{:S(2)}) copy-start(f32[128,64]{0,1:T(8,128)} %param.11) | copy-start | bytes 98308
  7.2 20.1 %copy-start.2 = (bf16[1,6144,128]{2,1,0:T(8,128)(2,1)S(1)}, bf16[1,6144,128]{2,1,0:T(8,128)(2,1)}, u32[]{:S(2)}) copy-start(bf16[1,6144,128]{2,1,0:T(8,128)(2,1)} %param.10) | copy-start | bytes 4718596
  9.0 17.0 %all-to-all-start = ((f32[8,64,128]{2,1,0:T(8,128)}), f32[8,64,128]{2,1,0:T(8,128)S(1)}, u32[]{:S(2)}, u32[]{:S(2)}) async-start(f32[8,64,128]{2,1,0:T(8,128)} %broadcast_in_dim.69), calls=%async_computation | async-start | bytes 524288 | tf_op jit(solution)/shard_map/all_to_all | solution.py:15
  16.3 107.5 %all-reduce.6.cloned.1.call-start = ((), (), s32[]{:S(2)}) async-start(), calls=%async_computation.6 | async-start | bytes 393216
  31.4 11.8 %collective-permute-start = (f32[64,4,768]{2,1,0:T(4,128)}, f32[64,4,768]{2,1,0:T(4,128)}, u32[]{:S(2)}, u32[]{:S(2)}) collective-permute-start(f32[64,4,768]{2,1,0:T(4,128)} %bitcast.59), channel_id=1, source_target_pairs={{0,1},{1,0},{2,3},{3,2},{4,5},{5,4},{6,7},{7,6},{8,9},{9,8},{10,11... | collective-permute-start | bytes 2359304 | tf_op jit(solution)/shard_map/ppermute | solution.py:19
  33.3 3.9 %copy-start.5 = (bf16[128,768]{1,0:T(8,128)(2,1)S(1)}, bf16[128,768]{1,0:T(8,128)(2,1)}, u32[]{:S(2)}) copy-start(bf16[128,768]{1,0:T(8,128)(2,1)} %param.8) | copy-start | bytes 589828
  34.5 133.7 %all-gather.2.cloned.1.call-start = ((), (), s32[]{:S(2)}) async-start(), calls=%async_computation.5 | async-start | bytes 1769472 | tf_op jit(solution)/shard_map/all_gather | solution.py:56
  39.8 3.2 %collective-permute-start.1 = (f32[1,128]{1,0:T(1,128)S(1)}, f32[1,128]{1,0:T(1,128)S(1)}, u32[]{:S(2)}, u32[]{:S(2)}) collective-permute-start(f32[1,128]{1,0:T(1,128)S(1)} %broadcast_in_dim.72), channel_id=1, source_target_pairs={{0,1},{1,0},{2,3},{3,2},{4,5},{5,4},{6,7},{7,6},{8,9},{9,8},{10,11... | collective-permute-start | bytes 1544 | tf_op jit(solution)/shard_map/ppermute | solution.py:19
  47.3 120.9 %copy-start.7 = (bf16[128,128]{1,0:T(8,128)(2,1)S(1)}, bf16[128,128]{1,0:T(8,128)(2,1)}, u32[]{:S(2)}) copy-start(bf16[128,128]{1,0:T(8,128)(2,1)} %param.9) | copy-start | bytes 98308
  120.6 51.3 %collective-permute-start.2 = (f16[256,7,128]{2,1,0:T(8,128)(2,1)}, f16[256,7,128]{2,1,0:T(8,128)(2,1)}, u32[]{:S(2)}, u32[]{:S(2)}) collective-permute-start(f16[256,7,128]{2,1,0:T(8,128)(2,1)} %all_to_all.26), channel_id=1, source_target_pairs={{0,1},{1,0},{2,3},{3,2},{4,5},{5,4},{6,7},{7,6},{8,9},{9,8},{10,11... | collective-permute-start | bytes 1376264 | tf_op jit(solution)/shard_map/ppermute | solution.py:19
  180.9 1.4 copy-start.4
  193.3 16.6 %all-to-all-start.3 = ((f32[8,70,128]{2,1,0:T(8,128)}), f32[8,70,128]{2,1,0:T(8,128)S(1)}, u32[]{:S(2)}, u32[]{:S(2)}) async-start(f32[8,70,128]{2,1,0:T(8,128)} %pad_maximum_fusion), calls=%async_computation.3 | async-start | bytes 589824 | tf_op jit(solution)/shard_map/all_to_all | solution.py:15
  202.0 29.1 %copy-start.3 = (f32[64,6144]{1,0:T(8,128)S(1)}, f32[64,6144]{1,0:T(8,128)}, u32[]{:S(2)}) copy-start(f32[64,6144]{1,0:T(8,128)} %reshape.49) | copy-start | bytes 4718596
  210.7 19.3 %all-to-all-start.4 = ((f32[8,65,128]{2,1,0:T(8,128)}), f32[8,65,128]{2,1,0:T(8,128)S(1)}, u32[]{:S(2)}, u32[]{:S(2)}) async-start(f32[8,65,128]{2,1,0:T(8,128)} %select_maximum_fusion), calls=%async_computation.4 | async-start | bytes 589824 | tf_op jit(solution)/shard_map/all_to_all | solution.py:15
  230.8 5.3 %copy-start.8 = (f32[64,128]{1,0:T(8,128)}, f32[64,128]{1,0:T(8,128)S(1)}, u32[]{:S(2)}) copy-start(f32[64,128]{1,0:T(8,128)S(1)} %convolution_multiply_fusion) | copy-start | bytes 98308
  231.0 5.1 %copy-start.1 = (f32[6144,128]{1,0:T(8,128)S(1)}, f32[6144,128]{1,0:T(8,128)}, u32[]{:S(2)}) copy-start(f32[6144,128]{1,0:T(8,128)} %convolution_add_fusion) | copy-start | bytes 9437188
Sparse Core Ops, SparseCore 0:
  34.6 87.6 all-reduce.5
  124.7 43.5 all-gather.1

commit v2 on v1

v2 whole, which is shorter than its diff:
```python
import functools

import jax
import jax.numpy as jnp
from jax import lax
from jax.experimental import pallas as pl
from jax.experimental.pallas import tpu as pltpu
from jax.sharding import Mesh, PartitionSpec as P

HIGH = lax.Precision.HIGHEST
F32, BF16, I16 = jnp.float32, jnp.bfloat16, jnp.int16
RANK = 64
WIDTH = 6144
BLOCK = 768
DP = ("x", "y", "h")
EXPERT = ("l", "c")
FLAT = ("x", "y", "h", "l")
LIMIT = 32 * 1024 * 1024
TOP = 32000.0
STEP = 64.0
USED = 96

VMEM = pl.BlockSpec(memory_space=pltpu.VMEM)
SMEM = pl.BlockSpec(memory_space=pltpu.SMEM)


def exchange(values, axes):
    return lax.all_to_all(values, axes, split_axis=0, concat_axis=0, tiled=True)


def swap_cores(values):
    return lax.ppermute(values, "c", [(0, 1), (1, 0)])


def three(values):
    high = values.astype(BF16)
    rest = values - high.astype(F32)
    middle = rest.astype(BF16)
    low = (rest - middle.astype(F32)).astype(BF16)
    return jnp.concatenate([high, middle, low], axis=0)


def folded(stacked):
    return stacked[:RANK] + stacked[RANK : 2 * RANK] + stacked[2 * RANK :]


def scale_of(largest):
    exponent = jnp.ceil(STEP * jnp.log2(jnp.maximum(largest, 1e-30))) + 1.0
    return exponent, jnp.exp2(exponent * (-1.0 / STEP)) * TOP


def lanes_of(shape):
    return lax.broadcasted_iota(jnp.int32, shape, 1)


def coded(values):
    return jnp.round(values).astype(jnp.int32).astype(I16)


def decoded(tile):
    wide = tile.astype(jnp.int32).astype(F32)
    return wide * (jnp.exp2(wide[:, 127:128] * (1.0 / STEP)) * (1.0 / TOP))


def error_kernel(block_ref, q_ref, error_ref, out_ref):
    del block_ref
    out_ref[...] = folded(
        lax.dot_general(
            three(q_ref[...]), error_ref[...], (((1,), (1,)), ((), ())), preferred_element_type=F32
        )
    )


def error_share(power_t, error, core):
    return pl.pallas_call(
        error_kernel,
        grid_spec=pltpu.PrefetchScalarGridSpec(
            num_scalar_prefetch=1,
            grid=(4,),
            in_specs=[
                pl.BlockSpec((RANK, 128), lambda i, core: (0, 0)),
                pl.BlockSpec((BLOCK, 128), lambda i, core: (2 * i + core[0], 0)),
            ],
            out_specs=pl.BlockSpec((RANK, BLOCK), lambda i, core: (0, i)),
        ),
        out_shape=jax.ShapeDtypeStruct((RANK, 4 * BLOCK), F32),
        compiler_params=pltpu.CompilerParams(vmem_limit_bytes=LIMIT),
        cost_estimate=pl.CostEstimate(
            flops=2 * 192 * 128 * 3072, bytes_accessed=3072 * 512, transcendentals=0
        ),
    )(core.reshape(1), power_t, error)


def share_kernel(place_ref, cq_ref, attn_ref, kept_ref, came_ref, out_ref, half_ref):
    cq = jnp.sum(cq_ref[:, :RANK, :], axis=0)
    from_attn = folded(jnp.dot(three(cq), attn_ref[...], preferred_element_type=F32))
    half_ref[...] = kept_ref[...] + came_ref[...]
    here = pl.ds(pl.multiple_of(place_ref[0] * BLOCK, BLOCK), BLOCK)
    half_ref[:, here] += from_attn
    lane = lanes_of((8, 128))
    for band in range(8):
        rows = slice(band * 8, band * 8 + 8)
        tiles = [half_ref[rows, t * 128 : t * 128 + 128] for t in range(24)]
        largest = functools.reduce(jnp.maximum, [jnp.abs(t) for t in tiles])
        exponent, factor = scale_of(jnp.max(largest, axis=1, keepdims=True))
        exponent = jnp.broadcast_to(exponent, (8, 128))
        factor = jnp.broadcast_to(factor, (8, 128))
        for group in range(8):
            a, b, c = (t * factor for t in tiles[group * 3 : group * 3 + 3])
            tail = jnp.where(
                lane < 32,
                pltpu.roll(a, 32, 1),
                jnp.where(lane < 64, pltpu.roll(b, 64, 1), pltpu.roll(c, 96, 1)),
            )
            a, b, c, tail = (jnp.where(lane < USED, t, exponent) for t in (a, b, c, tail))
            at = (band * 32 + group * 4) * 8
            out_ref[at : at + 16, :] = coded(jnp.concatenate([a, b], axis=0))
            out_ref[at + 16 : at + 32, :] = coded(jnp.concatenate([c, tail], axis=0))


def share_of(place, cq_all, attn_out, kept, came):
    return pl.pallas_call(
        share_kernel,
        in_specs=[SMEM, VMEM, VMEM, VMEM, VMEM],
        out_specs=VMEM,
        out_shape=jax.ShapeDtypeStruct((2048, 128), I16),
        scratch_shapes=[pltpu.VMEM((RANK, 4 * BLOCK), F32)],
        compiler_params=pltpu.CompilerParams(vmem_limit_bytes=LIMIT),
    )(place.reshape(1), cq_all, attn_out, kept, came)


def sum_kernel(in_ref, out_ref):
    def step(i, total):
        at = pl.multiple_of(i * 64, 64)
        parts = [decoded(in_ref[pl.ds(at + 16 * j, 16), :]) for j in range(4)]
        return total + ((parts[0] + parts[1]) + (parts[2] + parts[3]))

    total = lax.fori_loop(0, 32, step, jnp.zeros((16, 128), F32), unroll=4)
    total = total[:8] + total[8:]
    used = lanes_of((8, 128)) < USED
    largest = jnp.max(jnp.where(used, jnp.abs(total), 0.0), axis=1, keepdims=True)
    exponent, factor = scale_of(largest)
    tile = jnp.where(used, total * factor, exponent)
    tile = coded(jnp.concatenate([tile, tile], axis=0))
    out_ref[...] = jnp.broadcast_to(tile[None], (128, 16, 128)).reshape(2048, 128)


def summed(received):
    return pl.pallas_call(
        sum_kernel,
        in_specs=[VMEM],
        out_specs=VMEM,
        out_shape=jax.ShapeDtypeStruct((2048, 128), I16),
        compiler_params=pltpu.CompilerParams(vmem_limit_bytes=LIMIT),
    )(received)


def grad_kernel(attn_ref, cols_ref, error_ref, out_ref):
    grad = lax.dot_general(
        attn_ref[...], cols_ref[...], (((0,), (0,)), ((), ())), preferred_element_type=F32
    ) + error_ref[...].astype(F32)
    high = grad.astype(BF16)
    out_ref[:, :128] = high
    out_ref[:, 128:] = (grad - high.astype(F32)).astype(BF16)


def grad_of(gathered, out_cols, error):
    return pl.pallas_call(
        grad_kernel,
        grid=(8,),
        in_specs=[
            pl.BlockSpec((128, BLOCK), lambda i: (0, i)),
            pl.BlockSpec((128, 128), lambda i: (0, 0)),
            pl.BlockSpec((BLOCK, 128), lambda i: (i, 0)),
        ],
        out_specs=pl.BlockSpec((BLOCK, 256), lambda i: (i, 0)),
        out_shape=jax.ShapeDtypeStruct((WIDTH, 256), BF16),
        compiler_params=pltpu.CompilerParams(vmem_limit_bytes=LIMIT),
        cost_estimate=pl.CostEstimate(
            flops=2 * 128 * 128 * WIDTH, bytes_accessed=WIDTH * 1024, transcendentals=0
        ),
    )(gathered, out_cols, error)


def factor_kernel(core_ref, mine_ref, other_ref, grad_ref, raw_ref, gram_ref, p_ref):
    lane = lanes_of((16, 128))
    for ref, core in ((mine_ref, core_ref[0]), (other_ref, 1 - core_ref[0])):
        for pair in range(4):
            for group in range(8):
                first, second = [], []
                for band in (2 * pair, 2 * pair + 1):
                    at = (band * 32 + group * 4) * 8
                    first.append(decoded(ref[at : at + 16, :]))
                    second.append(decoded(ref[at + 16 : at + 32, :]))
                a = jnp.concatenate([t[:8] for t in first], axis=0)
                b = jnp.concatenate([t[8:] for t in first], axis=0)
                c = jnp.concatenate([t[:8] for t in second], axis=0)
                tail = jnp.concatenate([t[8:] for t in second], axis=0)
                for j, (tile, shift) in enumerate(((a, 96), (b, 64), (c, 32))):
                    tile = jnp.where(lane < USED, tile, pltpu.roll(tail, shift, 1))
                    place = group * 3 + j
                    row, column = place // 6, place % 6
                    at = (2 * row + core) * 3 + column // 2
                    lanes = slice(128 * (column % 2), 128 * (column % 2) + 128)
                    high = tile.astype(BF16)
                    low = (tile - high.astype(F32)).astype(BF16)
                    p_ref[at, pair * 16 : pair * 16 + 16, lanes] = high
                    p_ref[at, RANK + pair * 16 : RANK + pair * 16 + 16, lanes] = low
    raw = jnp.zeros((128, 256), F32)
    gram = jnp.zeros((128, 128), F32)
    for i in range(24):
        part = p_ref[i]
        raw += jnp.dot(part, grad_ref[i * 256 : i * 256 + 256, :], preferred_element_type=F32)
        gram += lax.dot_general(
            part, part, (((1,), (1,)), ((), ())), preferred_element_type=F32
        )
    raw = raw[:RANK] + raw[RANK:]
    raw_ref[...] = raw[:, :128] + raw[:, 128:]
    gram = gram[:RANK] + gram[RANK:]
    gram_ref[...] = gram[:, :RANK] + gram[:, RANK:]


def factor_of(core, mine, other, grad):
    return pl.pallas_call(
        factor_kernel,
        in_specs=[SMEM, VMEM, VMEM, VMEM],
        out_specs=[VMEM, VMEM, VMEM],
        out_shape=[
            jax.ShapeDtypeStruct((RANK, 128), F32),
            jax.ShapeDtypeStruct((RANK, RANK), F32),
            jax.ShapeDtypeStruct((24, 128, 256), BF16),
        ],
        compiler_params=pltpu.CompilerParams(vmem_limit_bytes=LIMIT),
    )(core.reshape(1), mine, other, grad)


def final_kernel(
    place_ref, inverse_ref, sums_ref, p_ref, grad_ref, approx_ref, q_ref, error_ref, expert_ref, full_ref
):
    sums = jnp.sum(sums_ref[...], axis=0)
    expert_ref[...] = sums[RANK : RANK + 1, :USED]
    inverse = inverse_ref[...]
    q_t = jnp.dot(inverse, sums[:RANK], precision=HIGH) * (1.0 / 64.0)
    q_ref[...] = q_t.T
    weights = jnp.dot(inverse.T, q_t, precision=HIGH)
    high = weights.astype(BF16)
    low = (weights - high.astype(F32)).astype(BF16)
    both = jnp.concatenate([high, low], axis=1)
    both = jnp.concatenate([both, both], axis=0)
    for i in range(24):
        rows = slice(i * 256, i * 256 + 256)
        part = lax.dot_general(
            p_ref[i], both, (((0,), (0,)), ((), ())), preferred_element_type=F32
        )
        part = part[:, :128] + part[:, 128:]
        full_ref[rows, :] = part
        grad = grad_ref[rows, :].astype(F32)
        error_ref[rows, :] = (grad[:, :128] + grad[:, 128:] - part).astype(BF16)
    here = pl.ds(pl.multiple_of(place_ref[0] * 96, 32), 96)
    approx_ref[...] = full_ref[here, :].astype(BF16)


def final_of(place, inverse, sums, p_parts, grad):
    return pl.pallas_call(
        final_kernel,
        in_specs=[SMEM, VMEM, VMEM, VMEM, VMEM],
        out_specs=[VMEM] * 4,
        out_shape=[
            jax.ShapeDtypeStruct((96, 128), BF16),
            jax.ShapeDtypeStruct((128, RANK), F32),
            jax.ShapeDtypeStruct((WIDTH, 128), BF16),
            jax.ShapeDtypeStruct((1, USED), F32),
        ],
        scratch_shapes=[pltpu.VMEM((WIDTH, 128), F32)],
        compiler_params=pltpu.CompilerParams(vmem_limit_bytes=LIMIT),
    )(place.reshape(1), inverse, sums, p_parts, grad)


def expert_partial(tokens, routes, route_logits, pair_score):
    first = 1.0 / (1.0 + jnp.exp(route_logits[:, 1] - route_logits[:, 0]))
    product = first * (1.0 - first) * (pair_score[:, 0] - pair_score[:, 1])
    rows = product.astype(BF16)[:, None]
    labels = jnp.arange(8, dtype=jnp.int32)[None, :]
    zero = jnp.zeros((), BF16)
    spread = jnp.where(routes[:, :1] == labels, rows, zero) + jnp.where(
        routes[:, 1:] == labels, -rows, zero
    )
    return lax.dot_general(spread, tokens, (((0,), (0,)), ((), ())), preferred_element_type=F32)


def local(attn_out, out_cols, error_in, power_q, tokens, routes, route_logits, pair_score):
    error = error_in[0]
    core = lax.axis_index("c").astype(jnp.int32)
    place = lax.axis_index("l").astype(jnp.int32)
    data = ((lax.axis_index("x") * 8 + lax.axis_index("y")) * 2 + lax.axis_index("h")).astype(jnp.int32)
    gathered = lax.all_gather(attn_out, EXPERT, axis=1, tiled=True)
    power_t = power_q.T

    part = lax.dot_general(
        power_t, out_cols.astype(F32), (((1,), (1,)), ((), ())), precision=HIGH
    )
    expert_rows = expert_partial(tokens, routes, route_logits, pair_score).reshape(8, 48, 128)
    cq_all = exchange(
        jnp.concatenate([jnp.broadcast_to(part, (8, RANK, 128)), expert_rows], axis=1), EXPERT
    )
    by_y = jnp.sum(cq_all[:, RANK:], axis=0).reshape(4, 8, 2, 96)
    by_y = by_y.transpose(1, 0, 2, 3).reshape(8, 6, 128)

    came = swap_cores(error_share(power_t, error, 1 - core))
    kept = error_share(power_t, error, core)
    codes = share_of(place, cq_all, attn_out, kept, came)
    piece = summed(exchange(codes.reshape(256, 8, 128), FLAT).reshape(2048, 128))
    mine = exchange(piece.reshape(256, 8, 128), FLAT).reshape(2048, 128)
    other = swap_cores(mine)
    grad = grad_of(gathered, out_cols, error)
    raw, gram, p_parts = factor_of(core, mine, other, grad)

    over_y = jnp.sum(
        exchange(jnp.concatenate([jnp.broadcast_to(raw, (8, RANK, 128)), by_y], axis=1), "y"),
        axis=0,
    )
    rest = jnp.pad(over_y[RANK:].reshape(8, 1, 96), ((0, 0), (0, 0), (0, 32)))
    sums = exchange(
        jnp.concatenate([jnp.broadcast_to(over_y[:RANK], (8, RANK, 128)), rest], axis=1),
        ("x", "h"),
    )

    factor = jnp.linalg.cholesky(gram, symmetrize_input=False)
    inverse = lax.linalg.triangular_solve(
        factor, jnp.eye(RANK, dtype=F32), left_side=True, lower=True
    )
    approx, q_new, error_out, expert_grad = final_of(data, inverse, sums, p_parts, grad)
    return approx, q_new, error_out[None], expert_grad


def solution(mesh):
    fine = Mesh(mesh.devices.reshape(4, 8, 2, 4, 2), DP + EXPERT)
    everyone = P(DP + EXPERT, None)
    return jax.shard_map(
        local,
        mesh=fine,
        in_specs=(
            P(DP, EXPERT),
            P(DP, EXPERT),
            P(DP, None, EXPERT),
            P(EXPERT, None),
            everyone,
            everyone,
            everyone,
            everyone,
        ),
        out_specs=(P(DP, EXPERT), P(EXPERT, None), P(DP, None, EXPERT), P(EXPERT, DP)),
        check_vma=False,
    )
```

time: 246 us -> 168 us (0.68)
  the two profiles are of different devices: /device:TPU:8 before, /device:TPU:64 now
where the time goes in v2:
time: 168 us; the launch traced here: 167 us
  blocking collectives  69.6 us (41%)
  starting transfers between devices  22.2 us (13%)
  waiting for transfers between devices  20.7 us (12%)
  other arithmetic  16.1 us (10%)
  Pallas kernels  16 us (10%)
  between operations  14.3 us (9%)
  local copies, waits for them, and re-layouts  7.22 us (4%)
    all_to_all x2, blocking collectives, exchange(): return lax.all_to_all(values, axes, split_axis=0, concat_axis=0, tiled=True)  69.6 us
    all_to_all x3, waiting for transfers between devices, exchange(): return lax.all_to_all(values, axes, split_axis=0, concat_axis=0, tiled=True)  20.2 us
    all_to_all x3, starting transfers between devices, exchange(): return lax.all_to_all(values, axes, split_axis=0, concat_axis=0, tiled=True)  18 us
    another operation x3, other arithmetic, local(): factor = jnp.linalg.cholesky(gram, symmetrize_input=False)  6.51 us
    unnamed x22, local copies, waits for them, and re-layouts  6.07 us
    another operation x2, other arithmetic, local(): lax.linalg.triangular_solve(factor, jnp.eye(RANK, dtype=F32), left_side=T...  5.55 us
    pallas_call x1, Pallas kernels, factor_of(): pl.pallas_call(factor_kernel, in_specs=[SMEM, VMEM, VMEM, VMEM], out_spec...  4.91 us
    ppermute x2, starting transfers between devices, swap_cores(): return lax.ppermute(values, 'c', [(0, 1), (1, 0)])  4.27 us
  transfers between devices with their start and end apart: 6, of which 4 were waited for; matrix products, arithmetic and copies ran while one was open for 8% of the time, Pallas kernels for 5%

profile of v2, /device:TPU:64, one launch (start us, length us, event | category | flops | bytes accessed | tf_op | source)
XLA Modules:
  0.0 167.1 jit_solution(7870090212565542024)
XLA Ops:
  7.2 0.0 copy-start
  7.2 0.0 copy-start.8
  7.2 0.0 copy-start.9
  7.2 0.8 slice_bitcast_fusion.1
  8.0 0.8 negate_bitcast_fusion
  8.8 0.5 convolution_bitcast_fusion
  9.3 0.2 fusion.16
  9.6 0.8 pad_maximum_fusion
  10.4 9.0 %all-to-all-start = ((f32[8,112,128]{2,1,0:T(8,128)}), f32[8,112,128]{2,1,0:T(8,128)}, u32[]{:S(2)}, u32[]{:S(2)}) async-start(f32[8,112,128]{2,1,0:T(8,128)} %pad_maximum_fusion), calls=%async_computation | async-start | bytes 917504 | tf_op jit(solution)/shard_map/all_to_all | solution.py:28
  19.4 0.0 all-gather.2.cloned.1.call-start
  19.4 2.2 %shard_map.112 = f32[64,3072]{1,0:T(8,128)} custom-call(s32[1]{0:T(128)} %bitcast.9.block_ref, f32[64,128]{1,0:T(8,128)S(1)} %bitcast.40, bf16[6144,128]{1,0:T(8,128)(2,1)S(1)} %bitcast.34), custom_call_target="tpu_custom_call" | custom-call | flops 150994944 | bytes 1572864 | tf_op jit(solution)/shard_map/pallas_call | solution.py:75
  21.6 2.2 %collective-permute-start = (f32[64,3072]{1,0:T(8,128)}, f32[64,3072]{1,0:T(8,128)}, u32[]{:S(2)}, u32[]{:S(2)}) collective-permute-start(f32[64,3072]{1,0:T(8,128)} %shard_map.112), channel_id=1, source_target_pairs={{0,1},{1,0},{2,3},{3,2},{4,5},{5,4},{6,7},{7,6},{8,9},{9,8},{10,11... | collective-permute-start | bytes 2359304 | tf_op jit(solution)/shard_map/ppermute | solution.py:32
  23.8 0.0 all-gather.2.cloned.1.call-update
  23.8 1.1 shard_map.111.kept_ref
  24.9 0.0 copy-start.4
  24.9 0.9 copy-done.4
  25.8 0.5 collective-permute-done.came_ref
  26.2 4.4 %all-to-all-done.cq_ref = f32[8,112,128]{2,1,0:T(8,128)} async-done(((f32[8,112,128]{2,1,0:T(8,128)}), f32[8,112,128]{2,1,0:T(8,128)}, u32[]{:S(2)}, u32[]{:S(2)}) %all-to-all-start) | async-done | bytes 458784 | tf_op jit(solution)/shard_map/all_to_all | solution.py:28
  30.6 0.0 copy-done.7
  30.6 1.1 copy-done.5
  31.7 1.9 %shard_map.113 = s16[2048,128]{1,0:T(8,128)(2,1)S(1)} custom-call(s32[1]{0:T(128)} %bitcast.2.place_ref, f32[8,112,128]{2,1,0:T(8,128)} %all-to-all-done.cq_ref, bf16[128,768]{1,0:T(8,128)(2,1)S(1)} %copy-done.7, f32[64,3072]{1,0:T(8,128)S(1)} %copy-done.5, f32[64,3072]{1,0:T(8,128)} %collective-permute-done.came_ref), custom_call_target="tpu_custom_call" | custom-call | tf_op jit(solution)/shard_map/pallas_call | solution.py:122
  33.7 39.0 %all_to_all.25 = s16[256,8,128]{2,1,0:T(8,128)(2,1)S(1)} all-to-all(s16[256,8,128]{2,1,0:T(8,128)(2,1)S(1)} %bitcast.39), channel_id=1, replica_groups=mesh['x'=4,'y'=8,'h'=2,'l'=4,'c'=2] {'x','y','h','l'}, dimensions={0} | all-to-all | bytes 1048576 | tf_op jit(solution)/shard_map/all_to_all | solution.py:28
  72.7 1.1 shard_map.114
  73.8 30.6 %all_to_all.26 = s16[256,8,128]{2,1,0:T(8,128)(2,1)} all-to-all(s16[256,8,128]{2,1,0:T(8,128)(2,1)S(1)} %bitcast.38), channel_id=1, replica_groups=mesh['x'=4,'y'=8,'h'=2,'l'=4,'c'=2] {'x','y','h','l'}, dimensions={0} | all-to-all | bytes 1048576 | tf_op jit(solution)/shard_map/all_to_all | solution.py:28
  104.4 2.1 %collective-permute-start.1 = (s16[2048,128]{1,0:T(8,128)(2,1)}, s16[2048,128]{1,0:T(8,128)(2,1)}, u32[]{:S(2)}, u32[]{:S(2)}) collective-permute-start(s16[2048,128]{1,0:T(8,128)(2,1)} %bitcast.13.mine_ref), channel_id=1, source_target_pairs={{0,1},{1,0},{2,3},{3,2},{4,5},{5,4},{6,7},{7,6},{8,9},{9,8},{10,11... | collective-permute-start | bytes 1572872 | tf_op jit(solution)/shard_map/ppermute | solution.py:32
  106.5 1.0 slice_reduce_fusion
  107.5 0.1 reshape.64
  107.6 0.1 reshape.65
  107.7 0.0 all-gather.2.cloned.1.call-done.attn_ref
  107.7 1.4 copy-done.6
  109.1 2.4 %shard_map.115.grad_ref = bf16[6144,256]{1,0:T(8,128)(2,1)S(1)} custom-call(bf16[128,6144]{1,0:T(8,128)(2,1)S(1)} %copy-done.6, bf16[128,128]{1,0:T(8,128)(2,1)S(1)} %copy-done.9, bf16[6144,128]{1,0:T(8,128)(2,1)S(1)} %bitcast.36), custom_call_target="tpu_custom_call" | custom-call | flops 201326592 | bytes 6291456 | tf_op jit(solution)/shard_map/pallas_call | solution.py:168
  111.5 0.0 collective-permute-done.1.other_ref
  111.5 4.9 %shard_map.116 = (f32[64,128]{1,0:T(8,128)S(1)}, f32[64,64]{1,0:T(8,128)S(1)}, bf16[24,128,256]{2,1,0:T(8,128)(2,1)S(1)}) custom-call(s32[1]{0:T(128)} %bitcast.1.block_ref.core_ref, s16[2048,128]{1,0:T(8,128)(2,1)} %bitcast.13.mine_ref, s16[2048,128]{1,0:T(8,128)(2,1)} %collective-permute-done.1.other_ref, bf16[6144,256]{1,0:T(8,128)(2,1)S(1)} %shard_map.115.grad_ref), custom_call_target="tpu_custom_call" | custom-call | tf_op jit(solution)/shard_map/pallas_call | solution.py:224
  116.5 0.7 pad_maximum_fusion.1
  117.2 3.8 %all-to-all-start.3 = ((f32[8,70,128]{2,1,0:T(8,128)}), f32[8,70,128]{2,1,0:T(8,128)S(1)}, u32[]{:S(2)}, u32[]{:S(2)}) async-start(f32[8,70,128]{2,1,0:T(8,128)} %pad_maximum_fusion.1), calls=%async_computation.3 | async-start | bytes 589824 | tf_op jit(solution)/shard_map/all_to_all | solution.py:28
  121.0 5.8 %cholesky.17 = f32[64,64]{1,0:T(8,128)S(1)} custom-call(f32[64,64]{1,0:T(8,128)S(1)} %get-tuple-element.11), custom_call_target="Cholesky" | custom-call | tf_op jit(solution)/shard_map/jit(cholesky)/cholesky | solution.py:328
  126.9 7.4 %all-to-all-done.3 = f32[8,70,128]{2,1,0:T(8,128)S(1)} async-done(((f32[8,70,128]{2,1,0:T(8,128)}), f32[8,70,128]{2,1,0:T(8,128)S(1)}, u32[]{:S(2)}, u32[]{:S(2)}) %all-to-all-start.3) | async-done | bytes 286752 | tf_op jit(solution)/shard_map/all_to_all | solution.py:28
  134.3 0.1 reshape.66
  134.4 0.7 select_maximum_fusion
  135.1 5.2 %all-to-all-start.4 = ((f32[8,65,128]{2,1,0:T(8,128)}), f32[8,65,128]{2,1,0:T(8,128)S(1)}, u32[]{:S(2)}, u32[]{:S(2)}) async-start(f32[8,65,128]{2,1,0:T(8,128)} %select_maximum_fusion), calls=%async_computation.4 | async-start | bytes 589824 | tf_op jit(solution)/shard_map/all_to_all | solution.py:28
  140.3 0.6 compare_reduce_fusion
  140.9 0.7 fusion.2
  141.6 4.9 %custom-call.6 = f32[1,64,64]{1,2,0:T(8,128)S(1)} custom-call(f32[1,64,64]{2,1,0:T(8,128)S(1)} %fusion.2), custom_call_target="InvertDiagBlocksLowerTriangular" | custom-call | tf_op jit(solution)/shard_map/triangular_solve | solution.py:329
  146.5 0.2 fusion.6.inverse_ref
  146.7 8.5 %all-to-all-done.4.sums_ref = f32[8,65,128]{2,1,0:T(8,128)S(1)} async-done(((f32[8,65,128]{2,1,0:T(8,128)}), f32[8,65,128]{2,1,0:T(8,128)S(1)}, u32[]{:S(2)}, u32[]{:S(2)}) %all-to-all-start.4) | async-done | bytes 266272 | tf_op jit(solution)/shard_map/all_to_all | solution.py:28
  155.2 1.9 %copy-done.2 = bf16[6144,256]{1,0:T(8,128)(2,1)S(1)} copy-done((bf16[6144,256]{1,0:T(8,128)(2,1)S(1)}, bf16[6144,256]{1,0:T(8,128)(2,1)}, u32[]{:S(2)}) %copy-start.2) | copy-done | bytes 3145752
  157.1 2.5 %shard_map.117 = (bf16[96,128]{1,0:T(8,128)(2,1)}, f32[128,64]{1,0:T(8,128)S(1)}, bf16[6144,128]{1,0:T(8,128)(2,1)}, f32[1,96]{1,0:T(1,128)}) custom-call(s32[1]{0:T(128)} %bitcast.place_ref, f32[64,64]{1,0:T(8,128)S(1)} %fusion.6.inverse_ref, f32[8,65,128]{2,1,0:T(8,128)S(1)} %all-to-all-done.4.sums_ref, bf16[24,128,256]{2,1,0:T(8,128)(2,1)S(1)} %get-tuple-element.13.p_ref, ...), custom_call_target="tpu_custom_call" | custom-call | tf_op jit(solution)/shard_map/pallas_call | solution.py:264
  159.6 0.7 copy.20
  (20 shorter events, 0.2 us)
Async XLA Ops:
  7.2 1.6 copy-start
  7.2 2.1 %copy-start.8 = (f32[128,64]{0,1:T(8,128)S(1)}, f32[128,64]{0,1:T(8,128)}, u32[]{:S(2)}) copy-start(f32[128,64]{0,1:T(8,128)} %param.11) | copy-start | bytes 98308
  7.2 2.1 %copy-start.9 = (bf16[128,128]{1,0:T(8,128)(2,1)S(1)}, bf16[128,128]{1,0:T(8,128)(2,1)}, u32[]{:S(2)}) copy-start(bf16[128,128]{1,0:T(8,128)(2,1)} %cols_ref.1) | copy-start | bytes 98308
  9.3 10.1 %copy-start.3 = (bf16[1,6144,128]{2,1,0:T(8,128)(2,1)S(1)}, bf16[1,6144,128]{2,1,0:T(8,128)(2,1)}, u32[]{:S(2)}) copy-start(bf16[1,6144,128]{2,1,0:T(8,128)(2,1)} %param.10) | copy-start | bytes 4718596
  10.4 20.2 %all-to-all-start = ((f32[8,112,128]{2,1,0:T(8,128)}), f32[8,112,128]{2,1,0:T(8,128)}, u32[]{:S(2)}, u32[]{:S(2)}) async-start(f32[8,112,128]{2,1,0:T(8,128)} %pad_maximum_fusion), calls=%async_computation | async-start | bytes 917504 | tf_op jit(solution)/shard_map/all_to_all | solution.py:28
  19.4 88.3 %all-gather.2.cloned.1.call-start = ((), (), s32[]{:S(2)}) async-start(), calls=%async_computation.5 | async-start | bytes 1769472 | tf_op jit(solution)/shard_map/all_gather | solution.py:296
  21.6 9.0 %copy-start.7 = (bf16[128,768]{1,0:T(8,128)(2,1)S(1)}, bf16[128,768]{1,0:T(8,128)(2,1)}, u32[]{:S(2)}) copy-start(bf16[128,768]{1,0:T(8,128)(2,1)} %attn_ref.1) | copy-start | bytes 589828
  21.6 4.6 %collective-permute-start = (f32[64,3072]{1,0:T(8,128)}, f32[64,3072]{1,0:T(8,128)}, u32[]{:S(2)}, u32[]{:S(2)}) collective-permute-start(f32[64,3072]{1,0:T(8,128)} %shard_map.112), channel_id=1, source_target_pairs={{0,1},{1,0},{2,3},{3,2},{4,5},{5,4},{6,7},{7,6},{8,9},{9,8},{10,11... | collective-permute-start | bytes 2359304 | tf_op jit(solution)/shard_map/ppermute | solution.py:32
  24.9 0.9 copy-start.4
  30.6 1.1 copy-start.5
  104.4 7.1 %collective-permute-start.1 = (s16[2048,128]{1,0:T(8,128)(2,1)}, s16[2048,128]{1,0:T(8,128)(2,1)}, u32[]{:S(2)}, u32[]{:S(2)}) collective-permute-start(s16[2048,128]{1,0:T(8,128)(2,1)} %bitcast.13.mine_ref), channel_id=1, source_target_pairs={{0,1},{1,0},{2,3},{3,2},{4,5},{5,4},{6,7},{7,6},{8,9},{9,8},{10,11... | collective-permute-start | bytes 1572872 | tf_op jit(solution)/shard_map/ppermute | solution.py:32
  107.7 1.4 copy-start.6
  111.5 4.9 %copy-start.1 = (bf16[6144,256]{1,0:T(8,128)(2,1)}, bf16[6144,256]{1,0:T(8,128)(2,1)S(1)}, u32[]{:S(2)}) copy-start(bf16[6144,256]{1,0:T(8,128)(2,1)S(1)} %shard_map.115.grad_ref) | copy-start | bytes 9437188
  117.2 17.0 %all-to-all-start.3 = ((f32[8,70,128]{2,1,0:T(8,128)}), f32[8,70,128]{2,1,0:T(8,128)S(1)}, u32[]{:S(2)}, u32[]{:S(2)}) async-start(f32[8,70,128]{2,1,0:T(8,128)} %pad_maximum_fusion.1), calls=%async_computation.3 | async-start | bytes 589824 | tf_op jit(solution)/shard_map/all_to_all | solution.py:28
  135.1 20.1 %all-to-all-start.4 = ((f32[8,65,128]{2,1,0:T(8,128)}), f32[8,65,128]{2,1,0:T(8,128)S(1)}, u32[]{:S(2)}, u32[]{:S(2)}) async-start(f32[8,65,128]{2,1,0:T(8,128)} %select_maximum_fusion), calls=%async_computation.4 | async-start | bytes 589824 | tf_op jit(solution)/shard_map/all_to_all | solution.py:28
  155.2 1.9 %copy-start.2 = (bf16[6144,256]{1,0:T(8,128)(2,1)S(1)}, bf16[6144,256]{1,0:T(8,128)(2,1)}, u32[]{:S(2)}) copy-start(bf16[6144,256]{1,0:T(8,128)(2,1)} %copy-done.1) | copy-start | bytes 9437188
Sparse Core Ops, SparseCore 0:
  23.9 46.5 all-gather.1

commit v3 on v2

v3 whole, which is shorter than its diff:
```python
import functools

import jax
import jax.numpy as jnp
from jax import lax
from jax.experimental import pallas as pl
from jax.experimental.pallas import tpu as pltpu
from jax.sharding import Mesh, PartitionSpec as P

HIGH = lax.Precision.HIGHEST
F32, BF16, I16 = jnp.float32, jnp.bfloat16, jnp.int16
RANK = 64
WIDTH = 6144
BLOCK = 768
DP = ("x", "y", "h")
EXPERT = ("l", "c")
FLAT = ("x", "y", "h", "l")
LIMIT = 12 * 1024 * 1024
TOP = 32000.0
STEP = 64.0
USED = 96

VMEM = pl.BlockSpec(memory_space=pltpu.VMEM)
SMEM = pl.BlockSpec(memory_space=pltpu.SMEM)
ANY = pl.BlockSpec(memory_space=pl.ANY)


def exchange(values, axes):
    return lax.all_to_all(values, axes, split_axis=0, concat_axis=0, tiled=True)


def swap_cores(values):
    return lax.ppermute(values, "c", [(0, 1), (1, 0)])


def three(values):
    high = values.astype(BF16)
    rest = values - high.astype(F32)
    middle = rest.astype(BF16)
    low = (rest - middle.astype(F32)).astype(BF16)
    return jnp.concatenate([high, middle, low], axis=0)


def folded(stacked):
    return stacked[:RANK] + stacked[RANK : 2 * RANK] + stacked[2 * RANK :]


def scale_of(largest):
    exponent = jnp.ceil(STEP * jnp.log2(jnp.maximum(largest, 1e-30))) + 1.0
    return exponent, jnp.exp2(exponent * (-1.0 / STEP)) * TOP


def lanes_of(shape):
    return lax.broadcasted_iota(jnp.int32, shape, 1)


def coded(values):
    return jnp.round(values).astype(jnp.int32).astype(I16)


def decoded(tile):
    wide = tile.astype(jnp.int32).astype(F32)
    return wide * (jnp.exp2(wide[:, 127:128] * (1.0 / STEP)) * (1.0 / TOP))


def error_kernel(block_ref, q_ref, error_ref, attn_ref, out_ref, pass_ref):
    del block_ref
    pass_ref[...] = attn_ref[...]
    out_ref[...] = folded(
        lax.dot_general(
            three(q_ref[...]), error_ref[...], (((1,), (1,)), ((), ())), preferred_element_type=F32
        )
    )


def error_share(power_t, error, core, attn_out):
    return pl.pallas_call(
        error_kernel,
        grid_spec=pltpu.PrefetchScalarGridSpec(
            num_scalar_prefetch=1,
            grid=(4,),
            in_specs=[
                pl.BlockSpec((RANK, 128), lambda i, core: (0, 0)),
                pl.BlockSpec((BLOCK, 128), lambda i, core: (2 * i + core[0], 0)),
                pl.BlockSpec((32, BLOCK), lambda i, core: (i, 0)),
            ],
            out_specs=[
                pl.BlockSpec((RANK, BLOCK), lambda i, core: (0, i)),
                pl.BlockSpec((32, BLOCK), lambda i, core: (i, 0)),
            ],
        ),
        out_shape=[
            jax.ShapeDtypeStruct((RANK, 4 * BLOCK), F32),
            jax.ShapeDtypeStruct((128, BLOCK), BF16),
        ],
        compiler_params=pltpu.CompilerParams(vmem_limit_bytes=LIMIT),
        cost_estimate=pl.CostEstimate(
            flops=2 * 192 * 128 * 3072, bytes_accessed=3072 * 512, transcendentals=0
        ),
    )(core.reshape(1), power_t, error, attn_out)


def share_kernel(place_ref, cq_ref, attn_ref, kept_ref, came_ref, out_ref, half_ref):
    cq = jnp.sum(cq_ref[:, :RANK, :], axis=0)
    from_attn = folded(jnp.dot(three(cq), attn_ref[...], preferred_element_type=F32))
    half_ref[...] = kept_ref[...] + came_ref[...]
    here = pl.ds(pl.multiple_of(place_ref[0] * BLOCK, BLOCK), BLOCK)
    half_ref[:, here] += from_attn
    lane = lanes_of((8, 128))
    for band in range(8):
        rows = slice(band * 8, band * 8 + 8)
        tiles = [half_ref[rows, t * 128 : t * 128 + 128] for t in range(24)]
        largest = functools.reduce(jnp.maximum, [jnp.abs(t) for t in tiles])
        exponent, factor = scale_of(jnp.max(largest, axis=1, keepdims=True))
        exponent = jnp.broadcast_to(exponent, (8, 128))
        factor = jnp.broadcast_to(factor, (8, 128))
        for group in range(8):
            a, b, c = (t * factor for t in tiles[group * 3 : group * 3 + 3])
            tail = jnp.where(
                lane < 32,
                pltpu.roll(a, 32, 1),
                jnp.where(lane < 64, pltpu.roll(b, 64, 1), pltpu.roll(c, 96, 1)),
            )
            a, b, c, tail = (jnp.where(lane < USED, t, exponent) for t in (a, b, c, tail))
            at = (band * 32 + group * 4) * 8
            out_ref[at : at + 16, :] = coded(jnp.concatenate([a, b], axis=0))
            out_ref[at + 16 : at + 32, :] = coded(jnp.concatenate([c, tail], axis=0))


def share_of(place, cq_all, attn_out, kept, came):
    return pl.pallas_call(
        share_kernel,
        in_specs=[SMEM, VMEM, VMEM, VMEM, VMEM],
        out_specs=VMEM,
        out_shape=jax.ShapeDtypeStruct((2048, 128), I16),
        scratch_shapes=[pltpu.VMEM((RANK, 4 * BLOCK), F32)],
        compiler_params=pltpu.CompilerParams(vmem_limit_bytes=LIMIT),
        cost_estimate=pl.CostEstimate(
            flops=2 * 192 * 128 * 768, bytes_accessed=6000000, transcendentals=0
        ),
    )(place.reshape(1), cq_all, attn_out, kept, came)


def sum_kernel(in_ref, grad_ref, out_ref):
    del grad_ref

    def step(i, total):
        at = pl.multiple_of(i * 64, 64)
        parts = [decoded(in_ref[pl.ds(at + 16 * j, 16), :]) for j in range(4)]
        return total + ((parts[0] + parts[1]) + (parts[2] + parts[3]))

    total = lax.fori_loop(0, 32, step, jnp.zeros((16, 128), F32), unroll=4)
    total = total[:8] + total[8:]
    used = lanes_of((8, 128)) < USED
    largest = jnp.max(jnp.where(used, jnp.abs(total), 0.0), axis=1, keepdims=True)
    exponent, factor = scale_of(largest)
    tile = jnp.where(used, total * factor, exponent)
    tile = coded(jnp.concatenate([tile, tile], axis=0))
    out_ref[...] = jnp.broadcast_to(tile[None], (128, 16, 128)).reshape(2048, 128)


def summed(received, grad):
    return pl.pallas_call(
        sum_kernel,
        in_specs=[VMEM, ANY],
        out_specs=VMEM,
        out_shape=jax.ShapeDtypeStruct((2048, 128), I16),
        compiler_params=pltpu.CompilerParams(vmem_limit_bytes=LIMIT),
        cost_estimate=pl.CostEstimate(flops=1000000, bytes_accessed=1500000, transcendentals=0),
    )(received, grad)


def grad_kernel(at_ref, own_ref, other_ref, cols_ref, error_ref, out_ref):
    step = pl.program_id(0)
    mine = lax.rem(step, 2) == at_ref[1]
    attn = jnp.where(mine, own_ref[0], other_ref[0])
    grad = lax.dot_general(
        attn, cols_ref[...], (((0,), (0,)), ((), ())), preferred_element_type=F32
    ) + error_ref[...].astype(F32)
    high = grad.astype(BF16)
    out_ref[:, :128] = high
    out_ref[:, 128:] = (grad - high.astype(F32)).astype(BF16)


def grad_of(place, core, own, other, out_cols, error):
    def slot(i, at):
        return (lax.rem(at[0] + 4 - i // 2, 4), 0, 0)

    return pl.pallas_call(
        grad_kernel,
        grid_spec=pltpu.PrefetchScalarGridSpec(
            num_scalar_prefetch=1,
            grid=(8,),
            in_specs=[
                pl.BlockSpec((1, 128, BLOCK), slot),
                pl.BlockSpec((1, 128, BLOCK), slot),
                pl.BlockSpec((128, 128), lambda i, at: (0, 0)),
                pl.BlockSpec((BLOCK, 128), lambda i, at: (i, 0)),
            ],
            out_specs=pl.BlockSpec((BLOCK, 256), lambda i, at: (i, 0)),
        ),
        out_shape=jax.ShapeDtypeStruct((WIDTH, 256), BF16),
        compiler_params=pltpu.CompilerParams(vmem_limit_bytes=LIMIT),
        cost_estimate=pl.CostEstimate(
            flops=2 * 128 * 128 * WIDTH, bytes_accessed=WIDTH * 1024, transcendentals=0
        ),
    )(jnp.stack([place, core]), own, other, out_cols, error)


def unpacked(ref, p_ref):
    lane = lanes_of((16, 128))
    for pair in range(4):
        for group in range(8):
            first, second = [], []
            for band in (2 * pair, 2 * pair + 1):
                at = (band * 32 + group * 4) * 8
                first.append(decoded(ref[at : at + 16, :]))
                second.append(decoded(ref[at + 16 : at + 32, :]))
            a = jnp.concatenate([t[:8] for t in first], axis=0)
            b = jnp.concatenate([t[8:] for t in first], axis=0)
            c = jnp.concatenate([t[:8] for t in second], axis=0)
            tail = jnp.concatenate([t[8:] for t in second], axis=0)
            for j, (tile, shift) in enumerate(((a, 96), (b, 64), (c, 32))):
                tile = jnp.where(lane < USED, tile, pltpu.roll(tail, shift, 1))
                place = group * 3 + j
                lanes = slice(128 * (place % 2), 128 * (place % 2) + 128)
                high = tile.astype(BF16)
                low = (tile - high.astype(F32)).astype(BF16)
                p_ref[place // 2, pair * 16 : pair * 16 + 16, lanes] = high
                p_ref[place // 2, RANK + pair * 16 : RANK + pair * 16 + 16, lanes] = low


def rows_of(i, core):
    return pl.ds(pl.multiple_of((2 * (i // 3) + core) * BLOCK + (i % 3) * 256, 256), 256)


def product(p_ref, grad_ref, core):
    total = jnp.zeros((128, 256), F32)
    for i in range(12):
        total += jnp.dot(p_ref[i], grad_ref[rows_of(i, core), :], preferred_element_type=F32)
    total = total[:RANK] + total[RANK:]
    return total[:, :128] + total[:, 128:]


def squared(p_ref):
    total = jnp.zeros((128, 128), F32)
    for i in range(12):
        total += lax.dot_general(
            p_ref[i], p_ref[i], (((1,), (1,)), ((), ())), preferred_element_type=F32
        )
    total = total[:RANK] + total[RANK:]
    return total[:, :RANK] + total[:, RANK:]


def mine_kernel(core_ref, codes_ref, grad_ref, raw_ref, gram_ref, p_ref):
    unpacked(codes_ref, p_ref)
    raw_ref[...] = product(p_ref, grad_ref, core_ref[0])
    gram_ref[...] = squared(p_ref)


def other_kernel(
    core_ref, codes_ref, grad_ref, mine_ref, square_ref, expert_ref, out_ref, gram_ref, p_ref
):
    unpacked(codes_ref, p_ref)
    gram_ref[...] = square_ref[...] + squared(p_ref)
    raw = mine_ref[...] + product(p_ref, grad_ref, 1 - core_ref[0])
    for i in range(8):
        out_ref[i, :RANK, :] = raw
        out_ref[i, RANK:, :] = expert_ref[i]


SQUARE = jax.ShapeDtypeStruct((RANK, RANK), F32)
HALF = jax.ShapeDtypeStruct((12, 128, 256), BF16)
HALF_COST = pl.CostEstimate(flops=2 * 128 * 256 * 3072, bytes_accessed=3000000, transcendentals=0)


def mine_of(core, codes, grad):
    return pl.pallas_call(
        mine_kernel,
        in_specs=[SMEM, VMEM, VMEM],
        out_specs=[VMEM, VMEM, VMEM],
        out_shape=[jax.ShapeDtypeStruct((RANK, 128), F32), SQUARE, HALF],
        compiler_params=pltpu.CompilerParams(vmem_limit_bytes=LIMIT),
        cost_estimate=HALF_COST,
    )(core.reshape(1), codes, grad)


def other_of(core, codes, grad, raw, square, by_y):
    return pl.pallas_call(
        other_kernel,
        in_specs=[SMEM, VMEM, VMEM, VMEM, VMEM, VMEM],
        out_specs=[VMEM, VMEM, VMEM],
        out_shape=[jax.ShapeDtypeStruct((8, RANK + 6, 128), F32), SQUARE, HALF],
        compiler_params=pltpu.CompilerParams(vmem_limit_bytes=LIMIT),
        cost_estimate=HALF_COST,
    )(core.reshape(1), codes, grad, raw, square, by_y)


def final_kernel(
    at_ref, inverse_ref, sums_ref, mine_ref, other_ref, grad_ref,
    approx_ref, q_ref, error_ref, expert_ref, full_ref,
):
    sums = jnp.sum(sums_ref[...], axis=0)
    expert_ref[...] = sums[RANK : RANK + 1, :USED]
    inverse = inverse_ref[...]
    q_t = jnp.dot(inverse, sums[:RANK], precision=HIGH) * (1.0 / 64.0)
    q_ref[...] = q_t
    weights = jnp.dot(inverse.T, q_t, precision=HIGH)
    high = weights.astype(BF16)
    low = (weights - high.astype(F32)).astype(BF16)
    both = jnp.concatenate([high, low], axis=1)
    both = jnp.concatenate([both, both], axis=0)
    for ref, core in ((mine_ref, at_ref[1]), (other_ref, 1 - at_ref[1])):
        for i in range(12):
            rows = rows_of(i, core)
            part = lax.dot_general(
                ref[i], both, (((0,), (0,)), ((), ())), preferred_element_type=F32
            )
            part = part[:, :128] + part[:, 128:]
            full_ref[rows, :] = part
            grad = grad_ref[rows, :].astype(F32)
            error_ref[rows, :] = (grad[:, :128] + grad[:, 128:] - part).astype(BF16)
    here = pl.ds(pl.multiple_of(at_ref[0] * 96, 32), 96)
    approx_ref[...] = full_ref[here, :].astype(BF16)


def final_of(data, core, inverse, sums, p_mine, p_other, grad):
    return pl.pallas_call(
        final_kernel,
        in_specs=[SMEM, VMEM, VMEM, VMEM, VMEM, VMEM],
        out_specs=[VMEM] * 4,
        out_shape=[
            jax.ShapeDtypeStruct((96, 128), BF16),
            jax.ShapeDtypeStruct((RANK, 128), F32),
            jax.ShapeDtypeStruct((WIDTH, 128), BF16),
            jax.ShapeDtypeStruct((1, USED), F32),
        ],
        scratch_shapes=[pltpu.VMEM((WIDTH, 128), F32)],
        compiler_params=pltpu.CompilerParams(vmem_limit_bytes=LIMIT),
    )(jnp.stack([data, core]), inverse, sums, p_mine, p_other, grad)


def first_kernel(q_ref, cols_ref, tokens_ref, routes_ref, logits_ref, score_ref, out_ref):
    part = folded(
        lax.dot_general(
            three(q_ref[...]), cols_ref[...], (((1,), (1,)), ((), ())), preferred_element_type=F32
        )
    )
    for i in range(8):
        out_ref[i, :RANK, :] = part
    first = 1.0 / (1.0 + jnp.exp(logits_ref[1:2, :] - logits_ref[0:1, :]))
    rows = first * (1.0 - first) * (score_ref[0:1, :] - score_ref[1:2, :])
    rows = jnp.broadcast_to(rows, (8, 128))
    label = lax.broadcasted_iota(jnp.int32, (8, 128), 0)
    spread = jnp.where(routes_ref[0:1, :] == label, rows, 0.0) - jnp.where(
        routes_ref[1:2, :] == label, rows, 0.0
    )
    experts = jnp.dot(spread.astype(BF16), tokens_ref[...], preferred_element_type=F32)
    for t in range(48):
        out_ref[:, RANK + t, :] = experts[:, t * 128 : t * 128 + 128]


def first_of(power_t, out_cols, tokens, routes_t, logits_t, score_t):
    return pl.pallas_call(
        first_kernel,
        in_specs=[VMEM] * 6,
        out_specs=VMEM,
        out_shape=jax.ShapeDtypeStruct((8, RANK + 48, 128), F32),
        compiler_params=pltpu.CompilerParams(vmem_limit_bytes=LIMIT),
    )(power_t, out_cols, tokens, routes_t, logits_t, score_t)


def local(attn_out, out_cols, error_in, power_q, tokens, routes, route_logits, pair_score):
    error = error_in[0]
    core = lax.axis_index("c").astype(jnp.int32)
    place = lax.axis_index("l").astype(jnp.int32)
    data = (lax.axis_index("x") * 8 + lax.axis_index("y")) * 2 + lax.axis_index("h")
    power_t = power_q.T

    cq_all = exchange(
        first_of(power_t, out_cols, tokens, routes.T, route_logits.T, pair_score.T), EXPERT
    )
    by_y = jnp.sum(cq_all[:, RANK:], axis=0).reshape(4, 8, 2, 96)
    by_y = by_y.transpose(1, 0, 2, 3).reshape(8, 6, 128)

    given, attn_first = error_share(power_t, error, 1 - core, attn_out)
    came = swap_cores(given)
    kept, attn_here = error_share(power_t, error, core, attn_first)
    shifted = [
        lax.ppermute(attn_here, "l", [(i, (i + k) % 4) for i in range(4)]) for k in (1, 2, 3)
    ]
    codes = share_of(place, cq_all, attn_out, kept, came)
    own = jnp.stack([attn_here, *shifted])
    grad = grad_of(place, core, own, swap_cores(own), out_cols, error)
    piece = summed(exchange(codes.reshape(256, 8, 128), FLAT).reshape(2048, 128), grad)
    mine = exchange(piece.reshape(256, 8, 128), FLAT).reshape(2048, 128)
    other = swap_cores(mine)
    raw, square, p_mine = mine_of(core, mine, grad)
    send, gram, p_other = other_of(core, other, grad, raw, square, by_y)

    over_y = jnp.sum(exchange(send, "y"), axis=0)
    rest = jnp.pad(over_y[RANK:].reshape(8, 1, 96), ((0, 0), (0, 0), (0, 32)))
    sums = exchange(
        jnp.concatenate([jnp.broadcast_to(over_y[:RANK], (8, RANK, 128)), rest], axis=1),
        ("x", "h"),
    )

    factor = jnp.linalg.cholesky(gram, symmetrize_input=False)
    inverse = lax.linalg.triangular_solve(
        factor, jnp.eye(RANK, dtype=F32), left_side=True, lower=True
    )
    approx, q_t, error_out, expert_grad = final_of(
        data.astype(jnp.int32), core, inverse, sums, p_mine, p_other, grad
    )
    return approx, q_t.T, error_out[None], expert_grad


def solution(mesh):
    fine = Mesh(mesh.devices.reshape(4, 8, 2, 4, 2), DP + EXPERT)
    everyone = P(DP + EXPERT, None)
    return jax.shard_map(
        local,
        mesh=fine,
        in_specs=(
            P(DP, EXPERT),
            P(DP, EXPERT),
            P(DP, None, EXPERT),
            P(EXPERT, None),
            everyone,
            everyone,
            everyone,
            everyone,
        ),
        out_specs=(P(DP, EXPERT), P(EXPERT, None), P(DP, None, EXPERT), P(EXPERT, DP)),
        check_vma=False,
    )
```

time: 168 us -> 160 us (0.952)
  blocking collectives: 69.6 us -> 28.9 us
  starting transfers between devices: 22.2 us -> 53.2 us
  between operations: 14.3 us -> 0.94 us
  waiting for transfers between devices: 20.7 us -> 28.9 us
  local copies, waits for them, and re-layouts: 7.22 us -> 12.1 us
  Pallas kernels: 16 us -> 19 us
    all_to_all x2 -> x1, blocking collectives: 69.6 us -> 28.9 us  [exchange(): return lax.all_to_all(values, axes, split_axis=0, concat_axis=0, tiled=True)]
    all_to_all x3 -> x4, starting transfers between devices: 18 us -> 36.1 us  [exchange(): return lax.all_to_all(values, axes, split_axis=0, concat_axis=0, tiled=True)]
    ppermute x0 -> x3, starting transfers between devices: none -> 11 us  [local(): lax.ppermute(attn_here, 'l', [(i, (i + k) % 4) for i in range(4)])]
    all_to_all x3 -> x4, waiting for transfers between devices: 20.2 us -> 26.8 us  [exchange(): return lax.all_to_all(values, axes, split_axis=0, concat_axis=0, tiled=True)]
    unnamed x22 -> x36, local copies, waits for them, and re-layouts: 6.07 us -> 11.8 us
    pallas_call x4 -> x6, Pallas kernels: 10.8 us -> 14.3 us  [the longest x1 3.02 us: final_of(): pl.pallas_call(final_kernel, in_specs=[SMEM, VMEM, VMEM, VMEM, VMEM, VMEM...]
    ppermute x2 -> x3, starting transfers between devices: 4.27 us -> 6.05 us  [swap_cores(): return lax.ppermute(values, 'c', [(0, 1), (1, 0)])]
    ppermute x2 -> x3, waiting for transfers between devices: 0.46 us -> 2.18 us  [swap_cores(): return lax.ppermute(values, 'c', [(0, 1), (1, 0)])]
  transfers between devices with their start and end apart: 6 -> 10, of which waited for: 4 -> 4; matrix products, arithmetic and copies ran while one was open for 8% -> 9% of each run, Pallas kernels for 5% -> 6%
where the time goes in v3:
time: 160 us; the launch traced here: 158 us
  starting transfers between devices  53.2 us (33%)
  waiting for transfers between devices  28.9 us (18%)
  blocking collectives  28.9 us (18%)
  Pallas kernels  19 us (12%)
  other arithmetic  15 us (9%)
  local copies, waits for them, and re-layouts  12.1 us (8%)
    all_to_all x4, starting transfers between devices, exchange(): return lax.all_to_all(values, axes, split_axis=0, concat_axis=0, tiled=True)  36.1 us
    all_to_all x1, blocking collectives, exchange(): return lax.all_to_all(values, axes, split_axis=0, concat_axis=0, tiled=True)  28.9 us
    all_to_all x4, waiting for transfers between devices, exchange(): return lax.all_to_all(values, axes, split_axis=0, concat_axis=0, tiled=True)  26.8 us
    unnamed x36, local copies, waits for them, and re-layouts  11.8 us
    ppermute x3, starting transfers between devices, local(): lax.ppermute(attn_here, 'l', [(i, (i + k) % 4) for i in range(4)])  11 us
    another operation x3, other arithmetic, local(): factor = jnp.linalg.cholesky(gram, symmetrize_input=False)  6.51 us
    ppermute x3, starting transfers between devices, swap_cores(): return lax.ppermute(values, 'c', [(0, 1), (1, 0)])  6.05 us
    another operation x2, other arithmetic, local(): lax.linalg.triangular_solve(factor, jnp.eye(RANK, dtype=F32), left_side=T...  5.55 us
  transfers between devices with their start and end apart: 10, of which 4 were waited for; matrix products, arithmetic and copies ran while one was open for 9% of the time, Pallas kernels for 6%

profile of v3, /device:TPU:64, one launch (start us, length us, event | category | flops | bytes accessed | tf_op | source)
XLA Modules:
  0.0 158.4 jit_solution(13580936586323024475)
XLA Ops:
  0.7 1.5 copy-done.3
  2.2 0.8 copy-done.11
  2.9 0.8 copy-done.13
  3.7 0.7 copy-done.15
  4.4 0.7 copy-done.16
  5.0 0.7 copy-done.17
  5.7 1.2 shard_map.111
  6.9 8.4 %all-to-all-start = ((f32[8,112,128]{2,1,0:T(8,128)}), f32[8,112,128]{2,1,0:T(8,128)S(1)}, u32[]{:S(2)}, u32[]{:S(2)}) async-start(f32[8,112,128]{2,1,0:T(8,128)} %shard_map.111), calls=%async_computation | async-start | bytes 917504 | tf_op jit(solution)/shard_map/all_to_all | solution.py:29
  15.3 2.1 %shard_map.112 = (f32[64,3072]{1,0:T(8,128)}, bf16[128,768]{1,0:T(8,128)(2,1)S(1)}) custom-call(s32[1]{0:T(128)} %bitcast.8.block_ref, f32[64,128]{1,0:T(8,128)S(1)} %bitcast.30, bf16[6144,128]{1,0:T(8,128)(2,1)S(1)} %bitcast.25, bf16[128,768]{1,0:T(8,128)(2,1)S(1)} %copy-done.6), custom_call_target="tpu_custom_call" | custom-call | flops 150994944 | bytes 1572864 | tf_op jit(solution)/shard_map/pallas_call | solution.py:77
  17.4 2.0 %collective-permute-start = (f32[64,3072]{1,0:T(8,128)}, f32[64,3072]{1,0:T(8,128)S(1)}, u32[]{:S(2)}, u32[]{:S(2)}) collective-permute-start(f32[64,3072]{1,0:T(8,128)} %get-tuple-element.20), channel_id=1, source_target_pairs={{0,1},{1,0},{2,3},{3,2},{4,5},{5,4},{6,7},{7,6},{8,9},{9,8},{10,11... | collective-permute-start | bytes 2359304 | tf_op jit(solution)/shard_map/ppermute | solution.py:33
  19.5 1.1 shard_map.113
  20.6 0.9 copy-done.4
  21.5 2.3 %collective-permute-start.3 = (bf16[128,768]{1,0:T(8,128)(2,1)S(1)}, bf16[128,768]{1,0:T(8,128)(2,1)S(1)}, u32[]{:S(2)}, u32[]{:S(2)}) collective-permute-start(bf16[128,768]{1,0:T(8,128)(2,1)S(1)} %get-tuple-element.21), channel_id=1, source_target_pairs={{0,6},{2,0},{4,2},{6,4},{1,7},{3,1},{5,3},{7,5},{8,14},{10,8},{12,... | collective-permute-start | bytes 589832 | tf_op jit(solution)/shard_map/ppermute | solution.py:390
  23.7 4.5 %collective-permute-start.2 = (bf16[128,768]{1,0:T(8,128)(2,1)S(1)}, bf16[128,768]{1,0:T(8,128)(2,1)S(1)}, u32[]{:S(2)}, u32[]{:S(2)}) collective-permute-start(bf16[128,768]{1,0:T(8,128)(2,1)S(1)} %get-tuple-element.21), channel_id=1, source_target_pairs={{0,4},{2,6},{4,0},{6,2},{1,5},{3,7},{5,1},{7,3},{8,12},{10,14},{12... | collective-permute-start | bytes 589832 | tf_op jit(solution)/shard_map/ppermute | solution.py:390
  28.2 4.3 %collective-permute-start.1 = (bf16[128,768]{1,0:T(8,128)(2,1)S(1)}, bf16[128,768]{1,0:T(8,128)(2,1)S(1)}, u32[]{:S(2)}, u32[]{:S(2)}) collective-permute-start(bf16[128,768]{1,0:T(8,128)(2,1)S(1)} %get-tuple-element.21), channel_id=1, source_target_pairs={{0,2},{2,4},{4,6},{6,0},{1,3},{3,5},{5,7},{7,1},{8,10},{10,12},{12... | collective-permute-start | bytes 589832 | tf_op jit(solution)/shard_map/ppermute | solution.py:390
  32.6 1.3 copy-done.5
  33.9 1.5 shard_map.114
  35.4 18.3 %all-to-all-start.1 = ((s16[256,8,128]{2,1,0:T(8,128)(2,1)}), s16[256,8,128]{2,1,0:T(8,128)(2,1)}, u32[]{:S(2)}, u32[]{:S(2)}) async-start(s16[256,8,128]{2,1,0:T(8,128)(2,1)} %bitcast.9), calls=%async_computation.1 | async-start | bytes 1048576 | tf_op jit(solution)/shard_map/all_to_all | solution.py:29
  53.7 0.1 pad_maximum_fusion.own_ref
  53.8 1.9 %collective-permute-start.4 = (bf16[4,128,768]{2,1,0:T(8,128)(2,1)S(1)}, bf16[4,128,768]{2,1,0:T(8,128)(2,1)S(1)}, u32[]{:S(2)}, u32[]{:S(2)}) collective-permute-start(bf16[4,128,768]{2,1,0:T(8,128)(2,1)S(1)} %pad_maximum_fusion.own_ref), channel_id=1, source_target_pairs={{0,1},{1,0},{2,3},{3,2},{4,5},{5,4},{6,7},{7,6},{8,9},{9,8},{10,11... | collective-permute-start | bytes 2359304 | tf_op jit(solution)/shard_map/ppermute | solution.py:33
  55.8 2.2 %collective-permute-done.4.other_ref = bf16[4,128,768]{2,1,0:T(8,128)(2,1)S(1)} collective-permute-done((bf16[4,128,768]{2,1,0:T(8,128)(2,1)S(1)}, bf16[4,128,768]{2,1,0:T(8,128)(2,1)S(1)}, u32[]{:S(2)}, u32[]{:S(2)}) %collective-permute-start.4) | collective-permute-done | bytes 786464 | tf_op jit(solution)/shard_map/ppermute | solution.py:33
  58.0 1.4 copy-done.1
  59.4 2.9 %shard_map.115.grad_ref = bf16[6144,256]{1,0:T(8,128)(2,1)S(1)} custom-call(s32[2]{0:T(128)S(1)} %pad_add_fusion.1.at_ref, bf16[4,128,768]{2,1,0:T(8,128)(2,1)S(1)} %pad_maximum_fusion.own_ref, bf16[4,128,768]{2,1,0:T(8,128)(2,1)S(1)} %collective-permute-done.4.other_ref, bf16[128,128]{1,0:T(8,128)(2,1)S(1)} %copy-done.14, bf16[6144,128]{1,0:T(8,128)(2,1)S(1)} %bitcast.27), custom_call_target="tpu_custom_call" | custom-call | flops 201326592 | bytes 6291456 | tf_op jit(solution)/shard_map/pallas_call | solution.py:189
  62.3 10.7 %all-to-all-done.1 = s16[256,8,128]{2,1,0:T(8,128)(2,1)} async-done(((s16[256,8,128]{2,1,0:T(8,128)(2,1)}), s16[256,8,128]{2,1,0:T(8,128)(2,1)}, u32[]{:S(2)}, u32[]{:S(2)}) %all-to-all-start.1) | async-done | bytes 524320 | tf_op jit(solution)/shard_map/all_to_all | solution.py:29
  73.0 2.1 %shard_map.116 = s16[2048,128]{1,0:T(8,128)(2,1)S(1)} custom-call(s16[2048,128]{1,0:T(8,128)(2,1)} %bitcast.10.in_ref, bf16[6144,256]{1,0:T(8,128)(2,1)S(1)} %shard_map.115.grad_ref), custom_call_target="tpu_custom_call" | custom-call | flops 1000000 | bytes 1500000 | tf_op jit(solution)/shard_map/pallas_call | solution.py:163
  75.2 28.9 %all_to_all.25 = s16[256,8,128]{2,1,0:T(8,128)(2,1)} all-to-all(s16[256,8,128]{2,1,0:T(8,128)(2,1)S(1)} %bitcast.28), channel_id=1, replica_groups=mesh['x'=4,'y'=8,'h'=2,'l'=4,'c'=2] {'x','y','h','l'}, dimensions={0} | all-to-all | bytes 1048576 | tf_op jit(solution)/shard_map/all_to_all | solution.py:29
  104.1 2.1 %collective-permute-start.5 = (s16[2048,128]{1,0:T(8,128)(2,1)}, s16[2048,128]{1,0:T(8,128)(2,1)}, u32[]{:S(2)}, u32[]{:S(2)}) collective-permute-start(s16[2048,128]{1,0:T(8,128)(2,1)} %bitcast.16.codes_ref), channel_id=1, source_target_pairs={{0,1},{1,0},{2,3},{3,2},{4,5},{5,4},{6,7},{7,6},{8,9},{9,8},{10,11... | collective-permute-start | bytes 1572872 | tf_op jit(solution)/shard_map/ppermute | solution.py:33
  106.2 1.0 slice_reduce_fusion
  107.2 0.1 reshape.53
  107.3 0.1 reshape.54.expert_ref
  107.4 2.1 %shard_map.117 = (f32[64,128]{1,0:T(8,128)S(1)}, f32[64,64]{1,0:T(8,128)S(1)}, bf16[12,128,256]{2,1,0:T(8,128)(2,1)S(1)}) custom-call(s32[1]{0:T(128)} %bitcast.1.block_ref.core_ref, s16[2048,128]{1,0:T(8,128)(2,1)} %bitcast.16.codes_ref, bf16[6144,256]{1,0:T(8,128)(2,1)S(1)} %shard_map.115.grad_ref), custom_call_target="tpu_custom_call" | custom-call | flops 201326592 | bytes 3000000 | tf_op jit(solution)/shard_map/pallas_call | solution.py:278
  109.5 3.0 %shard_map.118 = (f32[8,70,128]{2,1,0:T(8,128)}, f32[64,64]{1,0:T(8,128)S(1)}, bf16[12,128,256]{2,1,0:T(8,128)(2,1)S(1)}) custom-call(s32[1]{0:T(128)} %bitcast.1.block_ref.core_ref, s16[2048,128]{1,0:T(8,128)(2,1)} %collective-permute-done.5.codes_ref, bf16[6144,256]{1,0:T(8,128)(2,1)S(1)} %shard_map.115.grad_ref, ...), custom_call_target="tpu_custom_call" | custom-call | flops 201326592 | bytes 3000000 | tf_op jit(solution)/shard_map/pallas_call | solution.py:289
  112.5 0.9 copy-done.9
  113.4 4.1 %all-to-all-start.3 = ((f32[8,70,128]{2,1,0:T(8,128)}), f32[8,70,128]{2,1,0:T(8,128)}, u32[]{:S(2)}, u32[]{:S(2)}) async-start(f32[8,70,128]{2,1,0:T(8,128)} %get-tuple-element.25), calls=%async_computation.3 | async-start | bytes 589824 | tf_op jit(solution)/shard_map/all_to_all | solution.py:29
  117.6 5.8 %cholesky.17 = f32[64,64]{1,0:T(8,128)S(1)} custom-call(f32[64,64]{1,0:T(8,128)S(1)} %get-tuple-element.24), custom_call_target="Cholesky" | custom-call | tf_op jit(solution)/shard_map/jit(cholesky)/cholesky | solution.py:408
  123.4 7.5 %all-to-all-done.3 = f32[8,70,128]{2,1,0:T(8,128)} async-done(((f32[8,70,128]{2,1,0:T(8,128)}), f32[8,70,128]{2,1,0:T(8,128)}, u32[]{:S(2)}, u32[]{:S(2)}) %all-to-all-start.3) | async-done | bytes 286752 | tf_op jit(solution)/shard_map/all_to_all | solution.py:29
  131.0 1.0 reduce_sum.19
  132.0 0.1 reshape.55
  132.1 0.8 select_maximum_fusion
  132.9 5.3 %all-to-all-start.4 = ((f32[8,65,128]{2,1,0:T(8,128)}), f32[8,65,128]{2,1,0:T(8,128)S(1)}, u32[]{:S(2)}, u32[]{:S(2)}) async-start(f32[8,65,128]{2,1,0:T(8,128)} %select_maximum_fusion), calls=%async_computation.4 | async-start | bytes 589824 | tf_op jit(solution)/shard_map/all_to_all | solution.py:29
  138.1 0.6 compare_reduce_fusion
  138.8 0.7 fusion
  139.4 4.9 %custom-call.6 = f32[1,64,64]{1,2,0:T(8,128)S(1)} custom-call(f32[1,64,64]{2,1,0:T(8,128)S(1)} %fusion), custom_call_target="InvertDiagBlocksLowerTriangular" | custom-call | tf_op jit(solution)/shard_map/triangular_solve | solution.py:409
  144.3 0.2 fusion.1.inverse_ref
  144.6 8.5 %all-to-all-done.4.sums_ref = f32[8,65,128]{2,1,0:T(8,128)S(1)} async-done(((f32[8,65,128]{2,1,0:T(8,128)}), f32[8,65,128]{2,1,0:T(8,128)S(1)}, u32[]{:S(2)}, u32[]{:S(2)}) %all-to-all-start.4) | async-done | bytes 266272 | tf_op jit(solution)/shard_map/all_to_all | solution.py:29
  153.1 1.1 copy-done.8
  154.2 1.1 copy-done.10
  155.3 3.0 %shard_map.119 = (bf16[96,128]{1,0:T(8,128)(2,1)}, f32[64,128]{1,0:T(8,128)}, bf16[6144,128]{1,0:T(8,128)(2,1)}, f32[1,96]{1,0:T(1,128)}) custom-call(s32[2]{0:T(128)S(1)} %pad_add_fusion.at_ref, f32[64,64]{1,0:T(8,128)S(1)} %fusion.1.inverse_ref, f32[8,65,128]{2,1,0:T(8,128)S(1)} %all-to-all-done.4.sums_ref, bf16[12,128,256]{2,1,0:T(8,128)(2,1)S(1)} %copy-done.8, ...), custom_call_target="tpu_custom_call" | custom-call | tf_op jit(solution)/shard_map/pallas_call | solution.py:328
  (37 shorter events, 0.3 us)
Async XLA Ops:
  0.6 14.7 %copy-start = (bf16[1,6144,128]{2,1,0:T(8,128)(2,1)S(1)}, bf16[1,6144,128]{2,1,0:T(8,128)(2,1)}, u32[]{:S(2)}) copy-start(bf16[1,6144,128]{2,1,0:T(8,128)(2,1)} %param.10) | copy-start | bytes 4718596
  0.6 1.5 copy-start.3
  2.2 0.8 copy-start.11
  2.9 0.8 copy-start.13
  3.7 0.7 copy-start.15
  4.4 0.7 copy-start.16
  5.0 0.7 copy-start.17
  5.7 9.6 %copy-start.6 = (bf16[128,768]{1,0:T(8,128)(2,1)S(1)}, bf16[128,768]{1,0:T(8,128)(2,1)}, u32[]{:S(2)}) copy-start(bf16[128,768]{1,0:T(8,128)(2,1)} %attn_ref.3) | copy-start | bytes 589828
  5.7 9.6 %copy-start.12 = (f32[128,64]{0,1:T(8,128)S(1)}, f32[128,64]{0,1:T(8,128)}, u32[]{:S(2)}) copy-start(f32[128,64]{0,1:T(8,128)} %param.11) | copy-start | bytes 98308
  6.9 25.7 %all-to-all-start = ((f32[8,112,128]{2,1,0:T(8,128)}), f32[8,112,128]{2,1,0:T(8,128)S(1)}, u32[]{:S(2)}, u32[]{:S(2)}) async-start(f32[8,112,128]{2,1,0:T(8,128)} %shard_map.111), calls=%async_computation | async-start | bytes 917504 | tf_op jit(solution)/shard_map/all_to_all | solution.py:29
  17.4 15.1 %collective-permute-start = (f32[64,3072]{1,0:T(8,128)}, f32[64,3072]{1,0:T(8,128)S(1)}, u32[]{:S(2)}, u32[]{:S(2)}) collective-permute-start(f32[64,3072]{1,0:T(8,128)} %get-tuple-element.20), channel_id=1, source_target_pairs={{0,1},{1,0},{2,3},{3,2},{4,5},{5,4},{6,7},{7,6},{8,9},{9,8},{10,11... | collective-permute-start | bytes 2359304 | tf_op jit(solution)/shard_map/ppermute | solution.py:33
  20.6 0.9 copy-start.4
  21.5 32.3 %collective-permute-start.3 = (bf16[128,768]{1,0:T(8,128)(2,1)S(1)}, bf16[128,768]{1,0:T(8,128)(2,1)S(1)}, u32[]{:S(2)}, u32[]{:S(2)}) collective-permute-start(bf16[128,768]{1,0:T(8,128)(2,1)S(1)} %get-tuple-element.21), channel_id=1, source_target_pairs={{0,6},{2,0},{4,2},{6,4},{1,7},{3,1},{5,3},{7,5},{8,14},{10,8},{12,... | collective-permute-start | bytes 589832 | tf_op jit(solution)/shard_map/ppermute | solution.py:390
  23.7 30.0 %collective-permute-start.2 = (bf16[128,768]{1,0:T(8,128)(2,1)S(1)}, bf16[128,768]{1,0:T(8,128)(2,1)S(1)}, u32[]{:S(2)}, u32[]{:S(2)}) collective-permute-start(bf16[128,768]{1,0:T(8,128)(2,1)S(1)} %get-tuple-element.21), channel_id=1, source_target_pairs={{0,4},{2,6},{4,0},{6,2},{1,5},{3,7},{5,1},{7,3},{8,12},{10,14},{12... | collective-permute-start | bytes 589832 | tf_op jit(solution)/shard_map/ppermute | solution.py:390
  28.2 25.5 %collective-permute-start.1 = (bf16[128,768]{1,0:T(8,128)(2,1)S(1)}, bf16[128,768]{1,0:T(8,128)(2,1)S(1)}, u32[]{:S(2)}, u32[]{:S(2)}) collective-permute-start(bf16[128,768]{1,0:T(8,128)(2,1)S(1)} %get-tuple-element.21), channel_id=1, source_target_pairs={{0,2},{2,4},{4,6},{6,0},{1,3},{3,5},{5,7},{7,1},{8,10},{10,12},{12... | collective-permute-start | bytes 589832 | tf_op jit(solution)/shard_map/ppermute | solution.py:390
  32.5 2.8 %copy-start.2 = (f32[8,112,128]{2,1,0:T(8,128)}, f32[8,112,128]{2,1,0:T(8,128)S(1)}, u32[]{:S(2)}) copy-start(f32[8,112,128]{2,1,0:T(8,128)S(1)} %all-to-all-done.cq_ref) | copy-start | bytes 1376260
  32.6 1.3 copy-start.5
  35.4 22.7 %copy-start.14 = (bf16[128,128]{1,0:T(8,128)(2,1)S(1)}, bf16[128,128]{1,0:T(8,128)(2,1)}, u32[]{:S(2)}) copy-start(bf16[128,128]{1,0:T(8,128)(2,1)} %cols_ref.3) | copy-start | bytes 98308
  35.4 37.7 %all-to-all-start.1 = ((s16[256,8,128]{2,1,0:T(8,128)(2,1)}), s16[256,8,128]{2,1,0:T(8,128)(2,1)}, u32[]{:S(2)}, u32[]{:S(2)}) async-start(s16[256,8,128]{2,1,0:T(8,128)(2,1)} %bitcast.9), calls=%async_computation.1 | async-start | bytes 1048576 | tf_op jit(solution)/shard_map/all_to_all | solution.py:29
  53.8 4.2 %collective-permute-start.4 = (bf16[4,128,768]{2,1,0:T(8,128)(2,1)S(1)}, bf16[4,128,768]{2,1,0:T(8,128)(2,1)S(1)}, u32[]{:S(2)}, u32[]{:S(2)}) collective-permute-start(bf16[4,128,768]{2,1,0:T(8,128)(2,1)S(1)} %pad_maximum_fusion.own_ref), channel_id=1, source_target_pairs={{0,1},{1,0},{2,3},{3,2},{4,5},{5,4},{6,7},{7,6},{8,9},{9,8},{10,11... | collective-permute-start | bytes 2359304 | tf_op jit(solution)/shard_map/ppermute | solution.py:33
  58.0 1.4 copy-start.1
  104.1 5.4 %collective-permute-start.5 = (s16[2048,128]{1,0:T(8,128)(2,1)}, s16[2048,128]{1,0:T(8,128)(2,1)}, u32[]{:S(2)}, u32[]{:S(2)}) collective-permute-start(s16[2048,128]{1,0:T(8,128)(2,1)} %bitcast.16.codes_ref), channel_id=1, source_target_pairs={{0,1},{1,0},{2,3},{3,2},{4,5},{5,4},{6,7},{7,6},{8,9},{9,8},{10,11... | collective-permute-start | bytes 1572872 | tf_op jit(solution)/shard_map/ppermute | solution.py:33
  109.5 3.0 %copy-start.7 = (bf16[12,128,256]{2,1,0:T(8,128)(2,1)}, bf16[12,128,256]{2,1,0:T(8,128)(2,1)S(1)}, u32[]{:S(2)}) copy-start(bf16[12,128,256]{2,1,0:T(8,128)(2,1)S(1)} %get-tuple-element.26.mine_ref) | copy-start | bytes 2359300
  112.5 0.9 copy-start.9
  113.4 17.6 %all-to-all-start.3 = ((f32[8,70,128]{2,1,0:T(8,128)}), f32[8,70,128]{2,1,0:T(8,128)}, u32[]{:S(2)}, u32[]{:S(2)}) async-start(f32[8,70,128]{2,1,0:T(8,128)} %get-tuple-element.25), calls=%async_computation.3 | async-start | bytes 589824 | tf_op jit(solution)/shard_map/all_to_all | solution.py:29
  132.9 20.2 %all-to-all-start.4 = ((f32[8,65,128]{2,1,0:T(8,128)}), f32[8,65,128]{2,1,0:T(8,128)S(1)}, u32[]{:S(2)}, u32[]{:S(2)}) async-start(f32[8,65,128]{2,1,0:T(8,128)} %select_maximum_fusion), calls=%async_computation.4 | async-start | bytes 589824 | tf_op jit(solution)/shard_map/all_to_all | solution.py:29
  153.1 1.1 copy-start.8
  154.2 1.1 copy-start.10

commit v4 on v3

--- a/solution.py
+++ b/solution.py
@@ -16,6 +16,7 @@
 EXPERT = ("l", "c")
 FLAT = ("x", "y", "h", "l")
 LIMIT = 12 * 1024 * 1024
+MOST = 60 * 1024 * 1024
 TOP = 32000.0
 STEP = 64.0
 USED = 96
@@ -61,6 +62,37 @@
 def decoded(tile):
     wide = tile.astype(jnp.int32).astype(F32)
     return wide * (jnp.exp2(wide[:, 127:128] * (1.0 / STEP)) * (1.0 / TOP))
+
+
+def eye_of(rows):
+    shape = (rows, 128)
+    return lax.broadcasted_iota(jnp.int32, shape, 0) == lax.broadcasted_iota(jnp.int32, shape, 1)
+
+
+def packed(raw):
+    exponent, factor = scale_of(jnp.max(jnp.abs(raw), axis=1, keepdims=True))
+    row = jnp.sum(jnp.where(eye_of(RANK), exponent, 0.0), axis=0, keepdims=True)
+    return raw * factor, jnp.concatenate([row, jnp.zeros((7, 128), F32)], axis=0)
+
+
+def tagged(rows):
+    used = lanes_of(rows.shape) < USED
+    rows = jnp.where(used, rows, 0.0)
+    exponent, factor = scale_of(jnp.max(jnp.abs(rows), axis=1, keepdims=True))
+    return jnp.where(used, rows * factor, exponent)
+
+
+def collected(ref):
+    raw = jnp.zeros((RANK, 128), F32)
+    rows = jnp.zeros((8, 128), F32)
+    eye = eye_of(RANK)
+    for i in range(8):
+        codes = ref[i, :RANK, :].astype(jnp.int32).astype(F32)
+        rest = ref[i, RANK:, :].astype(jnp.int32).astype(F32)
+        exponent = jnp.sum(jnp.where(eye, rest[8:9, :], 0.0), axis=1, keepdims=True)
+        raw += codes * (jnp.exp2(exponent * (1.0 / STEP)) * (1.0 / TOP))
+        rows += rest[:8] * (jnp.exp2(rest[:8, 127:128] * (1.0 / STEP)) * (1.0 / TOP))
+    return raw, rows
 
 
 def error_kernel(block_ref, q_ref, error_ref, attn_ref, out_ref, pass_ref):
@@ -93,17 +125,28 @@
             jax.ShapeDtypeStruct((RANK, 4 * BLOCK), F32),
             jax.ShapeDtypeStruct((128, BLOCK), BF16),
         ],
-        compiler_params=pltpu.CompilerParams(vmem_limit_bytes=LIMIT),
+        compiler_params=pltpu.CompilerParams(vmem_limit_bytes=MOST),
         cost_estimate=pl.CostEstimate(
             flops=2 * 192 * 128 * 3072, bytes_accessed=3072 * 512, transcendentals=0
         ),
     )(core.reshape(1), power_t, error, attn_out)
 
 
-def share_kernel(place_ref, cq_ref, attn_ref, kept_ref, came_ref, out_ref, half_ref):
-    cq = jnp.sum(cq_ref[:, :RANK, :], axis=0)
-    from_attn = folded(jnp.dot(three(cq), attn_ref[...], preferred_element_type=F32))
-    half_ref[...] = kept_ref[...] + came_ref[...]
+def share_kernel(
+    place_ref, cq_ref, attn_ref, kept_ref, came_ref, out_ref, expert_ref, half_ref, other_ref, sems
+):
+    copies = [
+        pltpu.make_async_copy(kept_ref, half_ref, sems.at[0]),
+        pltpu.make_async_copy(came_ref, other_ref, sems.at[1]),
+    ]
+    for copy in copies:
+        copy.start()
+    total = jnp.sum(cq_ref[...], axis=0)
+    expert_ref[...] = total[RANK:]
+    from_attn = folded(jnp.dot(three(total[:RANK]), attn_ref[...], preferred_element_type=F32))
+    for copy in copies:
+        copy.wait()
+    half_ref[...] += other_ref[...]
     here = pl.ds(pl.multiple_of(place_ref[0] * BLOCK, BLOCK), BLOCK)
     half_ref[:, here] += from_attn
     lane = lanes_of((8, 128))
@@ -130,19 +173,26 @@
 def share_of(place, cq_all, attn_out, kept, came):
     return pl.pallas_call(
         share_kernel,
-        in_specs=[SMEM, VMEM, VMEM, VMEM, VMEM],
-        out_specs=VMEM,
-        out_shape=jax.ShapeDtypeStruct((2048, 128), I16),
-        scratch_shapes=[pltpu.VMEM((RANK, 4 * BLOCK), F32)],
-        compiler_params=pltpu.CompilerParams(vmem_limit_bytes=LIMIT),
+        in_specs=[SMEM, VMEM, VMEM, ANY, ANY],
+        out_specs=[VMEM, VMEM],
+        out_shape=[
+            jax.ShapeDtypeStruct((2048, 128), I16),
+            jax.ShapeDtypeStruct((48, 128), F32),
+        ],
+        scratch_shapes=[
+            pltpu.VMEM((RANK, 4 * BLOCK), F32),
+            pltpu.VMEM((RANK, 4 * BLOCK), F32),
+            pltpu.SemaphoreType.DMA((2,)),
+        ],
+        compiler_params=pltpu.CompilerParams(vmem_limit_bytes=61850000),
         cost_estimate=pl.CostEstimate(
             flops=2 * 192 * 128 * 768, bytes_accessed=6000000, transcendentals=0
         ),
     )(place.reshape(1), cq_all, attn_out, kept, came)
 
 
-def sum_kernel(in_ref, grad_ref, out_ref):
-    del grad_ref
+def sum_kernel(in_ref, grad_ref, expert_ref, out_ref):
+    del grad_ref, expert_ref
 
     def step(i, total):
         at = pl.multiple_of(i * 64, 64)
@@ -159,15 +209,15 @@
     out_ref[...] = jnp.broadcast_to(tile[None], (128, 16, 128)).reshape(2048, 128)
 
 
-def summed(received, grad):
+def summed(received, *others):
     return pl.pallas_call(
         sum_kernel,
-        in_specs=[VMEM, ANY],
+        in_specs=[VMEM, ANY, ANY],
         out_specs=VMEM,
         out_shape=jax.ShapeDtypeStruct((2048, 128), I16),
         compiler_params=pltpu.CompilerParams(vmem_limit_bytes=LIMIT),
         cost_estimate=pl.CostEstimate(flops=1000000, bytes_accessed=1500000, transcendentals=0),
-    )(received, grad)
+    )(received, *others)
 
 
 def grad_kernel(at_ref, own_ref, other_ref, cols_ref, error_ref, out_ref):
@@ -230,16 +280,39 @@
                 p_ref[place // 2, RANK + pair * 16 : RANK + pair * 16 + 16, lanes] = low
 
 
-def rows_of(i, core):
-    return pl.ds(pl.multiple_of((2 * (i // 3) + core) * BLOCK + (i % 3) * 256, 256), 256)
-
-
-def product(p_ref, grad_ref, core):
+def product(p_ref, grad_ref):
     total = jnp.zeros((128, 256), F32)
     for i in range(12):
-        total += jnp.dot(p_ref[i], grad_ref[rows_of(i, core), :], preferred_element_type=F32)
+        rows = slice(i * 256, i * 256 + 256)
+        total += jnp.dot(p_ref[i], grad_ref[rows, :], preferred_element_type=F32)
     total = total[:RANK] + total[RANK:]
     return total[:, :128] + total[:, 128:]
+
+
+def fetch(grad_ref, half_ref, core, sem):
+    copies = []
+    for i in range(4):
+        rows = pl.ds(pl.multiple_of((2 * i + core) * BLOCK, BLOCK), BLOCK)
+        copies.append(
+            pltpu.make_async_copy(
+                grad_ref.at[rows, :], half_ref.at[pl.ds(i * BLOCK, BLOCK), :], sem.at[i]
+            )
+        )
+        copies[-1].start()
+    return copies
+
+
+def half_of(core, codes_ref, grad_ref, p_ref, half_ref, keep_ref, sem):
+    copies = fetch(grad_ref, half_ref, core, sem)
+    unpacked(codes_ref, keep_ref)
+    out = pltpu.make_async_copy(keep_ref, p_ref, sem.at[4])
+    out.start()
+    square = squared(keep_ref)
+    for copy in copies:
+        copy.wait()
+    raw = product(keep_ref, half_ref)
+    out.wait()
+    return raw, square
 
 
 def squared(p_ref):
@@ -252,35 +325,49 @@
     return total[:, :RANK] + total[:, RANK:]
 
 
-def mine_kernel(core_ref, codes_ref, grad_ref, raw_ref, gram_ref, p_ref):
-    unpacked(codes_ref, p_ref)
-    raw_ref[...] = product(p_ref, grad_ref, core_ref[0])
-    gram_ref[...] = squared(p_ref)
+def mine_kernel(
+    core_ref, codes_ref, grad_ref, raw_ref, square_ref, p_ref, half_ref, keep_ref, sem
+):
+    raw_ref[...], square_ref[...] = half_of(
+        core_ref[0], codes_ref, grad_ref, p_ref, half_ref, keep_ref, sem
+    )
 
 
 def other_kernel(
-    core_ref, codes_ref, grad_ref, mine_ref, square_ref, expert_ref, out_ref, gram_ref, p_ref
+    core_ref, codes_ref, grad_ref, mine_ref, square_ref, expert_ref,
+    out_ref, gram_ref, p_ref, half_ref, keep_ref, sem,
 ):
-    unpacked(codes_ref, p_ref)
-    gram_ref[...] = square_ref[...] + squared(p_ref)
-    raw = mine_ref[...] + product(p_ref, grad_ref, 1 - core_ref[0])
+    raw, square = half_of(
+        1 - core_ref[0], codes_ref, grad_ref, p_ref, half_ref, keep_ref, sem
+    )
+    gram_ref[...] = square_ref[...] + square
+    codes, scales = packed(raw + mine_ref[...])
+    codes = coded(codes)
     for i in range(8):
-        out_ref[i, :RANK, :] = raw
-        out_ref[i, RANK:, :] = expert_ref[i]
+        rest = jnp.concatenate([tagged(expert_ref[i]), scales], axis=0)
+        out_ref[i, :RANK, :] = codes
+        out_ref[i, RANK:, :] = coded(rest)
 
 
 SQUARE = jax.ShapeDtypeStruct((RANK, RANK), F32)
+MESSAGE = jax.ShapeDtypeStruct((8, RANK + 16, 128), I16)
 HALF = jax.ShapeDtypeStruct((12, 128, 256), BF16)
+HALF_SCRATCH = [
+    pltpu.VMEM((4 * BLOCK, 256), BF16),
+    pltpu.VMEM((12, 128, 256), BF16),
+    pltpu.SemaphoreType.DMA((5,)),
+]
 HALF_COST = pl.CostEstimate(flops=2 * 128 * 256 * 3072, bytes_accessed=3000000, transcendentals=0)
 
 
 def mine_of(core, codes, grad):
     return pl.pallas_call(
         mine_kernel,
-        in_specs=[SMEM, VMEM, VMEM],
-        out_specs=[VMEM, VMEM, VMEM],
+        in_specs=[SMEM, VMEM, ANY],
+        out_specs=[VMEM, VMEM, ANY],
+        scratch_shapes=HALF_SCRATCH,
         out_shape=[jax.ShapeDtypeStruct((RANK, 128), F32), SQUARE, HALF],
-        compiler_params=pltpu.CompilerParams(vmem_limit_bytes=LIMIT),
+        compiler_params=pltpu.CompilerParams(vmem_limit_bytes=62200000),
         cost_estimate=HALF_COST,
     )(core.reshape(1), codes, grad)
 
@@ -288,55 +375,119 @@
 def other_of(core, codes, grad, raw, square, by_y):
     return pl.pallas_call(
         other_kernel,
-        in_specs=[SMEM, VMEM, VMEM, VMEM, VMEM, VMEM],
-        out_specs=[VMEM, VMEM, VMEM],
-        out_shape=[jax.ShapeDtypeStruct((8, RANK + 6, 128), F32), SQUARE, HALF],
-        compiler_params=pltpu.CompilerParams(vmem_limit_bytes=LIMIT),
+        in_specs=[SMEM, VMEM, ANY, VMEM, VMEM, VMEM],
+        out_specs=[VMEM, VMEM, ANY],
+        scratch_shapes=HALF_SCRATCH,
+        out_shape=[MESSAGE, SQUARE, HALF],
+        compiler_params=pltpu.CompilerParams(vmem_limit_bytes=62200000),
         cost_estimate=HALF_COST,
     )(core.reshape(1), codes, grad, raw, square, by_y)
 
 
+def after_kernel(in_ref, other_ref, out_ref):
+    del in_ref, other_ref, out_ref
+
+
+def after(values, other):
+    return pl.pallas_call(
+        after_kernel,
+        in_specs=[ANY, ANY],
+        out_specs=ANY,
+        out_shape=jax.ShapeDtypeStruct(values.shape, values.dtype),
+        input_output_aliases={0: 0},
+        compiler_params=pltpu.CompilerParams(vmem_limit_bytes=1024 * 1024),
+    )(values, other)
+
+
+def pass_kernel(in_ref, out_ref):
+    raw, rows = collected(in_ref)
+    codes, scales = packed(raw)
+    rows = tagged(rows)
+    for i in range(8):
+        mine = jnp.broadcast_to(rows[i : i + 1], (8, 128))
+        out_ref[i, :RANK, :] = coded(codes)
+        out_ref[i, RANK:, :] = coded(jnp.concatenate([mine, scales], axis=0))
+
+
+def passed(received):
+    return pl.pallas_call(
+        pass_kernel,
+        in_specs=[VMEM],
+        out_specs=VMEM,
+        out_shape=MESSAGE,
+        compiler_params=pltpu.CompilerParams(vmem_limit_bytes=LIMIT),
+    )(received)
+
+
 def final_kernel(
     at_ref, inverse_ref, sums_ref, mine_ref, other_ref, grad_ref,
-    approx_ref, q_ref, error_ref, expert_ref, full_ref,
+    approx_ref, q_ref, error_ref, expert_ref, full_ref, both_ref,
 ):
-    sums = jnp.sum(sums_ref[...], axis=0)
-    expert_ref[...] = sums[RANK : RANK + 1, :USED]
-    inverse = inverse_ref[...]
-    q_t = jnp.dot(inverse, sums[:RANK], precision=HIGH) * (1.0 / 64.0)
-    q_ref[...] = q_t
-    weights = jnp.dot(inverse.T, q_t, precision=HIGH)
-    high = weights.astype(BF16)
-    low = (weights - high.astype(F32)).astype(BF16)
-    both = jnp.concatenate([high, low], axis=1)
-    both = jnp.concatenate([both, both], axis=0)
+    step = pl.program_id(0)
+
+    @pl.when(step == 0)
+    def _():
+        raw, rows = collected(sums_ref)
+        expert_ref[...] = rows[:1, :USED]
+        inverse = inverse_ref[...]
+        q_t = jnp.dot(inverse, raw, precision=HIGH) * (1.0 / 64.0)
+        q_ref[...] = q_t
+        weights = jnp.dot(inverse.T, q_t, precision=HIGH)
+        high = weights.astype(BF16)
+        low = (weights - high.astype(F32)).astype(BF16)
+        both = jnp.concatenate([high, low], axis=1)
+        both_ref[...] = jnp.concatenate([both, both], axis=0)
+
     for ref, core in ((mine_ref, at_ref[1]), (other_ref, 1 - at_ref[1])):
-        for i in range(12):
-            rows = rows_of(i, core)
+        for i in range(3):
+            rows = pl.ds(pl.multiple_of(core * BLOCK + i * 256, 256), 256)
             part = lax.dot_general(
-                ref[i], both, (((0,), (0,)), ((), ())), preferred_element_type=F32
+                ref[i], both_ref[...], (((0,), (0,)), ((), ())), preferred_element_type=F32
             )
             part = part[:, :128] + part[:, 128:]
-            full_ref[rows, :] = part
+            full_ref[step, rows, :] = part
             grad = grad_ref[rows, :].astype(F32)
             error_ref[rows, :] = (grad[:, :128] + grad[:, 128:] - part).astype(BF16)
-    here = pl.ds(pl.multiple_of(at_ref[0] * 96, 32), 96)
-    approx_ref[...] = full_ref[here, :].astype(BF16)
+
+    @pl.when(step == 3)
+    def _():
+        first = at_ref[0] * 96
+        here = pl.ds(pl.multiple_of(lax.rem(first, 2 * BLOCK), 32), 96)
+        approx_ref[...] = full_ref[first // (2 * BLOCK), here, :].astype(BF16)
 
 
 def final_of(data, core, inverse, sums, p_mine, p_other, grad):
+    def whole(*shape):
+        return pl.BlockSpec(shape, lambda i, at: (0,) * len(shape))
+
+    half = pl.BlockSpec((3, 128, 256), lambda i, at: (i, 0, 0))
     return pl.pallas_call(
         final_kernel,
-        in_specs=[SMEM, VMEM, VMEM, VMEM, VMEM, VMEM],
-        out_specs=[VMEM] * 4,
+        grid_spec=pltpu.PrefetchScalarGridSpec(
+            num_scalar_prefetch=1,
+            grid=(4,),
+            in_specs=[
+                whole(RANK, RANK),
+                whole(8, RANK + 16, 128),
+                half,
+                half,
+                pl.BlockSpec((2 * BLOCK, 256), lambda i, at: (i, 0)),
+            ],
+            out_specs=[
+                whole(96, 128),
+                whole(RANK, 128),
+                pl.BlockSpec((2 * BLOCK, 128), lambda i, at: (i, 0)),
+                whole(1, USED),
+            ],
+            scratch_shapes=[pltpu.VMEM((4, 2 * BLOCK, 128), F32), pltpu.VMEM((128, 256), BF16)],
+        ),
         out_shape=[
             jax.ShapeDtypeStruct((96, 128), BF16),
             jax.ShapeDtypeStruct((RANK, 128), F32),
             jax.ShapeDtypeStruct((WIDTH, 128), BF16),
             jax.ShapeDtypeStruct((1, USED), F32),
         ],
-        scratch_shapes=[pltpu.VMEM((WIDTH, 128), F32)],
-        compiler_params=pltpu.CompilerParams(vmem_limit_bytes=LIMIT),
+        compiler_params=pltpu.CompilerParams(vmem_limit_bytes=62200000),
     )(jnp.stack([data, core]), inverse, sums, p_mine, p_other, grad)
 
 
@@ -361,12 +512,23 @@
 
 
 def first_of(power_t, out_cols, tokens, routes_t, logits_t, score_t):
+    def whole(*shape):
+        return pl.BlockSpec(shape, lambda i: (0,) * len(shape))
+
     return pl.pallas_call(
         first_kernel,
-        in_specs=[VMEM] * 6,
-        out_specs=VMEM,
+        grid=(1,),
+        in_specs=[
+            whole(RANK, 128),
+            whole(128, 128),
+            whole(128, WIDTH),
+            whole(2, 128),
+            whole(2, 128),
+            whole(2, 128),
+        ],
+        out_specs=whole(8, RANK + 48, 128),
         out_shape=jax.ShapeDtypeStruct((8, RANK + 48, 128), F32),
-        compiler_params=pltpu.CompilerParams(vmem_limit_bytes=LIMIT),
+        compiler_params=pltpu.CompilerParams(vmem_limit_bytes=MOST),
     )(power_t, out_cols, tokens, routes_t, logits_t, score_t)
 
 
@@ -380,30 +542,25 @@
     cq_all = exchange(
         first_of(power_t, out_cols, tokens, routes.T, route_logits.T, pair_score.T), EXPERT
     )
-    by_y = jnp.sum(cq_all[:, RANK:], axis=0).reshape(4, 8, 2, 96)
-    by_y = by_y.transpose(1, 0, 2, 3).reshape(8, 6, 128)
-
     given, attn_first = error_share(power_t, error, 1 - core, attn_out)
     came = swap_cores(given)
     kept, attn_here = error_share(power_t, error, core, attn_first)
-    shifted = [
-        lax.ppermute(attn_here, "l", [(i, (i + k) % 4) for i in range(4)]) for k in (1, 2, 3)
-    ]
-    codes = share_of(place, cq_all, attn_out, kept, came)
-    own = jnp.stack([attn_here, *shifted])
+    before = lax.ppermute(attn_here, "l", [(i, (i + 1) % 4) for i in range(4)])
+    codes, experts = share_of(place, cq_all, attn_out, kept, came)
+    near = jnp.stack([attn_here, before])
+    far = lax.ppermute(near, "l", [(i, (i + 2) % 4) for i in range(4)])
+    own = jnp.concatenate([near, far])
+    by_y = experts.reshape(4, 8, 2, 96).transpose(1, 0, 2, 3).reshape(8, 8, 96)
+    by_y = jnp.pad(by_y, ((0, 0), (0, 0), (0, 32)))
+    piece = summed(exchange(codes.reshape(256, 8, 128), FLAT).reshape(2048, 128), own, by_y)
     grad = grad_of(place, core, own, swap_cores(own), out_cols, error)
-    piece = summed(exchange(codes.reshape(256, 8, 128), FLAT).reshape(2048, 128), grad)
     mine = exchange(piece.reshape(256, 8, 128), FLAT).reshape(2048, 128)
+    mine = after(mine, grad)
     other = swap_cores(mine)
     raw, square, p_mine = mine_of(core, mine, grad)
     send, gram, p_other = other_of(core, other, grad, raw, square, by_y)
 
-    over_y = jnp.sum(exchange(send, "y"), axis=0)
-    rest = jnp.pad(over_y[RANK:].reshape(8, 1, 96), ((0, 0), (0, 0), (0, 32)))
-    sums = exchange(
-        jnp.concatenate([jnp.broadcast_to(over_y[:RANK], (8, RANK, 128)), rest], axis=1),
-        ("x", "h"),
-    )
+    sums = exchange(passed(exchange(send, "y")), ("x", "h"))
 
     factor = jnp.linalg.cholesky(gram, symmetrize_input=False)
     inverse = lax.linalg.triangular_solve(

time: 160 us -> 177 us (1.11)
  blocking collectives: 28.9 us -> 0 us
  waiting for transfers between devices: 28.9 us -> 51.5 us
  Pallas kernels: 19 us -> 35.7 us
  starting transfers between devices: 53.2 us -> 68.6 us
  local copies, waits for them, and re-layouts: 12.1 us -> 4.14 us
    ppermute x3 -> x2, waiting for transfers between devices: 0.01 us -> 30.2 us  [the longest x1 17 us: local(): far = lax.ppermute(near, 'l', [(i, (i + 2) % 4) for i in range(4)])]
    all_to_all x1 -> x0, blocking collectives: 28.9 us -> none  [exchange(): return lax.all_to_all(values, axes, split_axis=0, concat_axis=0, tiled=True)]
    all_to_all x4 -> x5, starting transfers between devices: 36.1 us -> 56.1 us  [exchange(): return lax.all_to_all(values, axes, split_axis=0, concat_axis=0, tiled=True)]
    pallas_call x6 -> x8, Pallas kernels: 12.9 us -> 25.2 us  [the longest x1 6.26 us: final_of(): pl.pallas_call(final_kernel, grid_spec=pltpu.PrefetchScalarGridSpec(num_s...]
    unnamed x36 -> x22, local copies, waits for them, and re-layouts: 11.8 us -> 4.03 us
    all_to_all x4 -> x5, waiting for transfers between devices: 26.8 us -> 19.2 us  [exchange(): return lax.all_to_all(values, axes, split_axis=0, concat_axis=0, tiled=True)]
    ppermute x3 -> x2, starting transfers between devices: 11 us -> 6.48 us  [the longest x1 3.37 us: local(): before = lax.ppermute(attn_here, 'l', [(i, (i + 1) % 4) for i in range(4)])]
    pallas_call x2, Pallas kernels: 3.21 us -> 7.52 us  [error_share(): pl.pallas_call(error_kernel, grid_spec=pltpu.PrefetchScalarGridSpec(num_s...]
  transfers between devices with their start and end apart: 10 -> 10, of which waited for: 4 -> 7; matrix products, arithmetic and copies ran while one was open for 9% -> 8% of each run, Pallas kernels for 6% -> 9%
where the time goes in v4:
time: 177 us; the launch traced here: 175 us
  starting transfers between devices  68.6 us (39%)
  waiting for transfers between devices  51.5 us (29%)
  Pallas kernels  35.7 us (20%)
  other arithmetic  13.7 us (8%)
  local copies, waits for them, and re-layouts  4.14 us (2%)
    all_to_all x5, starting transfers between devices, exchange(): return lax.all_to_all(values, axes, split_axis=0, concat_axis=0, tiled=True)  56.1 us
    all_to_all x5, waiting for transfers between devices, exchange(): return lax.all_to_all(values, axes, split_axis=0, concat_axis=0, tiled=True)  19.2 us
    ppermute x1, waiting for transfers between devices, local(): far = lax.ppermute(near, 'l', [(i, (i + 2) % 4) for i in range(4)])  17 us
    ppermute x1, waiting for transfers between devices, local(): before = lax.ppermute(attn_here, 'l', [(i, (i + 1) % 4) for i in range(4)])  13.2 us
    pallas_call x2, Pallas kernels, error_share(): pl.pallas_call(error_kernel, grid_spec=pltpu.PrefetchScalarGridSpec(num_s...  7.52 us
    another operation x3, other arithmetic, local(): factor = jnp.linalg.cholesky(gram, symmetrize_input=False)  7.27 us
    pallas_call x1, Pallas kernels, final_of(): pl.pallas_call(final_kernel, grid_spec=pltpu.PrefetchScalarGridSpec(num_s...  6.26 us
    ppermute x3, starting transfers between devices, swap_cores(): return lax.ppermute(values, 'c', [(0, 1), (1, 0)])  6.06 us
  transfers between devices with their start and end apart: 10, of which 7 were waited for; matrix products, arithmetic and copies ran while one was open for 8% of the time, Pallas kernels for 9%

profile of v4, /device:TPU:64, one launch (start us, length us, event | category | flops | bytes accessed | tf_op | source)
XLA Modules:
  0.0 175.4 jit_solution(4227104205030144107)
XLA Ops:
  0.6 2.6 %shard_map.111 = f32[8,112,128]{2,1,0:T(8,128)} custom-call(f32[64,128]{1,0:T(8,128)} %bitcast.34, bf16[128,128]{1,0:T(8,128)(2,1)} %cols_ref.3, bf16[128,6144]{1,0:T(8,128)(2,1)} %tokens_ref.1, s32[2,128]{1,0:T(2,128)} %bitcast.38, f32[2,128]{1,0:T(2,128)} %bitcast.39, f32[2,128]{1,0:T(2,128)} %bitcast.40), custom_call_target="tpu_custom_call" | custom-call | tf_op jit(solution)/shard_map/pallas_call | solution.py:518
  3.2 8.4 %all-to-all-start = ((f32[8,112,128]{2,1,0:T(8,128)}), f32[8,112,128]{2,1,0:T(8,128)S(1)}, u32[]{:S(2)}, u32[]{:S(2)}) async-start(f32[8,112,128]{2,1,0:T(8,128)} %shard_map.111), calls=%async_computation | async-start | bytes 917504 | tf_op jit(solution)/shard_map/all_to_all | solution.py:30
  11.7 3.7 %shard_map.112 = (f32[64,3072]{1,0:T(8,128)}, bf16[128,768]{1,0:T(8,128)(2,1)}) custom-call(s32[1]{0:T(128)} %bitcast.8.block_ref, f32[64,128]{1,0:T(8,128)} %bitcast.35, bf16[6144,128]{1,0:T(8,128)(2,1)} %bitcast.25, bf16[128,768]{1,0:T(8,128)(2,1)} %attn_ref.3), custom_call_target="tpu_custom_call" | custom-call | flops 150994944 | bytes 1572864 | tf_op jit(solution)/shard_map/pallas_call | solution.py:109
  15.4 2.0 %collective-permute-start = (f32[64,3072]{1,0:T(8,128)}, f32[64,3072]{1,0:T(8,128)S(1)}, u32[]{:S(2)}, u32[]{:S(2)}) collective-permute-start(f32[64,3072]{1,0:T(8,128)} %get-tuple-element.22), channel_id=1, source_target_pairs={{0,1},{1,0},{2,3},{3,2},{4,5},{5,4},{6,7},{7,6},{8,9},{9,8},{10,11... | collective-permute-start | bytes 2359304 | tf_op jit(solution)/shard_map/ppermute | solution.py:34
  17.4 3.8 %shard_map.113 = (f32[64,3072]{1,0:T(8,128)}, bf16[128,768]{1,0:T(8,128)(2,1)}) custom-call(s32[1]{0:T(128)} %bitcast.1.block_ref.core_ref, f32[64,128]{1,0:T(8,128)} %bitcast.36, bf16[6144,128]{1,0:T(8,128)(2,1)} %bitcast.26, bf16[128,768]{1,0:T(8,128)(2,1)} %get-tuple-element.20.attn_ref), custom_call_target="tpu_custom_call" | custom-call | flops 150994944 | bytes 1572864 | tf_op jit(solution)/shard_map/pallas_call | solution.py:109
  21.2 0.0 collective-permute-done.came_ref
  21.2 0.0 copy-start.7
  21.3 1.5 all-to-all-done.cq_ref
  22.8 0.8 copy-done.6
  23.5 4.2 %shard_map.114 = (s16[2048,128]{1,0:T(8,128)(2,1)}, f32[48,128]{1,0:T(8,128)}) custom-call(s32[1]{0:T(128)} %bitcast.2.place_ref, f32[8,112,128]{2,1,0:T(8,128)} %copy-done.6, bf16[128,768]{1,0:T(8,128)(2,1)} %attn_ref.3, f32[64,3072]{1,0:T(8,128)} %get-tuple-element.21.kept_ref, f32[64,3072]{1,0:T(8,128)} %copy-done.7), custom_call_target="tpu_custom_call" | custom-call | flops 37748736 | bytes 6000000 | tf_op jit(solution)/shard_map/pallas_call | solution.py:174
  27.8 0.0 copy-start.10
  27.8 19.5 %all-to-all-start.1 = ((s16[256,8,128]{2,1,0:T(8,128)(2,1)}), s16[256,8,128]{2,1,0:T(8,128)(2,1)S(1)}, u32[]{:S(2)}, u32[]{:S(2)}) async-start(s16[256,8,128]{2,1,0:T(8,128)(2,1)} %bitcast.33), calls=%async_computation.1 | async-start | bytes 1048576 | tf_op jit(solution)/shard_map/all_to_all | solution.py:30
  47.3 3.4 %collective-permute-start.1 = (bf16[128,768]{1,0:T(8,128)(2,1)S(1)}, bf16[128,768]{1,0:T(8,128)(2,1)S(1)}, u32[]{:S(2)}, u32[]{:S(2)}) collective-permute-start(bf16[128,768]{1,0:T(8,128)(2,1)S(1)} %copy-done.8), channel_id=1, source_target_pairs={{0,2},{2,4},{4,6},{6,0},{1,3},{3,5},{5,7},{7,1},{8,10},{10,12},{12... | collective-permute-start | bytes 589832 | tf_op jit(solution)/shard_map/ppermute | solution.py:548
  50.7 13.2 %collective-permute-done.1 = bf16[128,768]{1,0:T(8,128)(2,1)S(1)} collective-permute-done((bf16[128,768]{1,0:T(8,128)(2,1)S(1)}, bf16[128,768]{1,0:T(8,128)(2,1)S(1)}, u32[]{:S(2)}, u32[]{:S(2)}) %collective-permute-start.1) | collective-permute-done | bytes 196640 | tf_op jit(solution)/shard_map/ppermute | solution.py:548
  63.9 3.1 %collective-permute-start.2 = (bf16[2,128,768]{2,1,0:T(8,128)(2,1)S(1)}, bf16[2,128,768]{2,1,0:T(8,128)(2,1)S(1)}, u32[]{:S(2)}, u32[]{:S(2)}) collective-permute-start(bf16[2,128,768]{2,1,0:T(8,128)(2,1)S(1)} %pad_maximum_fusion.1), channel_id=1, source_target_pairs={{0,4},{2,6},{4,0},{6,2},{1,5},{3,7},{5,1},{7,3},{8,12},{10,14},{12... | collective-permute-start | bytes 1179656 | tf_op jit(solution)/shard_map/ppermute | solution.py:551
  67.1 17.0 %collective-permute-done.2 = bf16[2,128,768]{2,1,0:T(8,128)(2,1)S(1)} collective-permute-done((bf16[2,128,768]{2,1,0:T(8,128)(2,1)S(1)}, bf16[2,128,768]{2,1,0:T(8,128)(2,1)S(1)}, u32[]{:S(2)}, u32[]{:S(2)}) %collective-permute-start.2) | collective-permute-done | bytes 393248 | tf_op jit(solution)/shard_map/ppermute | solution.py:551
  84.0 0.1 pad_maximum_fusion.grad_ref.own_ref
  84.1 0.0 copy-start.2
  84.1 0.0 copy-start.5
  84.2 0.1 reshape.48
  84.3 0.0 all-to-all-done.1
  84.3 1.9 %shard_map.115 = s16[2048,128]{1,0:T(8,128)(2,1)} custom-call(s16[2048,128]{1,0:T(8,128)(2,1)S(1)} %bitcast.28, bf16[4,128,768]{2,1,0:T(8,128)(2,1)S(1)} %pad_maximum_fusion.grad_ref.own_ref, f32[8,8,128]{2,1,0:T(8,128)S(1)} %pad.4.expert_ref), custom_call_target="tpu_custom_call" | custom-call | flops 1000000 | bytes 1500000 | tf_op jit(solution)/shard_map/pallas_call | solution.py:213
  86.2 19.2 %all-to-all-start.2 = ((s16[256,8,128]{2,1,0:T(8,128)(2,1)}), s16[256,8,128]{2,1,0:T(8,128)(2,1)}, u32[]{:S(2)}, u32[]{:S(2)}) async-start(s16[256,8,128]{2,1,0:T(8,128)(2,1)} %bitcast.15), calls=%async_computation.2 | async-start | bytes 1048576 | tf_op jit(solution)/shard_map/all_to_all | solution.py:30
  105.5 1.9 %collective-permute-start.3 = (bf16[4,128,768]{2,1,0:T(8,128)(2,1)S(1)}, bf16[4,128,768]{2,1,0:T(8,128)(2,1)S(1)}, u32[]{:S(2)}, u32[]{:S(2)}) collective-permute-start(bf16[4,128,768]{2,1,0:T(8,128)(2,1)S(1)} %pad_maximum_fusion.grad_ref.own_ref), channel_id=1, source_target_pairs={{0,1},{1,0},{2,3},{3,2},{4,5},{5,4},{6,7},{7,6},{8,9},{9,8},{10,11... | collective-permute-start | bytes 2359304 | tf_op jit(solution)/shard_map/ppermute | solution.py:34
  107.4 0.1 pad_add_fusion.1.at_ref
  107.5 2.2 %collective-permute-done.3.other_ref = bf16[4,128,768]{2,1,0:T(8,128)(2,1)S(1)} collective-permute-done((bf16[4,128,768]{2,1,0:T(8,128)(2,1)S(1)}, bf16[4,128,768]{2,1,0:T(8,128)(2,1)S(1)}, u32[]{:S(2)}, u32[]{:S(2)}) %collective-permute-start.3) | collective-permute-done | bytes 786464 | tf_op jit(solution)/shard_map/ppermute | solution.py:34
  109.6 1.4 copy-done.1
  111.1 1.1 copy-done.3
  112.2 2.9 %shard_map.116.other_ref.grad_ref = bf16[6144,256]{1,0:T(8,128)(2,1)S(1)} custom-call(s32[2]{0:T(128)S(1)} %pad_add_fusion.1.at_ref, bf16[4,128,768]{2,1,0:T(8,128)(2,1)S(1)} %copy-done.3, bf16[4,128,768]{2,1,0:T(8,128)(2,1)S(1)} %collective-permute-done.3.other_ref, bf16[128,128]{1,0:T(8,128)(2,1)S(1)} %copy-done.5, bf16[6144,128]{1,0:T(8,128)(2,1)S(1)} %bitcast.27), custom_call_target="tpu_custom_call" | custom-call | flops 201326592 | bytes 6291456 | tf_op jit(solution)/shard_map/pallas_call | solution.py:239
  115.1 0.0 copy-done.4
  115.1 9.3 %all-to-all-done.2 = s16[256,8,128]{2,1,0:T(8,128)(2,1)} async-done(((s16[256,8,128]{2,1,0:T(8,128)(2,1)}), s16[256,8,128]{2,1,0:T(8,128)(2,1)}, u32[]{:S(2)}, u32[]{:S(2)}) %all-to-all-start.2) | async-done | bytes 524320 | tf_op jit(solution)/shard_map/all_to_all | solution.py:30
  124.4 2.1 %collective-permute-start.4 = (s16[2048,128]{1,0:T(8,128)(2,1)}, s16[2048,128]{1,0:T(8,128)(2,1)}, u32[]{:S(2)}, u32[]{:S(2)}) collective-permute-start(s16[2048,128]{1,0:T(8,128)(2,1)} %shard_map.117.codes_ref), channel_id=1, source_target_pairs={{0,1},{1,0},{2,3},{3,2},{4,5},{5,4},{6,7},{7,6},{8,9},{9,8},{10,11... | collective-permute-start | bytes 1572872 | tf_op jit(solution)/shard_map/ppermute | solution.py:34
  126.6 4.5 %shard_map.118 = (f32[64,128]{1,0:T(8,128)}, f32[64,64]{1,0:T(8,128)}, bf16[12,128,256]{2,1,0:T(8,128)(2,1)}) custom-call(s32[1]{0:T(128)} %bitcast.1.block_ref.core_ref, s16[2048,128]{1,0:T(8,128)(2,1)} %shard_map.117.codes_ref, bf16[6144,256]{1,0:T(8,128)(2,1)} %copy-done), custom_call_target="tpu_custom_call" | custom-call | flops 201326592 | bytes 3000000 | tf_op jit(solution)/shard_map/pallas_call | solution.py:364
  131.1 0.0 collective-permute-done.4.codes_ref
  131.1 4.7 %shard_map.119 = (s16[8,80,128]{2,1,0:T(8,128)(2,1)}, f32[64,64]{1,0:T(8,128)}, bf16[12,128,256]{2,1,0:T(8,128)(2,1)}) custom-call(s32[1]{0:T(128)} %bitcast.1.block_ref.core_ref, s16[2048,128]{1,0:T(8,128)(2,1)} %collective-permute-done.4.codes_ref, bf16[6144,256]{1,0:T(8,128)(2,1)} %copy-done, f32[64,128]{1,0:T(8,128)} %get-tuple-element.26.mine_ref, ...), custom_call_target="tpu_custom_call" | custom-call | flops 201326592 | bytes 3000000 | tf_op jit(solution)/shard_map/pallas_call | solution.py:376
  135.8 3.7 %all-to-all-start.3 = ((s16[8,80,128]{2,1,0:T(8,128)(2,1)}), s16[8,80,128]{2,1,0:T(8,128)(2,1)S(1)}, u32[]{:S(2)}, u32[]{:S(2)}) async-start(s16[8,80,128]{2,1,0:T(8,128)(2,1)} %get-tuple-element.29), calls=%async_computation.3 | async-start | bytes 327680 | tf_op jit(solution)/shard_map/all_to_all | solution.py:30
  139.6 0.7 pad_add_fusion.at_ref
  140.2 6.6 %cholesky.17 = f32[64,64]{1,0:T(8,128)S(1)} custom-call(f32[64,64]{1,0:T(8,128)} %get-tuple-element.28), custom_call_target="Cholesky" | custom-call | tf_op jit(solution)/shard_map/jit(cholesky)/cholesky | solution.py:565
  146.9 0.6 compare_reduce_fusion
  147.5 2.5 %all-to-all-done.3.in_ref = s16[8,80,128]{2,1,0:T(8,128)(2,1)S(1)} async-done(((s16[8,80,128]{2,1,0:T(8,128)(2,1)}), s16[8,80,128]{2,1,0:T(8,128)(2,1)S(1)}, u32[]{:S(2)}, u32[]{:S(2)}) %all-to-all-start.3) | async-done | bytes 163872 | tf_op jit(solution)/shard_map/all_to_all | solution.py:30
  150.0 1.0 shard_map.120
  151.0 5.1 %all-to-all-start.4 = ((s16[8,80,128]{2,1,0:T(8,128)(2,1)}), s16[8,80,128]{2,1,0:T(8,128)(2,1)S(1)}, u32[]{:S(2)}, u32[]{:S(2)}) async-start(s16[8,80,128]{2,1,0:T(8,128)(2,1)} %shard_map.120), calls=%async_computation.4 | async-start | bytes 327680 | tf_op jit(solution)/shard_map/all_to_all | solution.py:30
  156.1 0.7 fusion
  156.8 4.9 %custom-call.6 = f32[1,64,64]{1,2,0:T(8,128)S(1)} custom-call(f32[1,64,64]{2,1,0:T(8,128)S(1)} %fusion), custom_call_target="InvertDiagBlocksLowerTriangular" | custom-call | tf_op jit(solution)/shard_map/triangular_solve | solution.py:566
  161.7 0.8 fusion.1.inverse_ref
  162.5 5.9 %all-to-all-done.4.sums_ref = s16[8,80,128]{2,1,0:T(8,128)(2,1)S(1)} async-done(((s16[8,80,128]{2,1,0:T(8,128)(2,1)}), s16[8,80,128]{2,1,0:T(8,128)(2,1)S(1)}, u32[]{:S(2)}, u32[]{:S(2)}) %all-to-all-start.4) | async-done | bytes 163872 | tf_op jit(solution)/shard_map/all_to_all | solution.py:30
  168.4 0.7 copy-done.9
  169.1 6.3 %shard_map.121 = (bf16[96,128]{1,0:T(8,128)(2,1)}, f32[64,128]{1,0:T(8,128)}, bf16[6144,128]{1,0:T(8,128)(2,1)}, f32[1,96]{1,0:T(1,128)}) custom-call(s32[2]{0:T(128)} %pad_add_fusion.at_ref, f32[64,64]{1,0:T(8,128)} %fusion.1.inverse_ref, s16[8,80,128]{2,1,0:T(8,128)(2,1)} %copy-done.9, bf16[12,128,256]{2,1,0:T(8,128)(2,1)} %get-tuple-element.30.mine_ref, ...), custom_call_target="tpu_custom_call" | custom-call | tf_op jit(solution)/shard_map/pallas_call | solution.py:464
  (18 shorter events, 0.1 us)
Async XLA Ops:
  3.2 19.5 %all-to-all-start = ((f32[8,112,128]{2,1,0:T(8,128)}), f32[8,112,128]{2,1,0:T(8,128)S(1)}, u32[]{:S(2)}, u32[]{:S(2)}) async-start(f32[8,112,128]{2,1,0:T(8,128)} %shard_map.111), calls=%async_computation | async-start | bytes 917504 | tf_op jit(solution)/shard_map/all_to_all | solution.py:30
  15.4 5.9 %collective-permute-start = (f32[64,3072]{1,0:T(8,128)}, f32[64,3072]{1,0:T(8,128)S(1)}, u32[]{:S(2)}, u32[]{:S(2)}) collective-permute-start(f32[64,3072]{1,0:T(8,128)} %get-tuple-element.22), channel_id=1, source_target_pairs={{0,1},{1,0},{2,3},{3,2},{4,5},{5,4},{6,7},{7,6},{8,9},{9,8},{10,11... | collective-permute-start | bytes 2359304 | tf_op jit(solution)/shard_map/ppermute | solution.py:34
  21.2 1.5 copy-start.7
  22.8 0.8 copy-start.6
  23.5 23.8 %copy-start.8 = (bf16[128,768]{1,0:T(8,128)(2,1)S(1)}, bf16[128,768]{1,0:T(8,128)(2,1)}, u32[]{:S(2)}) copy-start(bf16[128,768]{1,0:T(8,128)(2,1)} %get-tuple-element.24) | copy-start | bytes 589828
  27.8 56.4 %copy-start.10 = (f32[48,128]{1,0:T(8,128)S(1)}, f32[48,128]{1,0:T(8,128)}, u32[]{:S(2)}) copy-start(f32[48,128]{1,0:T(8,128)} %get-tuple-element.25) | copy-start | bytes 73732
  27.8 56.5 %all-to-all-start.1 = ((s16[256,8,128]{2,1,0:T(8,128)(2,1)}), s16[256,8,128]{2,1,0:T(8,128)(2,1)S(1)}, u32[]{:S(2)}, u32[]{:S(2)}) async-start(s16[256,8,128]{2,1,0:T(8,128)(2,1)} %bitcast.33), calls=%async_computation.1 | async-start | bytes 1048576 | tf_op jit(solution)/shard_map/all_to_all | solution.py:30
  47.3 16.6 %collective-permute-start.1 = (bf16[128,768]{1,0:T(8,128)(2,1)S(1)}, bf16[128,768]{1,0:T(8,128)(2,1)S(1)}, u32[]{:S(2)}, u32[]{:S(2)}) collective-permute-start(bf16[128,768]{1,0:T(8,128)(2,1)S(1)} %copy-done.8), channel_id=1, source_target_pairs={{0,2},{2,4},{4,6},{6,0},{1,3},{3,5},{5,7},{7,1},{8,10},{10,12},{12... | collective-permute-start | bytes 589832 | tf_op jit(solution)/shard_map/ppermute | solution.py:548
  63.9 20.1 %collective-permute-start.2 = (bf16[2,128,768]{2,1,0:T(8,128)(2,1)S(1)}, bf16[2,128,768]{2,1,0:T(8,128)(2,1)S(1)}, u32[]{:S(2)}, u32[]{:S(2)}) collective-permute-start(bf16[2,128,768]{2,1,0:T(8,128)(2,1)S(1)} %pad_maximum_fusion.1), channel_id=1, source_target_pairs={{0,4},{2,6},{4,0},{6,2},{1,5},{3,7},{5,1},{7,3},{8,12},{10,14},{12... | collective-permute-start | bytes 1179656 | tf_op jit(solution)/shard_map/ppermute | solution.py:551
  84.1 23.3 %copy-start.2 = (bf16[4,128,768]{2,1,0:T(8,128)(2,1)}, bf16[4,128,768]{2,1,0:T(8,128)(2,1)S(1)}, u32[]{:S(2)}) copy-start(bf16[4,128,768]{2,1,0:T(8,128)(2,1)S(1)} %pad_maximum_fusion.grad_ref.own_ref) | copy-start | bytes 2359300
  84.1 25.5 %copy-start.5 = (bf16[128,128]{1,0:T(8,128)(2,1)S(1)}, bf16[128,128]{1,0:T(8,128)(2,1)}, u32[]{:S(2)}) copy-start(bf16[128,128]{1,0:T(8,128)(2,1)} %cols_ref.3) | copy-start | bytes 98308
  84.3 30.8 %copy-start.4 = (f32[8,8,128]{2,1,0:T(8,128)}, f32[8,8,128]{2,1,0:T(8,128)S(1)}, u32[]{:S(2)}) copy-start(f32[8,8,128]{2,1,0:T(8,128)S(1)} %pad.4.expert_ref) | copy-start | bytes 98308
  86.2 38.2 %all-to-all-start.2 = ((s16[256,8,128]{2,1,0:T(8,128)(2,1)}), s16[256,8,128]{2,1,0:T(8,128)(2,1)}, u32[]{:S(2)}, u32[]{:S(2)}) async-start(s16[256,8,128]{2,1,0:T(8,128)(2,1)} %bitcast.15), calls=%async_computation.2 | async-start | bytes 1048576 | tf_op jit(solution)/shard_map/all_to_all | solution.py:30
  105.5 4.2 %collective-permute-start.3 = (bf16[4,128,768]{2,1,0:T(8,128)(2,1)S(1)}, bf16[4,128,768]{2,1,0:T(8,128)(2,1)S(1)}, u32[]{:S(2)}, u32[]{:S(2)}) collective-permute-start(bf16[4,128,768]{2,1,0:T(8,128)(2,1)S(1)} %pad_maximum_fusion.grad_ref.own_ref), channel_id=1, source_target_pairs={{0,1},{1,0},{2,3},{3,2},{4,5},{5,4},{6,7},{7,6},{8,9},{9,8},{10,11... | collective-permute-start | bytes 2359304 | tf_op jit(solution)/shard_map/ppermute | solution.py:34
  109.6 1.4 copy-start.1
  111.0 1.1 copy-start.3
  115.1 9.3 %copy-start = (bf16[6144,256]{1,0:T(8,128)(2,1)}, bf16[6144,256]{1,0:T(8,128)(2,1)S(1)}, u32[]{:S(2)}) copy-start(bf16[6144,256]{1,0:T(8,128)(2,1)S(1)} %shard_map.116.other_ref.grad_ref) | copy-start | bytes 9437188
  124.4 6.6 %collective-permute-start.4 = (s16[2048,128]{1,0:T(8,128)(2,1)}, s16[2048,128]{1,0:T(8,128)(2,1)}, u32[]{:S(2)}, u32[]{:S(2)}) collective-permute-start(s16[2048,128]{1,0:T(8,128)(2,1)} %shard_map.117.codes_ref), channel_id=1, source_target_pairs={{0,1},{1,0},{2,3},{3,2},{4,5},{5,4},{6,7},{7,6},{8,9},{9,8},{10,11... | collective-permute-start | bytes 1572872 | tf_op jit(solution)/shard_map/ppermute | solution.py:34
  135.8 14.2 %all-to-all-start.3 = ((s16[8,80,128]{2,1,0:T(8,128)(2,1)}), s16[8,80,128]{2,1,0:T(8,128)(2,1)S(1)}, u32[]{:S(2)}, u32[]{:S(2)}) async-start(s16[8,80,128]{2,1,0:T(8,128)(2,1)} %get-tuple-element.29), calls=%async_computation.3 | async-start | bytes 327680 | tf_op jit(solution)/shard_map/all_to_all | solution.py:30
  151.0 17.4 %all-to-all-start.4 = ((s16[8,80,128]{2,1,0:T(8,128)(2,1)}), s16[8,80,128]{2,1,0:T(8,128)(2,1)S(1)}, u32[]{:S(2)}, u32[]{:S(2)}) async-start(s16[8,80,128]{2,1,0:T(8,128)(2,1)} %shard_map.120), calls=%async_computation.4 | async-start | bytes 327680 | tf_op jit(solution)/shard_map/all_to_all | solution.py:30
  168.4 0.7 copy-start.9

commit v5 on v3

--- a/solution.py
+++ b/solution.py
@@ -16,6 +16,7 @@
 EXPERT = ("l", "c")
 FLAT = ("x", "y", "h", "l")
 LIMIT = 12 * 1024 * 1024
+MOST = 60 * 1024 * 1024
 TOP = 32000.0
 STEP = 64.0
 USED = 96
@@ -61,6 +62,37 @@
 def decoded(tile):
     wide = tile.astype(jnp.int32).astype(F32)
     return wide * (jnp.exp2(wide[:, 127:128] * (1.0 / STEP)) * (1.0 / TOP))
+
+
+def eye_of(rows):
+    shape = (rows, 128)
+    return lax.broadcasted_iota(jnp.int32, shape, 0) == lax.broadcasted_iota(jnp.int32, shape, 1)
+
+
+def packed(raw):
+    exponent, factor = scale_of(jnp.max(jnp.abs(raw), axis=1, keepdims=True))
+    row = jnp.sum(jnp.where(eye_of(RANK), exponent, 0.0), axis=0, keepdims=True)
+    return raw * factor, jnp.concatenate([row, jnp.zeros((7, 128), F32)], axis=0)
+
+
+def tagged(rows):
+    used = lanes_of(rows.shape) < USED
+    rows = jnp.where(used, rows, 0.0)
+    exponent, factor = scale_of(jnp.max(jnp.abs(rows), axis=1, keepdims=True))
+    return jnp.where(used, rows * factor, exponent)
+
+
+def collected(ref):
+    raw = jnp.zeros((RANK, 128), F32)
+    rows = jnp.zeros((8, 128), F32)
+    eye = eye_of(RANK)
+    for i in range(8):
+        codes = ref[i, :RANK, :].astype(jnp.int32).astype(F32)
+        rest = ref[i, RANK:, :].astype(jnp.int32).astype(F32)
+        exponent = jnp.sum(jnp.where(eye, rest[8:9, :], 0.0), axis=1, keepdims=True)
+        raw += codes * (jnp.exp2(exponent * (1.0 / STEP)) * (1.0 / TOP))
+        rows += rest[:8] * (jnp.exp2(rest[:8, 127:128] * (1.0 / STEP)) * (1.0 / TOP))
+    return raw, rows
 
 
 def error_kernel(block_ref, q_ref, error_ref, attn_ref, out_ref, pass_ref):
@@ -100,9 +132,10 @@
     )(core.reshape(1), power_t, error, attn_out)
 
 
-def share_kernel(place_ref, cq_ref, attn_ref, kept_ref, came_ref, out_ref, half_ref):
-    cq = jnp.sum(cq_ref[:, :RANK, :], axis=0)
-    from_attn = folded(jnp.dot(three(cq), attn_ref[...], preferred_element_type=F32))
+def share_kernel(place_ref, cq_ref, attn_ref, kept_ref, came_ref, out_ref, expert_ref, half_ref):
+    total = jnp.sum(cq_ref[...], axis=0)
+    expert_ref[...] = total[RANK:]
+    from_attn = folded(jnp.dot(three(total[:RANK]), attn_ref[...], preferred_element_type=F32))
     half_ref[...] = kept_ref[...] + came_ref[...]
     here = pl.ds(pl.multiple_of(place_ref[0] * BLOCK, BLOCK), BLOCK)
     half_ref[:, here] += from_attn
@@ -131,8 +164,11 @@
     return pl.pallas_call(
         share_kernel,
         in_specs=[SMEM, VMEM, VMEM, VMEM, VMEM],
-        out_specs=VMEM,
-        out_shape=jax.ShapeDtypeStruct((2048, 128), I16),
+        out_specs=[VMEM, VMEM],
+        out_shape=[
+            jax.ShapeDtypeStruct((2048, 128), I16),
+            jax.ShapeDtypeStruct((48, 128), F32),
+        ],
         scratch_shapes=[pltpu.VMEM((RANK, 4 * BLOCK), F32)],
         compiler_params=pltpu.CompilerParams(vmem_limit_bytes=LIMIT),
         cost_estimate=pl.CostEstimate(
@@ -141,8 +177,8 @@
     )(place.reshape(1), cq_all, attn_out, kept, came)
 
 
-def sum_kernel(in_ref, grad_ref, out_ref):
-    del grad_ref
+def sum_kernel(in_ref, grad_ref, expert_ref, out_ref):
+    del grad_ref, expert_ref
 
     def step(i, total):
         at = pl.multiple_of(i * 64, 64)
@@ -159,15 +195,15 @@
     out_ref[...] = jnp.broadcast_to(tile[None], (128, 16, 128)).reshape(2048, 128)
 
 
-def summed(received, grad):
+def summed(received, *others):
     return pl.pallas_call(
         sum_kernel,
-        in_specs=[VMEM, ANY],
+        in_specs=[VMEM, ANY, ANY],
         out_specs=VMEM,
         out_shape=jax.ShapeDtypeStruct((2048, 128), I16),
         compiler_params=pltpu.CompilerParams(vmem_limit_bytes=LIMIT),
         cost_estimate=pl.CostEstimate(flops=1000000, bytes_accessed=1500000, transcendentals=0),
-    )(received, grad)
+    )(received, *others)
 
 
 def grad_kernel(at_ref, own_ref, other_ref, cols_ref, error_ref, out_ref):
@@ -252,10 +288,10 @@
     return total[:, :RANK] + total[:, RANK:]
 
 
-def mine_kernel(core_ref, codes_ref, grad_ref, raw_ref, gram_ref, p_ref):
+def mine_kernel(core_ref, codes_ref, grad_ref, raw_ref, square_ref, p_ref):
     unpacked(codes_ref, p_ref)
     raw_ref[...] = product(p_ref, grad_ref, core_ref[0])
-    gram_ref[...] = squared(p_ref)
+    square_ref[...] = squared(p_ref)
 
 
 def other_kernel(
@@ -263,13 +299,16 @@
 ):
     unpacked(codes_ref, p_ref)
     gram_ref[...] = square_ref[...] + squared(p_ref)
-    raw = mine_ref[...] + product(p_ref, grad_ref, 1 - core_ref[0])
+    codes, scales = packed(mine_ref[...] + product(p_ref, grad_ref, 1 - core_ref[0]))
+    codes = coded(codes)
     for i in range(8):
-        out_ref[i, :RANK, :] = raw
-        out_ref[i, RANK:, :] = expert_ref[i]
+        rest = jnp.concatenate([tagged(expert_ref[i]), scales], axis=0)
+        out_ref[i, :RANK, :] = codes
+        out_ref[i, RANK:, :] = coded(rest)
 
 
 SQUARE = jax.ShapeDtypeStruct((RANK, RANK), F32)
+MESSAGE = jax.ShapeDtypeStruct((8, RANK + 16, 128), I16)
 HALF = jax.ShapeDtypeStruct((12, 128, 256), BF16)
 HALF_COST = pl.CostEstimate(flops=2 * 128 * 256 * 3072, bytes_accessed=3000000, transcendentals=0)
 
@@ -290,20 +329,40 @@
         other_kernel,
         in_specs=[SMEM, VMEM, VMEM, VMEM, VMEM, VMEM],
         out_specs=[VMEM, VMEM, VMEM],
-        out_shape=[jax.ShapeDtypeStruct((8, RANK + 6, 128), F32), SQUARE, HALF],
+        out_shape=[MESSAGE, SQUARE, HALF],
         compiler_params=pltpu.CompilerParams(vmem_limit_bytes=LIMIT),
         cost_estimate=HALF_COST,
     )(core.reshape(1), codes, grad, raw, square, by_y)
+
+
+def pass_kernel(in_ref, out_ref):
+    raw, rows = collected(in_ref)
+    codes, scales = packed(raw)
+    rows = tagged(rows)
+    for i in range(8):
+        mine = jnp.broadcast_to(rows[i : i + 1], (8, 128))
+        out_ref[i, :RANK, :] = coded(codes)
+        out_ref[i, RANK:, :] = coded(jnp.concatenate([mine, scales], axis=0))
+
+
+def passed(received):
+    return pl.pallas_call(
+        pass_kernel,
+        in_specs=[VMEM],
+        out_specs=VMEM,
+        out_shape=MESSAGE,
+        compiler_params=pltpu.CompilerParams(vmem_limit_bytes=LIMIT),
+    )(received)
 
 
 def final_kernel(
     at_ref, inverse_ref, sums_ref, mine_ref, other_ref, grad_ref,
     approx_ref, q_ref, error_ref, expert_ref, full_ref,
 ):
-    sums = jnp.sum(sums_ref[...], axis=0)
-    expert_ref[...] = sums[RANK : RANK + 1, :USED]
+    raw, rows = collected(sums_ref)
+    expert_ref[...] = rows[:1, :USED]
     inverse = inverse_ref[...]
-    q_t = jnp.dot(inverse, sums[:RANK], precision=HIGH) * (1.0 / 64.0)
+    q_t = jnp.dot(inverse, raw, precision=HIGH) * (1.0 / 64.0)
     q_ref[...] = q_t
     weights = jnp.dot(inverse.T, q_t, precision=HIGH)
     high = weights.astype(BF16)
@@ -361,12 +420,23 @@
 
 
 def first_of(power_t, out_cols, tokens, routes_t, logits_t, score_t):
+    def whole(*shape):
+        return pl.BlockSpec(shape, lambda i: (0,) * len(shape))
+
     return pl.pallas_call(
         first_kernel,
-        in_specs=[VMEM] * 6,
-        out_specs=VMEM,
+        grid=(1,),
+        in_specs=[
+            whole(RANK, 128),
+            whole(128, 128),
+            whole(128, WIDTH),
+            whole(2, 128),
+            whole(2, 128),
+            whole(2, 128),
+        ],
+        out_specs=whole(8, RANK + 48, 128),
         out_shape=jax.ShapeDtypeStruct((8, RANK + 48, 128), F32),
-        compiler_params=pltpu.CompilerParams(vmem_limit_bytes=LIMIT),
+        compiler_params=pltpu.CompilerParams(vmem_limit_bytes=MOST),
     )(power_t, out_cols, tokens, routes_t, logits_t, score_t)
 
 
@@ -380,30 +450,24 @@
     cq_all = exchange(
         first_of(power_t, out_cols, tokens, routes.T, route_logits.T, pair_score.T), EXPERT
     )
-    by_y = jnp.sum(cq_all[:, RANK:], axis=0).reshape(4, 8, 2, 96)
-    by_y = by_y.transpose(1, 0, 2, 3).reshape(8, 6, 128)
-
     given, attn_first = error_share(power_t, error, 1 - core, attn_out)
     came = swap_cores(given)
     kept, attn_here = error_share(power_t, error, core, attn_first)
     shifted = [
         lax.ppermute(attn_here, "l", [(i, (i + k) % 4) for i in range(4)]) for k in (1, 2, 3)
     ]
-    codes = share_of(place, cq_all, attn_out, kept, came)
     own = jnp.stack([attn_here, *shifted])
+    codes, experts = share_of(place, cq_all, attn_out, kept, came)
+    by_y = experts.reshape(4, 8, 2, 96).transpose(1, 0, 2, 3).reshape(8, 8, 96)
+    by_y = jnp.pad(by_y, ((0, 0), (0, 0), (0, 32)))
     grad = grad_of(place, core, own, swap_cores(own), out_cols, error)
-    piece = summed(exchange(codes.reshape(256, 8, 128), FLAT).reshape(2048, 128), grad)
+    piece = summed(exchange(codes.reshape(256, 8, 128), FLAT).reshape(2048, 128), grad, by_y)
     mine = exchange(piece.reshape(256, 8, 128), FLAT).reshape(2048, 128)
     other = swap_cores(mine)
     raw, square, p_mine = mine_of(core, mine, grad)
     send, gram, p_other = other_of(core, other, grad, raw, square, by_y)
 
-    over_y = jnp.sum(exchange(send, "y"), axis=0)
-    rest = jnp.pad(over_y[RANK:].reshape(8, 1, 96), ((0, 0), (0, 0), (0, 32)))
-    sums = exchange(
-        jnp.concatenate([jnp.broadcast_to(over_y[:RANK], (8, RANK, 128)), rest], axis=1),
-        ("x", "h"),
-    )
+    sums = exchange(passed(exchange(send, "y")), ("x", "h"))
 
     factor = jnp.linalg.cholesky(gram, symmetrize_input=False)
     inverse = lax.linalg.triangular_solve(

time: 160 us -> 151 us (0.944)
  waiting for transfers between devices: 28.9 us -> 18.2 us
  blocking collectives: 28.9 us -> 32.5 us
  Pallas kernels: 19 us -> 21.8 us
  other arithmetic: 15 us -> 13.2 us
    all_to_all x4, waiting for transfers between devices: 26.8 us -> 17 us  [exchange(): return lax.all_to_all(values, axes, split_axis=0, concat_axis=0, tiled=True)]
    all_to_all x1, blocking collectives: 28.9 us -> 32.5 us  [exchange(): return lax.all_to_all(values, axes, split_axis=0, concat_axis=0, tiled=True)]
    pallas_call x2 -> x3, Pallas kernels: 3.28 us -> 5.82 us  [the longest x1 2.73 us: first_of(): pl.pallas_call(first_kernel, grid=(1,), in_specs=[whole(RANK, 128), whole...]
    reduce_sum x2 -> x0, other arithmetic: 1.94 us -> none  [the longest x1 0.98 us: local(): over_y = jnp.sum(exchange(send, 'y'), axis=0)]
    unnamed x36 -> x30, local copies, waits for them, and re-layouts: 11.8 us -> 10.6 us
where the time goes in v5:
time: 151 us; the launch traced here: 150 us
  starting transfers between devices  52.7 us (35%)
  blocking collectives  32.5 us (22%)
  Pallas kernels  21.8 us (14%)
  waiting for transfers between devices  18.2 us (12%)
  other arithmetic  13.2 us (9%)
  local copies, waits for them, and re-layouts  10.7 us (7%)
    all_to_all x4, starting transfers between devices, exchange(): return lax.all_to_all(values, axes, split_axis=0, concat_axis=0, tiled=True)  35.6 us
    all_to_all x1, blocking collectives, exchange(): return lax.all_to_all(values, axes, split_axis=0, concat_axis=0, tiled=True)  32.5 us
    all_to_all x4, waiting for transfers between devices, exchange(): return lax.all_to_all(values, axes, split_axis=0, concat_axis=0, tiled=True)  17 us
    ppermute x3, starting transfers between devices, local(): lax.ppermute(attn_here, 'l', [(i, (i + k) % 4) for i in range(4)])  11 us
    unnamed x30, local copies, waits for them, and re-layouts  10.6 us
    another operation x3, other arithmetic, local(): factor = jnp.linalg.cholesky(gram, symmetrize_input=False)  6.52 us
    ppermute x3, starting transfers between devices, swap_cores(): return lax.ppermute(values, 'c', [(0, 1), (1, 0)])  6.06 us
    another operation x2, other arithmetic, local(): lax.linalg.triangular_solve(factor, jnp.eye(RANK, dtype=F32), left_side=T...  5.55 us
  transfers between devices with their start and end apart: 10, of which 4 were waited for; matrix products, arithmetic and copies ran while one was open for 9% of the time, Pallas kernels for 6%

profile of v5, /device:TPU:64, one launch (start us, length us, event | category | flops | bytes accessed | tf_op | source)
XLA Modules:
  0.0 150.3 jit_solution(7077800059457125993)
XLA Ops:
  0.7 0.0 copy-start
  0.7 2.7 %shard_map.111 = f32[8,112,128]{2,1,0:T(8,128)} custom-call(f32[64,128]{1,0:T(8,128)} %bitcast.31, bf16[128,128]{1,0:T(8,128)(2,1)} %cols_ref.3, bf16[128,6144]{1,0:T(8,128)(2,1)} %tokens_ref.1, s32[2,128]{1,0:T(2,128)} %bitcast.38, f32[2,128]{1,0:T(2,128)} %bitcast.39, f32[2,128]{1,0:T(2,128)} %bitcast.40), custom_call_target="tpu_custom_call" | custom-call | tf_op jit(solution)/shard_map/pallas_call | solution.py:426
  3.4 8.4 %all-to-all-start = ((f32[8,112,128]{2,1,0:T(8,128)}), f32[8,112,128]{2,1,0:T(8,128)S(1)}, u32[]{:S(2)}, u32[]{:S(2)}) async-start(f32[8,112,128]{2,1,0:T(8,128)} %shard_map.111), calls=%async_computation | async-start | bytes 917504 | tf_op jit(solution)/shard_map/all_to_all | solution.py:30
  11.8 2.1 %shard_map.112 = (f32[64,3072]{1,0:T(8,128)}, bf16[128,768]{1,0:T(8,128)(2,1)S(1)}) custom-call(s32[1]{0:T(128)} %bitcast.8.block_ref, f32[64,128]{1,0:T(8,128)S(1)} %bitcast.32, bf16[6144,128]{1,0:T(8,128)(2,1)S(1)} %bitcast.27, bf16[128,768]{1,0:T(8,128)(2,1)S(1)} %copy-done.12), custom_call_target="tpu_custom_call" | custom-call | flops 150994944 | bytes 1572864 | tf_op jit(solution)/shard_map/pallas_call | solution.py:109
  14.0 2.0 %collective-permute-start = (f32[64,3072]{1,0:T(8,128)}, f32[64,3072]{1,0:T(8,128)S(1)}, u32[]{:S(2)}, u32[]{:S(2)}) collective-permute-start(f32[64,3072]{1,0:T(8,128)} %get-tuple-element.22), channel_id=1, source_target_pairs={{0,1},{1,0},{2,3},{3,2},{4,5},{5,4},{6,7},{7,6},{8,9},{9,8},{10,11... | collective-permute-start | bytes 2359304 | tf_op jit(solution)/shard_map/ppermute | solution.py:34
  16.0 1.1 shard_map.113
  17.1 0.9 copy-done.8
  18.0 2.3 %collective-permute-start.3 = (bf16[128,768]{1,0:T(8,128)(2,1)S(1)}, bf16[128,768]{1,0:T(8,128)(2,1)S(1)}, u32[]{:S(2)}, u32[]{:S(2)}) collective-permute-start(bf16[128,768]{1,0:T(8,128)(2,1)S(1)} %get-tuple-element.24), channel_id=1, source_target_pairs={{0,6},{2,0},{4,2},{6,4},{1,7},{3,1},{5,3},{7,5},{8,14},{10,8},{12,... | collective-permute-start | bytes 589832 | tf_op jit(solution)/shard_map/ppermute | solution.py:457
  20.2 4.5 %collective-permute-start.2 = (bf16[128,768]{1,0:T(8,128)(2,1)S(1)}, bf16[128,768]{1,0:T(8,128)(2,1)S(1)}, u32[]{:S(2)}, u32[]{:S(2)}) collective-permute-start(bf16[128,768]{1,0:T(8,128)(2,1)S(1)} %get-tuple-element.24), channel_id=1, source_target_pairs={{0,4},{2,6},{4,0},{6,2},{1,5},{3,7},{5,1},{7,3},{8,12},{10,14},{12... | collective-permute-start | bytes 589832 | tf_op jit(solution)/shard_map/ppermute | solution.py:457
  24.8 4.3 %collective-permute-start.1 = (bf16[128,768]{1,0:T(8,128)(2,1)S(1)}, bf16[128,768]{1,0:T(8,128)(2,1)}, u32[]{:S(2)}, u32[]{:S(2)}) collective-permute-start(bf16[128,768]{1,0:T(8,128)(2,1)S(1)} %get-tuple-element.24), channel_id=1, source_target_pairs={{0,2},{2,4},{4,6},{6,0},{1,3},{3,5},{5,7},{7,1},{8,10},{10,12},{12... | collective-permute-start | bytes 589832 | tf_op jit(solution)/shard_map/ppermute | solution.py:457
  29.1 0.0 all-to-all-done.cq_ref
  29.1 1.1 copy-done.9
  30.2 1.5 %shard_map.114 = (s16[2048,128]{1,0:T(8,128)(2,1)}, f32[48,128]{1,0:T(8,128)S(1)}) custom-call(s32[1]{0:T(128)} %bitcast.2.place_ref, f32[8,112,128]{2,1,0:T(8,128)S(1)} %all-to-all-done.cq_ref, bf16[128,768]{1,0:T(8,128)(2,1)S(1)} %copy-done.12, f32[64,3072]{1,0:T(8,128)S(1)} %copy-done.9, f32[64,3072]{1,0:T(8,128)S(1)} %collective-permute-done.came_ref), custom_call_target="tpu_custom_call" | custom-call | flops 37748736 | bytes 6000000 | tf_op jit(solution)/shard_map/pallas_call | solution.py:164
  31.8 18.3 %all-to-all-start.1 = ((s16[256,8,128]{2,1,0:T(8,128)(2,1)}), s16[256,8,128]{2,1,0:T(8,128)(2,1)}, u32[]{:S(2)}, u32[]{:S(2)}) async-start(s16[256,8,128]{2,1,0:T(8,128)(2,1)} %bitcast.9), calls=%async_computation.1 | async-start | bytes 1048576 | tf_op jit(solution)/shard_map/all_to_all | solution.py:30
  50.1 1.0 pad_maximum_fusion.own_ref
  51.2 1.9 %collective-permute-start.4 = (bf16[4,128,768]{2,1,0:T(8,128)(2,1)S(1)}, bf16[4,128,768]{2,1,0:T(8,128)(2,1)S(1)}, u32[]{:S(2)}, u32[]{:S(2)}) collective-permute-start(bf16[4,128,768]{2,1,0:T(8,128)(2,1)S(1)} %pad_maximum_fusion.own_ref), channel_id=1, source_target_pairs={{0,1},{1,0},{2,3},{3,2},{4,5},{5,4},{6,7},{7,6},{8,9},{9,8},{10,11... | collective-permute-start | bytes 2359304 | tf_op jit(solution)/shard_map/ppermute | solution.py:34
  53.1 0.0 copy-start.2
  53.1 0.9 copy-done.2
  54.0 0.1 pad_add_fusion.1.at_ref
  54.0 0.1 reshape.48
  54.2 1.2 collective-permute-done.4.other_ref
  55.3 0.9 copy-done.10
  56.2 1.4 copy-done.1
  57.6 1.1 copy-done.3
  58.8 1.1 copy-done.11
  59.9 2.9 %shard_map.115.grad_ref = bf16[6144,256]{1,0:T(8,128)(2,1)S(1)} custom-call(s32[2]{0:T(128)S(1)} %pad_add_fusion.1.at_ref, bf16[4,128,768]{2,1,0:T(8,128)(2,1)S(1)} %copy-done.3, bf16[4,128,768]{2,1,0:T(8,128)(2,1)S(1)} %copy-done.11, bf16[128,128]{1,0:T(8,128)(2,1)S(1)} %copy-done.14, bf16[6144,128]{1,0:T(8,128)(2,1)S(1)} %bitcast.29), custom_call_target="tpu_custom_call" | custom-call | flops 201326592 | bytes 6291456 | tf_op jit(solution)/shard_map/pallas_call | solution.py:225
  62.8 6.6 %all-to-all-done.1 = s16[256,8,128]{2,1,0:T(8,128)(2,1)} async-done(((s16[256,8,128]{2,1,0:T(8,128)(2,1)}), s16[256,8,128]{2,1,0:T(8,128)(2,1)}, u32[]{:S(2)}, u32[]{:S(2)}) %all-to-all-start.1) | async-done | bytes 524320 | tf_op jit(solution)/shard_map/all_to_all | solution.py:30
  69.4 2.1 %shard_map.116 = s16[2048,128]{1,0:T(8,128)(2,1)S(1)} custom-call(s16[2048,128]{1,0:T(8,128)(2,1)} %bitcast.10.in_ref, bf16[6144,256]{1,0:T(8,128)(2,1)S(1)} %shard_map.115.grad_ref, f32[8,8,128]{2,1,0:T(8,128)S(1)} %pad.4.expert_ref), custom_call_target="tpu_custom_call" | custom-call | flops 1000000 | bytes 1500000 | tf_op jit(solution)/shard_map/pallas_call | solution.py:199
  71.6 32.5 %all_to_all.25 = s16[256,8,128]{2,1,0:T(8,128)(2,1)} all-to-all(s16[256,8,128]{2,1,0:T(8,128)(2,1)S(1)} %bitcast.30), channel_id=1, replica_groups=mesh['x'=4,'y'=8,'h'=2,'l'=4,'c'=2] {'x','y','h','l'}, dimensions={0} | all-to-all | bytes 1048576 | tf_op jit(solution)/shard_map/all_to_all | solution.py:30
  104.1 2.1 %collective-permute-start.5 = (s16[2048,128]{1,0:T(8,128)(2,1)}, s16[2048,128]{1,0:T(8,128)(2,1)}, u32[]{:S(2)}, u32[]{:S(2)}) collective-permute-start(s16[2048,128]{1,0:T(8,128)(2,1)} %bitcast.18.codes_ref), channel_id=1, source_target_pairs={{0,1},{1,0},{2,3},{3,2},{4,5},{5,4},{6,7},{7,6},{8,9},{9,8},{10,11... | collective-permute-start | bytes 1572872 | tf_op jit(solution)/shard_map/ppermute | solution.py:34
  106.2 2.1 %shard_map.117 = (f32[64,128]{1,0:T(8,128)S(1)}, f32[64,64]{1,0:T(8,128)S(1)}, bf16[12,128,256]{2,1,0:T(8,128)(2,1)S(1)}) custom-call(s32[1]{0:T(128)} %bitcast.1.block_ref.core_ref, s16[2048,128]{1,0:T(8,128)(2,1)} %bitcast.18.codes_ref, bf16[6144,256]{1,0:T(8,128)(2,1)S(1)} %shard_map.115.grad_ref), custom_call_target="tpu_custom_call" | custom-call | flops 201326592 | bytes 3000000 | tf_op jit(solution)/shard_map/pallas_call | solution.py:317
  108.3 0.0 copy-start.4
  108.3 3.1 %shard_map.118 = (s16[8,80,128]{2,1,0:T(8,128)(2,1)}, f32[64,64]{1,0:T(8,128)S(1)}, bf16[12,128,256]{2,1,0:T(8,128)(2,1)S(1)}) custom-call(s32[1]{0:T(128)} %bitcast.1.block_ref.core_ref, s16[2048,128]{1,0:T(8,128)(2,1)} %collective-permute-done.5.codes_ref, bf16[6144,256]{1,0:T(8,128)(2,1)S(1)} %shard_map.115.grad_ref, ...), custom_call_target="tpu_custom_call" | custom-call | flops 201326592 | bytes 3000000 | tf_op jit(solution)/shard_map/pallas_call | solution.py:328
  111.4 0.9 copy-done.6
  112.3 3.8 %all-to-all-start.3 = ((s16[8,80,128]{2,1,0:T(8,128)(2,1)}), s16[8,80,128]{2,1,0:T(8,128)(2,1)S(1)}, u32[]{:S(2)}, u32[]{:S(2)}) async-start(s16[8,80,128]{2,1,0:T(8,128)(2,1)} %get-tuple-element.29), calls=%async_computation.3 | async-start | bytes 327680 | tf_op jit(solution)/shard_map/all_to_all | solution.py:30
  116.0 0.1 pad_add_fusion.at_ref
  116.1 5.8 %cholesky.17 = f32[64,64]{1,0:T(8,128)S(1)} custom-call(f32[64,64]{1,0:T(8,128)S(1)} %get-tuple-element.28), custom_call_target="Cholesky" | custom-call | tf_op jit(solution)/shard_map/jit(cholesky)/cholesky | solution.py:472
  122.0 0.6 compare_reduce_fusion
  122.6 3.8 %all-to-all-done.3.in_ref = s16[8,80,128]{2,1,0:T(8,128)(2,1)S(1)} async-done(((s16[8,80,128]{2,1,0:T(8,128)(2,1)}), s16[8,80,128]{2,1,0:T(8,128)(2,1)S(1)}, u32[]{:S(2)}, u32[]{:S(2)}) %all-to-all-start.3) | async-done | bytes 163872 | tf_op jit(solution)/shard_map/all_to_all | solution.py:30
  126.5 1.0 shard_map.119
  127.4 5.1 %all-to-all-start.4 = ((s16[8,80,128]{2,1,0:T(8,128)(2,1)}), s16[8,80,128]{2,1,0:T(8,128)(2,1)S(1)}, u32[]{:S(2)}, u32[]{:S(2)}) async-start(s16[8,80,128]{2,1,0:T(8,128)(2,1)} %shard_map.119), calls=%async_computation.4 | async-start | bytes 327680 | tf_op jit(solution)/shard_map/all_to_all | solution.py:30
  132.6 0.7 fusion
  133.2 4.9 %custom-call.6 = f32[1,64,64]{1,2,0:T(8,128)S(1)} custom-call(f32[1,64,64]{2,1,0:T(8,128)S(1)} %fusion), custom_call_target="InvertDiagBlocksLowerTriangular" | custom-call | tf_op jit(solution)/shard_map/triangular_solve | solution.py:473
  138.1 0.2 fusion.1.inverse_ref
  138.4 6.5 %all-to-all-done.4.sums_ref = s16[8,80,128]{2,1,0:T(8,128)(2,1)S(1)} async-done(((s16[8,80,128]{2,1,0:T(8,128)(2,1)}), s16[8,80,128]{2,1,0:T(8,128)(2,1)S(1)}, u32[]{:S(2)}, u32[]{:S(2)}) %all-to-all-start.4) | async-done | bytes 163872 | tf_op jit(solution)/shard_map/all_to_all | solution.py:30
  144.9 1.1 copy-done.5
  146.0 1.1 copy-done.7
  147.1 3.2 %shard_map.120 = (bf16[96,128]{1,0:T(8,128)(2,1)}, f32[64,128]{1,0:T(8,128)}, bf16[6144,128]{1,0:T(8,128)(2,1)}, f32[1,96]{1,0:T(1,128)}) custom-call(s32[2]{0:T(128)S(1)} %pad_add_fusion.at_ref, f32[64,64]{1,0:T(8,128)S(1)} %fusion.1.inverse_ref, s16[8,80,128]{2,1,0:T(8,128)(2,1)S(1)} %all-to-all-done.4.sums_ref, bf16[12,128,256]{2,1,0:T(8,128)(2,1)S(1)} %copy-done.5, ...), custom_call_target="tpu_custom_call" | custom-call | tf_op jit(solution)/shard_map/pallas_call | solution.py:387
  (25 shorter events, 0.1 us)
Async XLA Ops:
  0.6 11.2 %copy-start.13 = (f32[128,64]{0,1:T(8,128)S(1)}, f32[128,64]{0,1:T(8,128)}, u32[]{:S(2)}) copy-start(f32[128,64]{0,1:T(8,128)} %param.11) | copy-start | bytes 98308
  0.6 11.2 %copy-start.12 = (bf16[128,768]{1,0:T(8,128)(2,1)S(1)}, bf16[128,768]{1,0:T(8,128)(2,1)}, u32[]{:S(2)}) copy-start(bf16[128,768]{1,0:T(8,128)(2,1)} %attn_ref.3) | copy-start | bytes 589828
  0.7 11.2 %copy-start = (bf16[1,6144,128]{2,1,0:T(8,128)(2,1)S(1)}, bf16[1,6144,128]{2,1,0:T(8,128)(2,1)}, u32[]{:S(2)}) copy-start(bf16[1,6144,128]{2,1,0:T(8,128)(2,1)} %param.10) | copy-start | bytes 4718596
  3.4 25.7 %all-to-all-start = ((f32[8,112,128]{2,1,0:T(8,128)}), f32[8,112,128]{2,1,0:T(8,128)S(1)}, u32[]{:S(2)}, u32[]{:S(2)}) async-start(f32[8,112,128]{2,1,0:T(8,128)} %shard_map.111), calls=%async_computation | async-start | bytes 917504 | tf_op jit(solution)/shard_map/all_to_all | solution.py:30
  14.0 15.1 %collective-permute-start = (f32[64,3072]{1,0:T(8,128)}, f32[64,3072]{1,0:T(8,128)S(1)}, u32[]{:S(2)}, u32[]{:S(2)}) collective-permute-start(f32[64,3072]{1,0:T(8,128)} %get-tuple-element.22), channel_id=1, source_target_pairs={{0,1},{1,0},{2,3},{3,2},{4,5},{5,4},{6,7},{7,6},{8,9},{9,8},{10,11... | collective-permute-start | bytes 2359304 | tf_op jit(solution)/shard_map/ppermute | solution.py:34
  17.1 0.9 copy-start.8
  18.0 32.1 %collective-permute-start.3 = (bf16[128,768]{1,0:T(8,128)(2,1)S(1)}, bf16[128,768]{1,0:T(8,128)(2,1)S(1)}, u32[]{:S(2)}, u32[]{:S(2)}) collective-permute-start(bf16[128,768]{1,0:T(8,128)(2,1)S(1)} %get-tuple-element.24), channel_id=1, source_target_pairs={{0,6},{2,0},{4,2},{6,4},{1,7},{3,1},{5,3},{7,5},{8,14},{10,8},{12,... | collective-permute-start | bytes 589832 | tf_op jit(solution)/shard_map/ppermute | solution.py:457
  20.2 29.9 %collective-permute-start.2 = (bf16[128,768]{1,0:T(8,128)(2,1)S(1)}, bf16[128,768]{1,0:T(8,128)(2,1)S(1)}, u32[]{:S(2)}, u32[]{:S(2)}) collective-permute-start(bf16[128,768]{1,0:T(8,128)(2,1)S(1)} %get-tuple-element.24), channel_id=1, source_target_pairs={{0,4},{2,6},{4,0},{6,2},{1,5},{3,7},{5,1},{7,3},{8,12},{10,14},{12... | collective-permute-start | bytes 589832 | tf_op jit(solution)/shard_map/ppermute | solution.py:457
  24.8 25.4 %collective-permute-start.1 = (bf16[128,768]{1,0:T(8,128)(2,1)S(1)}, bf16[128,768]{1,0:T(8,128)(2,1)}, u32[]{:S(2)}, u32[]{:S(2)}) collective-permute-start(bf16[128,768]{1,0:T(8,128)(2,1)S(1)} %get-tuple-element.24), channel_id=1, source_target_pairs={{0,2},{2,4},{4,6},{6,0},{1,3},{3,5},{5,7},{7,1},{8,10},{10,12},{12... | collective-permute-start | bytes 589832 | tf_op jit(solution)/shard_map/ppermute | solution.py:457
  29.1 1.1 copy-start.9
  31.8 24.5 %copy-start.14 = (bf16[128,128]{1,0:T(8,128)(2,1)S(1)}, bf16[128,128]{1,0:T(8,128)(2,1)}, u32[]{:S(2)}) copy-start(bf16[128,128]{1,0:T(8,128)(2,1)} %cols_ref.3) | copy-start | bytes 98308
  31.8 37.7 %all-to-all-start.1 = ((s16[256,8,128]{2,1,0:T(8,128)(2,1)}), s16[256,8,128]{2,1,0:T(8,128)(2,1)}, u32[]{:S(2)}, u32[]{:S(2)}) async-start(s16[256,8,128]{2,1,0:T(8,128)(2,1)} %bitcast.9), calls=%async_computation.1 | async-start | bytes 1048576 | tf_op jit(solution)/shard_map/all_to_all | solution.py:30
  51.2 4.2 %collective-permute-start.4 = (bf16[4,128,768]{2,1,0:T(8,128)(2,1)S(1)}, bf16[4,128,768]{2,1,0:T(8,128)(2,1)S(1)}, u32[]{:S(2)}, u32[]{:S(2)}) collective-permute-start(bf16[4,128,768]{2,1,0:T(8,128)(2,1)S(1)} %pad_maximum_fusion.own_ref), channel_id=1, source_target_pairs={{0,1},{1,0},{2,3},{3,2},{4,5},{5,4},{6,7},{7,6},{8,9},{9,8},{10,11... | collective-permute-start | bytes 2359304 | tf_op jit(solution)/shard_map/ppermute | solution.py:34
  53.1 0.9 copy-start.2
  55.3 0.9 copy-start.10
  56.2 1.4 copy-start.1
  57.6 1.1 copy-start.3
  58.8 1.1 copy-start.11
  104.1 4.2 %collective-permute-start.5 = (s16[2048,128]{1,0:T(8,128)(2,1)}, s16[2048,128]{1,0:T(8,128)(2,1)}, u32[]{:S(2)}, u32[]{:S(2)}) collective-permute-start(s16[2048,128]{1,0:T(8,128)(2,1)} %bitcast.18.codes_ref), channel_id=1, source_target_pairs={{0,1},{1,0},{2,3},{3,2},{4,5},{5,4},{6,7},{7,6},{8,9},{9,8},{10,11... | collective-permute-start | bytes 1572872 | tf_op jit(solution)/shard_map/ppermute | solution.py:34
  108.3 3.1 %copy-start.4 = (bf16[12,128,256]{2,1,0:T(8,128)(2,1)}, bf16[12,128,256]{2,1,0:T(8,128)(2,1)S(1)}, u32[]{:S(2)}) copy-start(bf16[12,128,256]{2,1,0:T(8,128)(2,1)S(1)} %get-tuple-element.30.mine_ref) | copy-start | bytes 2359300
  111.4 0.9 copy-start.6
  112.3 14.2 %all-to-all-start.3 = ((s16[8,80,128]{2,1,0:T(8,128)(2,1)}), s16[8,80,128]{2,1,0:T(8,128)(2,1)S(1)}, u32[]{:S(2)}, u32[]{:S(2)}) async-start(s16[8,80,128]{2,1,0:T(8,128)(2,1)} %get-tuple-element.29), calls=%async_computation.3 | async-start | bytes 327680 | tf_op jit(solution)/shard_map/all_to_all | solution.py:30
  127.4 17.4 %all-to-all-start.4 = ((s16[8,80,128]{2,1,0:T(8,128)(2,1)}), s16[8,80,128]{2,1,0:T(8,128)(2,1)S(1)}, u32[]{:S(2)}, u32[]{:S(2)}) async-start(s16[8,80,128]{2,1,0:T(8,128)(2,1)} %shard_map.119), calls=%async_computation.4 | async-start | bytes 327680 | tf_op jit(solution)/shard_map/all_to_all | solution.py:30
  144.9 1.1 copy-start.5
  146.0 1.1 copy-start.7

commit v6 on v5

--- a/solution.py
+++ b/solution.py
@@ -132,11 +132,16 @@
     )(core.reshape(1), power_t, error, attn_out)
 
 
-def share_kernel(place_ref, cq_ref, attn_ref, kept_ref, came_ref, out_ref, expert_ref, half_ref):
+def share_kernel(
+    place_ref, cq_ref, attn_ref, kept_ref, came_ref, out_ref, expert_ref, half_ref, sem
+):
+    copy = pltpu.make_async_copy(kept_ref, half_ref, sem)
+    copy.start()
     total = jnp.sum(cq_ref[...], axis=0)
     expert_ref[...] = total[RANK:]
     from_attn = folded(jnp.dot(three(total[:RANK]), attn_ref[...], preferred_element_type=F32))
-    half_ref[...] = kept_ref[...] + came_ref[...]
+    copy.wait()
+    half_ref[...] += came_ref[...]
     here = pl.ds(pl.multiple_of(place_ref[0] * BLOCK, BLOCK), BLOCK)
     half_ref[:, here] += from_attn
     lane = lanes_of((8, 128))
@@ -163,14 +168,14 @@
 def share_of(place, cq_all, attn_out, kept, came):
     return pl.pallas_call(
         share_kernel,
-        in_specs=[SMEM, VMEM, VMEM, VMEM, VMEM],
+        in_specs=[SMEM, VMEM, VMEM, ANY, VMEM],
         out_specs=[VMEM, VMEM],
         out_shape=[
             jax.ShapeDtypeStruct((2048, 128), I16),
             jax.ShapeDtypeStruct((48, 128), F32),
         ],
-        scratch_shapes=[pltpu.VMEM((RANK, 4 * BLOCK), F32)],
-        compiler_params=pltpu.CompilerParams(vmem_limit_bytes=LIMIT),
+        scratch_shapes=[pltpu.VMEM((RANK, 4 * BLOCK), F32), pltpu.SemaphoreType.DMA(())],
+        compiler_params=pltpu.CompilerParams(vmem_limit_bytes=55000000),
         cost_estimate=pl.CostEstimate(
             flops=2 * 192 * 128 * 768, bytes_accessed=6000000, transcendentals=0
         ),
@@ -220,7 +225,7 @@
 
 def grad_of(place, core, own, other, out_cols, error):
     def slot(i, at):
-        return (lax.rem(at[0] + 4 - i // 2, 4), 0, 0)
+        return (lax.bitwise_xor(at[0], i // 2), 0, 0)
 
     return pl.pallas_call(
         grad_kernel,
@@ -357,8 +362,20 @@
 
 def final_kernel(
     at_ref, inverse_ref, sums_ref, mine_ref, other_ref, grad_ref,
-    approx_ref, q_ref, error_ref, expert_ref, full_ref,
+    approx_ref, q_ref, error_ref, expert_ref, full_ref, p_ref, rows_ref, sem,
 ):
+    copies = {}
+    for half, ref in enumerate((mine_ref, other_ref)):
+        core = at_ref[1] if half == 0 else 1 - at_ref[1]
+        copies[half] = pltpu.make_async_copy(ref, p_ref.at[half], sem.at[half])
+        copies[half].start()
+        for i in range(4):
+            here = pl.ds(pl.multiple_of((2 * i + core) * BLOCK, BLOCK), BLOCK)
+            there = pl.ds((4 * half + i) * BLOCK, BLOCK)
+            copies[half, i] = pltpu.make_async_copy(
+                grad_ref.at[here, :], rows_ref.at[there, :], sem.at[2 + 4 * half + i]
+            )
+            copies[half, i].start()
     raw, rows = collected(sums_ref)
     expert_ref[...] = rows[:1, :USED]
     inverse = inverse_ref[...]
@@ -369,15 +386,19 @@
     low = (weights - high.astype(F32)).astype(BF16)
     both = jnp.concatenate([high, low], axis=1)
     both = jnp.concatenate([both, both], axis=0)
-    for ref, core in ((mine_ref, at_ref[1]), (other_ref, 1 - at_ref[1])):
+    for half, core in ((0, at_ref[1]), (1, 1 - at_ref[1])):
+        copies[half].wait()
         for i in range(12):
+            if i % 3 == 0:
+                copies[half, i // 3].wait()
             rows = rows_of(i, core)
             part = lax.dot_general(
-                ref[i], both, (((0,), (0,)), ((), ())), preferred_element_type=F32
+                p_ref[half, i], both, (((0,), (0,)), ((), ())), preferred_element_type=F32
             )
             part = part[:, :128] + part[:, 128:]
             full_ref[rows, :] = part
-            grad = grad_ref[rows, :].astype(F32)
+            at = half * 4 * BLOCK + i * 256
+            grad = rows_ref[at : at + 256, :].astype(F32)
             error_ref[rows, :] = (grad[:, :128] + grad[:, 128:] - part).astype(BF16)
     here = pl.ds(pl.multiple_of(at_ref[0] * 96, 32), 96)
     approx_ref[...] = full_ref[here, :].astype(BF16)
@@ -386,7 +407,7 @@
 def final_of(data, core, inverse, sums, p_mine, p_other, grad):
     return pl.pallas_call(
         final_kernel,
-        in_specs=[SMEM, VMEM, VMEM, VMEM, VMEM, VMEM],
+        in_specs=[SMEM, VMEM, VMEM, ANY, ANY, ANY],
         out_specs=[VMEM] * 4,
         out_shape=[
             jax.ShapeDtypeStruct((96, 128), BF16),
@@ -394,8 +415,13 @@
             jax.ShapeDtypeStruct((WIDTH, 128), BF16),
             jax.ShapeDtypeStruct((1, USED), F32),
         ],
-        scratch_shapes=[pltpu.VMEM((WIDTH, 128), F32)],
-        compiler_params=pltpu.CompilerParams(vmem_limit_bytes=LIMIT),
+        scratch_shapes=[
+            pltpu.VMEM((WIDTH, 128), F32),
+            pltpu.VMEM((2, 12, 128, 256), BF16),
+            pltpu.VMEM((WIDTH, 256), BF16),
+            pltpu.SemaphoreType.DMA((10,)),
+        ],
+        compiler_params=pltpu.CompilerParams(vmem_limit_bytes=55000000),
     )(jnp.stack([data, core]), inverse, sums, p_mine, p_other, grad)
 
 
@@ -454,7 +480,7 @@
     came = swap_cores(given)
     kept, attn_here = error_share(power_t, error, core, attn_first)
     shifted = [
-        lax.ppermute(attn_here, "l", [(i, (i + k) % 4) for i in range(4)]) for k in (1, 2, 3)
+        lax.ppermute(attn_here, "l", [(i, i ^ k) for i in range(4)]) for k in (1, 2, 3)
     ]
     own = jnp.stack([attn_here, *shifted])
     codes, experts = share_of(place, cq_all, attn_out, kept, came)

time: 151 us -> 157 us (1.040)
  starting transfers between devices: 52.7 us -> 58.9 us
  Pallas kernels: 21.8 us -> 25.4 us
  local copies, waits for them, and re-layouts: 10.7 us -> 7.35 us
    all_to_all x4, starting transfers between devices: 35.6 us -> 43.2 us  [exchange(): return lax.all_to_all(values, axes, split_axis=0, concat_axis=0, tiled=True)]
    pallas_call x2, Pallas kernels: 4.7 us -> 9.38 us  [the longest x1 5.37 us: final_of(): pl.pallas_call(final_kernel, in_specs=[SMEM, VMEM, VMEM, ANY, ANY, ANY],...]
    unnamed x30 -> x28, local copies, waits for them, and re-layouts: 10.6 us -> 7.24 us
  transfers between devices with their start and end apart: 10 -> 10, of which waited for: 4 -> 4; matrix products, arithmetic and copies ran while one was open for 9% -> 8% of each run, Pallas kernels for 6% -> 7%
where the time goes in v6:
time: 157 us; the launch traced here: 156 us
  starting transfers between devices  58.9 us (38%)
  blocking collectives  32.3 us (21%)
  Pallas kernels  25.4 us (16%)
  waiting for transfers between devices  18.7 us (12%)
  other arithmetic  12.3 us (8%)
  local copies, waits for them, and re-layouts  7.35 us (5%)
    all_to_all x4, starting transfers between devices, exchange(): return lax.all_to_all(values, axes, split_axis=0, concat_axis=0, tiled=True)  43.2 us
    all_to_all x1, blocking collectives, exchange(): return lax.all_to_all(values, axes, split_axis=0, concat_axis=0, tiled=True)  32.3 us
    all_to_all x4, waiting for transfers between devices, exchange(): return lax.all_to_all(values, axes, split_axis=0, concat_axis=0, tiled=True)  17.5 us
    ppermute x3, starting transfers between devices, local(): lax.ppermute(attn_here, 'l', [(i, i ^ k) for i in range(4)])  9.59 us
    unnamed x28, local copies, waits for them, and re-layouts  7.24 us
    another operation x3, other arithmetic, local(): factor = jnp.linalg.cholesky(gram, symmetrize_input=False)  6.52 us
    ppermute x3, starting transfers between devices, swap_cores(): return lax.ppermute(values, 'c', [(0, 1), (1, 0)])  6.07 us
    another operation x2, other arithmetic, local(): lax.linalg.triangular_solve(factor, jnp.eye(RANK, dtype=F32), left_side=T...  5.55 us
  transfers between devices with their start and end apart: 10, of which 4 were waited for; matrix products, arithmetic and copies ran while one was open for 8% of the time, Pallas kernels for 7%

profile of v6, /device:TPU:64, one launch (start us, length us, event | category | flops | bytes accessed | tf_op | source)
XLA Modules:
  0.0 156.3 jit_solution(908279613503869247)
XLA Ops:
  0.7 0.0 copy-start.1
  0.7 2.7 %shard_map.111 = f32[8,112,128]{2,1,0:T(8,128)} custom-call(f32[64,128]{1,0:T(8,128)} %bitcast.31, bf16[128,128]{1,0:T(8,128)(2,1)} %cols_ref.3, bf16[128,6144]{1,0:T(8,128)(2,1)} %tokens_ref.1, s32[2,128]{1,0:T(2,128)} %bitcast.39, f32[2,128]{1,0:T(2,128)} %bitcast.40, f32[2,128]{1,0:T(2,128)} %bitcast.41), custom_call_target="tpu_custom_call" | custom-call | tf_op jit(solution)/shard_map/pallas_call | solution.py:452
  3.4 8.4 %all-to-all-start = ((f32[8,112,128]{2,1,0:T(8,128)}), f32[8,112,128]{2,1,0:T(8,128)S(1)}, u32[]{:S(2)}, u32[]{:S(2)}) async-start(f32[8,112,128]{2,1,0:T(8,128)} %shard_map.111), calls=%async_computation | async-start | bytes 917504 | tf_op jit(solution)/shard_map/all_to_all | solution.py:30
  11.8 1.1 shard_map.112
  12.9 2.1 %collective-permute-start = (f32[64,3072]{1,0:T(8,128)S(1)}, f32[64,3072]{1,0:T(8,128)}, u32[]{:S(2)}, u32[]{:S(2)}) collective-permute-start(f32[64,3072]{1,0:T(8,128)S(1)} %get-tuple-element.22), channel_id=1, source_target_pairs={{0,1},{1,0},{2,3},{3,2},{4,5},{5,4},{6,7},{7,6},{8,9},{9,8},{10,11... | collective-permute-start | bytes 2359304 | tf_op jit(solution)/shard_map/ppermute | solution.py:34
  15.0 1.1 shard_map.113
  16.1 0.0 copy-start.8
  16.1 0.9 copy-done.8
  17.0 3.4 %collective-permute-start.3 = (bf16[128,768]{1,0:T(8,128)(2,1)S(1)}, bf16[128,768]{1,0:T(8,128)(2,1)S(1)}, u32[]{:S(2)}, u32[]{:S(2)}) collective-permute-start(bf16[128,768]{1,0:T(8,128)(2,1)S(1)} %get-tuple-element.24), channel_id=1, source_target_pairs={{0,6},{2,4},{4,2},{6,0},{1,7},{3,5},{5,3},{7,1},{8,14},{10,12},{12... | collective-permute-start | bytes 589832 | tf_op jit(solution)/shard_map/ppermute | solution.py:483
  20.3 3.1 %collective-permute-start.2 = (bf16[128,768]{1,0:T(8,128)(2,1)S(1)}, bf16[128,768]{1,0:T(8,128)(2,1)S(1)}, u32[]{:S(2)}, u32[]{:S(2)}) collective-permute-start(bf16[128,768]{1,0:T(8,128)(2,1)S(1)} %get-tuple-element.24), channel_id=1, source_target_pairs={{0,4},{2,6},{4,0},{6,2},{1,5},{3,7},{5,1},{7,3},{8,12},{10,14},{12... | collective-permute-start | bytes 589832 | tf_op jit(solution)/shard_map/ppermute | solution.py:483
  23.5 3.1 %collective-permute-start.1 = (bf16[128,768]{1,0:T(8,128)(2,1)S(1)}, bf16[128,768]{1,0:T(8,128)(2,1)S(1)}, u32[]{:S(2)}, u32[]{:S(2)}) collective-permute-start(bf16[128,768]{1,0:T(8,128)(2,1)S(1)} %get-tuple-element.24), channel_id=1, source_target_pairs={{0,2},{2,0},{4,6},{6,4},{1,3},{3,1},{5,7},{7,5},{8,10},{10,8},{12,... | collective-permute-start | bytes 589832 | tf_op jit(solution)/shard_map/ppermute | solution.py:483
  26.6 0.0 all-to-all-done.cq_ref
  26.6 4.0 %shard_map.114 = (s16[2048,128]{1,0:T(8,128)(2,1)}, f32[48,128]{1,0:T(8,128)S(1)}) custom-call(s32[1]{0:T(128)} %bitcast.2.place_ref, f32[8,112,128]{2,1,0:T(8,128)S(1)} %all-to-all-done.cq_ref, bf16[128,768]{1,0:T(8,128)(2,1)S(1)} %copy-done.11, f32[64,3072]{1,0:T(8,128)} %copy-done.8, f32[64,3072]{1,0:T(8,128)} %collective-permute-done.came_ref), custom_call_target="tpu_custom_call" | custom-call | flops 37748736 | bytes 6000000 | tf_op jit(solution)/shard_map/pallas_call | solution.py:169
  30.6 0.0 copy-start.13
  30.6 25.8 %all-to-all-start.1 = ((s16[256,8,128]{2,1,0:T(8,128)(2,1)}), s16[256,8,128]{2,1,0:T(8,128)(2,1)}, u32[]{:S(2)}, u32[]{:S(2)}) async-start(s16[256,8,128]{2,1,0:T(8,128)(2,1)} %bitcast.9), calls=%async_computation.1 | async-start | bytes 1048576 | tf_op jit(solution)/shard_map/all_to_all | solution.py:30
  56.4 0.0 collective-permute-done.2
  56.4 0.1 pad_maximum_fusion.own_ref
  56.5 1.9 %collective-permute-start.4 = (bf16[4,128,768]{2,1,0:T(8,128)(2,1)S(1)}, bf16[4,128,768]{2,1,0:T(8,128)(2,1)S(1)}, u32[]{:S(2)}, u32[]{:S(2)}) collective-permute-start(bf16[4,128,768]{2,1,0:T(8,128)(2,1)S(1)} %pad_maximum_fusion.own_ref), channel_id=1, source_target_pairs={{0,1},{1,0},{2,3},{3,2},{4,5},{5,4},{6,7},{7,6},{8,9},{9,8},{10,11... | collective-permute-start | bytes 2359304 | tf_op jit(solution)/shard_map/ppermute | solution.py:34
  58.5 0.0 copy-start.3
  58.5 0.9 copy-done.3
  59.3 0.1 pad_add_fusion.1.at_ref
  59.4 0.1 reshape.48
  59.5 1.2 collective-permute-done.4.other_ref
  60.7 0.9 copy-done.9
  61.6 1.4 copy-done.2
  63.0 1.1 copy-done.4
  64.2 1.1 copy-done.10
  65.3 2.9 %shard_map.115.grad_ref = bf16[6144,256]{1,0:T(8,128)(2,1)S(1)} custom-call(s32[2]{0:T(128)S(1)} %pad_add_fusion.1.at_ref, bf16[4,128,768]{2,1,0:T(8,128)(2,1)S(1)} %copy-done.4, bf16[4,128,768]{2,1,0:T(8,128)(2,1)S(1)} %copy-done.10, bf16[128,128]{1,0:T(8,128)(2,1)S(1)} %copy-done.13, bf16[6144,128]{1,0:T(8,128)(2,1)S(1)} %bitcast.29), custom_call_target="tpu_custom_call" | custom-call | flops 201326592 | bytes 6291456 | tf_op jit(solution)/shard_map/pallas_call | solution.py:230
  68.2 7.2 %all-to-all-done.1 = s16[256,8,128]{2,1,0:T(8,128)(2,1)} async-done(((s16[256,8,128]{2,1,0:T(8,128)(2,1)}), s16[256,8,128]{2,1,0:T(8,128)(2,1)}, u32[]{:S(2)}, u32[]{:S(2)}) %all-to-all-start.1) | async-done | bytes 524320 | tf_op jit(solution)/shard_map/all_to_all | solution.py:30
  75.3 2.1 %shard_map.116 = s16[2048,128]{1,0:T(8,128)(2,1)S(1)} custom-call(s16[2048,128]{1,0:T(8,128)(2,1)} %bitcast.10.in_ref, bf16[6144,256]{1,0:T(8,128)(2,1)S(1)} %shard_map.115.grad_ref, f32[8,8,128]{2,1,0:T(8,128)S(1)} %pad.4.expert_ref), custom_call_target="tpu_custom_call" | custom-call | flops 1000000 | bytes 1500000 | tf_op jit(solution)/shard_map/pallas_call | solution.py:204
  77.5 32.3 %all_to_all.25 = s16[256,8,128]{2,1,0:T(8,128)(2,1)} all-to-all(s16[256,8,128]{2,1,0:T(8,128)(2,1)S(1)} %bitcast.30), channel_id=1, replica_groups=mesh['x'=4,'y'=8,'h'=2,'l'=4,'c'=2] {'x','y','h','l'}, dimensions={0} | all-to-all | bytes 1048576 | tf_op jit(solution)/shard_map/all_to_all | solution.py:30
  109.8 2.1 %collective-permute-start.5 = (s16[2048,128]{1,0:T(8,128)(2,1)}, s16[2048,128]{1,0:T(8,128)(2,1)}, u32[]{:S(2)}, u32[]{:S(2)}) collective-permute-start(s16[2048,128]{1,0:T(8,128)(2,1)} %bitcast.18.codes_ref), channel_id=1, source_target_pairs={{0,1},{1,0},{2,3},{3,2},{4,5},{5,4},{6,7},{7,6},{8,9},{9,8},{10,11... | collective-permute-start | bytes 1572872 | tf_op jit(solution)/shard_map/ppermute | solution.py:34
  111.9 2.1 %shard_map.117 = (f32[64,128]{1,0:T(8,128)S(1)}, f32[64,64]{1,0:T(8,128)S(1)}, bf16[12,128,256]{2,1,0:T(8,128)(2,1)S(1)}) custom-call(s32[1]{0:T(128)} %bitcast.1.block_ref.core_ref, s16[2048,128]{1,0:T(8,128)(2,1)} %bitcast.18.codes_ref, bf16[6144,256]{1,0:T(8,128)(2,1)S(1)} %shard_map.115.grad_ref), custom_call_target="tpu_custom_call" | custom-call | flops 201326592 | bytes 3000000 | tf_op jit(solution)/shard_map/pallas_call | solution.py:322
  114.0 0.0 copy-start.5
  114.1 3.1 %shard_map.118 = (s16[8,80,128]{2,1,0:T(8,128)(2,1)}, f32[64,64]{1,0:T(8,128)S(1)}, bf16[12,128,256]{2,1,0:T(8,128)(2,1)S(1)}) custom-call(s32[1]{0:T(128)} %bitcast.1.block_ref.core_ref, s16[2048,128]{1,0:T(8,128)(2,1)} %collective-permute-done.5.codes_ref, bf16[6144,256]{1,0:T(8,128)(2,1)S(1)} %shard_map.115.grad_ref, ...), custom_call_target="tpu_custom_call" | custom-call | flops 201326592 | bytes 3000000 | tf_op jit(solution)/shard_map/pallas_call | solution.py:333
  117.2 0.9 copy-done.7
  118.1 3.9 %all-to-all-start.3 = ((s16[8,80,128]{2,1,0:T(8,128)(2,1)}), s16[8,80,128]{2,1,0:T(8,128)(2,1)S(1)}, u32[]{:S(2)}, u32[]{:S(2)}) async-start(s16[8,80,128]{2,1,0:T(8,128)(2,1)} %get-tuple-element.29), calls=%async_computation.3 | async-start | bytes 327680 | tf_op jit(solution)/shard_map/all_to_all | solution.py:30
  121.9 0.1 pad_add_fusion.at_ref
  122.0 5.8 %cholesky.17 = f32[64,64]{1,0:T(8,128)S(1)} custom-call(f32[64,64]{1,0:T(8,128)S(1)} %get-tuple-element.28), custom_call_target="Cholesky" | custom-call | tf_op jit(solution)/shard_map/jit(cholesky)/cholesky | solution.py:498
  127.9 0.6 compare_reduce_fusion
  128.5 3.8 %all-to-all-done.3.in_ref = s16[8,80,128]{2,1,0:T(8,128)(2,1)S(1)} async-done(((s16[8,80,128]{2,1,0:T(8,128)(2,1)}), s16[8,80,128]{2,1,0:T(8,128)(2,1)S(1)}, u32[]{:S(2)}, u32[]{:S(2)}) %all-to-all-start.3) | async-done | bytes 163872 | tf_op jit(solution)/shard_map/all_to_all | solution.py:30
  132.4 1.0 shard_map.119
  133.3 5.1 %all-to-all-start.4 = ((s16[8,80,128]{2,1,0:T(8,128)(2,1)}), s16[8,80,128]{2,1,0:T(8,128)(2,1)S(1)}, u32[]{:S(2)}, u32[]{:S(2)}) async-start(s16[8,80,128]{2,1,0:T(8,128)(2,1)} %shard_map.119), calls=%async_computation.4 | async-start | bytes 327680 | tf_op jit(solution)/shard_map/all_to_all | solution.py:30
  138.5 0.7 fusion
  139.2 4.9 %custom-call.6 = f32[1,64,64]{1,2,0:T(8,128)S(1)} custom-call(f32[1,64,64]{2,1,0:T(8,128)S(1)} %fusion), custom_call_target="InvertDiagBlocksLowerTriangular" | custom-call | tf_op jit(solution)/shard_map/triangular_solve | solution.py:499
  144.0 0.2 fusion.1.inverse_ref
  144.3 6.5 %all-to-all-done.4.sums_ref = s16[8,80,128]{2,1,0:T(8,128)(2,1)S(1)} async-done(((s16[8,80,128]{2,1,0:T(8,128)(2,1)}), s16[8,80,128]{2,1,0:T(8,128)(2,1)S(1)}, u32[]{:S(2)}, u32[]{:S(2)}) %all-to-all-start.4) | async-done | bytes 163872 | tf_op jit(solution)/shard_map/all_to_all | solution.py:30
  150.8 5.4 %shard_map.120 = (bf16[96,128]{1,0:T(8,128)(2,1)}, f32[64,128]{1,0:T(8,128)}, bf16[6144,128]{1,0:T(8,128)(2,1)}, f32[1,96]{1,0:T(1,128)}) custom-call(s32[2]{0:T(128)S(1)} %pad_add_fusion.at_ref, f32[64,64]{1,0:T(8,128)S(1)} %fusion.1.inverse_ref, s16[8,80,128]{2,1,0:T(8,128)(2,1)S(1)} %all-to-all-done.4.sums_ref, bf16[12,128,256]{2,1,0:T(8,128)(2,1)S(1)} %copy-done.6, ...), custom_call_target="tpu_custom_call" | custom-call | tf_op jit(solution)/shard_map/pallas_call | solution.py:408
  (23 shorter events, 0.1 us)
Async XLA Ops:
  0.6 11.2 %copy-start.12 = (f32[128,64]{0,1:T(8,128)S(1)}, f32[128,64]{0,1:T(8,128)}, u32[]{:S(2)}) copy-start(f32[128,64]{0,1:T(8,128)} %param.11) | copy-start | bytes 98308
  0.6 11.2 %copy-start.11 = (bf16[128,768]{1,0:T(8,128)(2,1)S(1)}, bf16[128,768]{1,0:T(8,128)(2,1)}, u32[]{:S(2)}) copy-start(bf16[128,768]{1,0:T(8,128)(2,1)} %attn_ref.3) | copy-start | bytes 589828
  0.7 11.2 %copy-start.1 = (bf16[1,6144,128]{2,1,0:T(8,128)(2,1)S(1)}, bf16[1,6144,128]{2,1,0:T(8,128)(2,1)}, u32[]{:S(2)}) copy-start(bf16[1,6144,128]{2,1,0:T(8,128)(2,1)} %param.10) | copy-start | bytes 4718596
  3.4 23.2 %all-to-all-start = ((f32[8,112,128]{2,1,0:T(8,128)}), f32[8,112,128]{2,1,0:T(8,128)S(1)}, u32[]{:S(2)}, u32[]{:S(2)}) async-start(f32[8,112,128]{2,1,0:T(8,128)} %shard_map.111), calls=%async_computation | async-start | bytes 917504 | tf_op jit(solution)/shard_map/all_to_all | solution.py:30
  12.9 13.7 %collective-permute-start = (f32[64,3072]{1,0:T(8,128)S(1)}, f32[64,3072]{1,0:T(8,128)}, u32[]{:S(2)}, u32[]{:S(2)}) collective-permute-start(f32[64,3072]{1,0:T(8,128)S(1)} %get-tuple-element.22), channel_id=1, source_target_pairs={{0,1},{1,0},{2,3},{3,2},{4,5},{5,4},{6,7},{7,6},{8,9},{9,8},{10,11... | collective-permute-start | bytes 2359304 | tf_op jit(solution)/shard_map/ppermute | solution.py:34
  16.1 0.9 copy-start.8
  17.0 39.4 %collective-permute-start.3 = (bf16[128,768]{1,0:T(8,128)(2,1)S(1)}, bf16[128,768]{1,0:T(8,128)(2,1)S(1)}, u32[]{:S(2)}, u32[]{:S(2)}) collective-permute-start(bf16[128,768]{1,0:T(8,128)(2,1)S(1)} %get-tuple-element.24), channel_id=1, source_target_pairs={{0,6},{2,4},{4,2},{6,0},{1,7},{3,5},{5,3},{7,1},{8,14},{10,12},{12... | collective-permute-start | bytes 589832 | tf_op jit(solution)/shard_map/ppermute | solution.py:483
  20.3 36.1 %collective-permute-start.2 = (bf16[128,768]{1,0:T(8,128)(2,1)S(1)}, bf16[128,768]{1,0:T(8,128)(2,1)S(1)}, u32[]{:S(2)}, u32[]{:S(2)}) collective-permute-start(bf16[128,768]{1,0:T(8,128)(2,1)S(1)} %get-tuple-element.24), channel_id=1, source_target_pairs={{0,4},{2,6},{4,0},{6,2},{1,5},{3,7},{5,1},{7,3},{8,12},{10,14},{12... | collective-permute-start | bytes 589832 | tf_op jit(solution)/shard_map/ppermute | solution.py:483
  23.5 32.9 %collective-permute-start.1 = (bf16[128,768]{1,0:T(8,128)(2,1)S(1)}, bf16[128,768]{1,0:T(8,128)(2,1)S(1)}, u32[]{:S(2)}, u32[]{:S(2)}) collective-permute-start(bf16[128,768]{1,0:T(8,128)(2,1)S(1)} %get-tuple-element.24), channel_id=1, source_target_pairs={{0,2},{2,0},{4,6},{6,4},{1,3},{3,1},{5,7},{7,5},{8,10},{10,8},{12,... | collective-permute-start | bytes 589832 | tf_op jit(solution)/shard_map/ppermute | solution.py:483
  30.6 31.0 %copy-start.13 = (bf16[128,128]{1,0:T(8,128)(2,1)S(1)}, bf16[128,128]{1,0:T(8,128)(2,1)}, u32[]{:S(2)}) copy-start(bf16[128,128]{1,0:T(8,128)(2,1)} %cols_ref.3) | copy-start | bytes 98308
  30.6 44.7 %all-to-all-start.1 = ((s16[256,8,128]{2,1,0:T(8,128)(2,1)}), s16[256,8,128]{2,1,0:T(8,128)(2,1)}, u32[]{:S(2)}, u32[]{:S(2)}) async-start(s16[256,8,128]{2,1,0:T(8,128)(2,1)} %bitcast.9), calls=%async_computation.1 | async-start | bytes 1048576 | tf_op jit(solution)/shard_map/all_to_all | solution.py:30
  56.5 4.2 %collective-permute-start.4 = (bf16[4,128,768]{2,1,0:T(8,128)(2,1)S(1)}, bf16[4,128,768]{2,1,0:T(8,128)(2,1)S(1)}, u32[]{:S(2)}, u32[]{:S(2)}) collective-permute-start(bf16[4,128,768]{2,1,0:T(8,128)(2,1)S(1)} %pad_maximum_fusion.own_ref), channel_id=1, source_target_pairs={{0,1},{1,0},{2,3},{3,2},{4,5},{5,4},{6,7},{7,6},{8,9},{9,8},{10,11... | collective-permute-start | bytes 2359304 | tf_op jit(solution)/shard_map/ppermute | solution.py:34
  58.5 0.9 copy-start.3
  60.7 0.9 copy-start.9
  61.6 1.4 copy-start.2
  63.0 1.1 copy-start.4
  64.2 1.1 copy-start.10
  68.2 45.9 %copy-start = (bf16[6144,256]{1,0:T(8,128)(2,1)}, bf16[6144,256]{1,0:T(8,128)(2,1)S(1)}, u32[]{:S(2)}) copy-start(bf16[6144,256]{1,0:T(8,128)(2,1)S(1)} %shard_map.115.grad_ref) | copy-start | bytes 9437188
  109.8 4.2 %collective-permute-start.5 = (s16[2048,128]{1,0:T(8,128)(2,1)}, s16[2048,128]{1,0:T(8,128)(2,1)}, u32[]{:S(2)}, u32[]{:S(2)}) collective-permute-start(s16[2048,128]{1,0:T(8,128)(2,1)} %bitcast.18.codes_ref), channel_id=1, source_target_pairs={{0,1},{1,0},{2,3},{3,2},{4,5},{5,4},{6,7},{7,6},{8,9},{9,8},{10,11... | collective-permute-start | bytes 1572872 | tf_op jit(solution)/shard_map/ppermute | solution.py:34
  114.0 3.1 %copy-start.5 = (bf16[12,128,256]{2,1,0:T(8,128)(2,1)}, bf16[12,128,256]{2,1,0:T(8,128)(2,1)S(1)}, u32[]{:S(2)}) copy-start(bf16[12,128,256]{2,1,0:T(8,128)(2,1)S(1)} %get-tuple-element.30.mine_ref) | copy-start | bytes 2359300
  117.2 0.9 copy-start.7
  118.1 32.7 %copy-start.6 = (bf16[12,128,256]{2,1,0:T(8,128)(2,1)S(1)}, bf16[12,128,256]{2,1,0:T(8,128)(2,1)}, u32[]{:S(2)}) copy-start(bf16[12,128,256]{2,1,0:T(8,128)(2,1)} %copy-done.5) | copy-start | bytes 2359300
  118.1 14.3 %all-to-all-start.3 = ((s16[8,80,128]{2,1,0:T(8,128)(2,1)}), s16[8,80,128]{2,1,0:T(8,128)(2,1)S(1)}, u32[]{:S(2)}, u32[]{:S(2)}) async-start(s16[8,80,128]{2,1,0:T(8,128)(2,1)} %get-tuple-element.29), calls=%async_computation.3 | async-start | bytes 327680 | tf_op jit(solution)/shard_map/all_to_all | solution.py:30
  133.3 17.4 %all-to-all-start.4 = ((s16[8,80,128]{2,1,0:T(8,128)(2,1)}), s16[8,80,128]{2,1,0:T(8,128)(2,1)S(1)}, u32[]{:S(2)}, u32[]{:S(2)}) async-start(s16[8,80,128]{2,1,0:T(8,128)(2,1)} %shard_map.119), calls=%async_computation.4 | async-start | bytes 327680 | tf_op jit(solution)/shard_map/all_to_all | solution.py:30

commit v7 on v5

--- a/solution.py
+++ b/solution.py
@@ -69,10 +69,19 @@
     return lax.broadcasted_iota(jnp.int32, shape, 0) == lax.broadcasted_iota(jnp.int32, shape, 1)
 
 
-def packed(raw):
-    exponent, factor = scale_of(jnp.max(jnp.abs(raw), axis=1, keepdims=True))
-    row = jnp.sum(jnp.where(eye_of(RANK), exponent, 0.0), axis=0, keepdims=True)
-    return raw * factor, jnp.concatenate([row, jnp.zeros((7, 128), F32)], axis=0)
+def packed(rows):
+    exponent, factor = scale_of(jnp.max(jnp.abs(rows), axis=1, keepdims=True))
+    eye = eye_of(rows.shape[0])
+    return rows * factor, jnp.sum(jnp.where(eye, exponent, 0.0), axis=0, keepdims=True)
+
+
+def unscaled(codes, row):
+    exponent = jnp.sum(jnp.where(eye_of(codes.shape[0]), row, 0.0), axis=1, keepdims=True)
+    return codes * (jnp.exp2(exponent * (1.0 / STEP)) * (1.0 / TOP))
+
+
+def floats(codes):
+    return codes.astype(jnp.int32).astype(F32)
 
 
 def tagged(rows):
@@ -85,18 +94,15 @@
 def collected(ref):
     raw = jnp.zeros((RANK, 128), F32)
     rows = jnp.zeros((8, 128), F32)
-    eye = eye_of(RANK)
     for i in range(8):
-        codes = ref[i, :RANK, :].astype(jnp.int32).astype(F32)
-        rest = ref[i, RANK:, :].astype(jnp.int32).astype(F32)
-        exponent = jnp.sum(jnp.where(eye, rest[8:9, :], 0.0), axis=1, keepdims=True)
-        raw += codes * (jnp.exp2(exponent * (1.0 / STEP)) * (1.0 / TOP))
+        rest = floats(ref[i, RANK:, :])
+        raw += unscaled(floats(ref[i, :RANK, :]), rest[8:9])
         rows += rest[:8] * (jnp.exp2(rest[:8, 127:128] * (1.0 / STEP)) * (1.0 / TOP))
     return raw, rows
 
 
-def error_kernel(block_ref, q_ref, error_ref, attn_ref, out_ref, pass_ref):
-    del block_ref
+def error_kernel(block_ref, q_ref, error_ref, attn_ref, other_ref, out_ref, pass_ref):
+    del block_ref, other_ref
     pass_ref[...] = attn_ref[...]
     out_ref[...] = folded(
         lax.dot_general(
@@ -105,7 +111,7 @@
     )
 
 
-def error_share(power_t, error, core, attn_out):
+def error_share(power_t, error, core, attn_out, other):
     return pl.pallas_call(
         error_kernel,
         grid_spec=pltpu.PrefetchScalarGridSpec(
@@ -115,6 +121,7 @@
                 pl.BlockSpec((RANK, 128), lambda i, core: (0, 0)),
                 pl.BlockSpec((BLOCK, 128), lambda i, core: (2 * i + core[0], 0)),
                 pl.BlockSpec((32, BLOCK), lambda i, core: (i, 0)),
+                ANY,
             ],
             out_specs=[
                 pl.BlockSpec((RANK, BLOCK), lambda i, core: (0, i)),
@@ -129,11 +136,15 @@
         cost_estimate=pl.CostEstimate(
             flops=2 * 192 * 128 * 3072, bytes_accessed=3072 * 512, transcendentals=0
         ),
-    )(core.reshape(1), power_t, error, attn_out)
+    )(core.reshape(1), power_t, error, attn_out, other)
 
 
 def share_kernel(place_ref, cq_ref, attn_ref, kept_ref, came_ref, out_ref, expert_ref, half_ref):
-    total = jnp.sum(cq_ref[...], axis=0)
+    total = jnp.zeros((RANK + 48, 128), F32)
+    for i in range(8):
+        total += unscaled(
+            floats(cq_ref[i, : RANK + 48, :]), floats(cq_ref[i, RANK + 48 :, :])[:1]
+        )
     expert_ref[...] = total[RANK:]
     from_attn = folded(jnp.dot(three(total[:RANK]), attn_ref[...], preferred_element_type=F32))
     half_ref[...] = kept_ref[...] + came_ref[...]
@@ -177,15 +188,23 @@
     )(place.reshape(1), cq_all, attn_out, kept, came)
 
 
-def sum_kernel(in_ref, grad_ref, expert_ref, out_ref):
+def sum_kernel(in_ref, grad_ref, expert_ref, out_ref, tiles_ref, sem):
     del grad_ref, expert_ref
+    copies = []
+    for i in range(4):
+        here = pl.ds(512 * i, 512)
+        copies.append(pltpu.make_async_copy(in_ref.at[here, :], tiles_ref.at[here, :], sem.at[i]))
+        copies[-1].start()
 
     def step(i, total):
         at = pl.multiple_of(i * 64, 64)
-        parts = [decoded(in_ref[pl.ds(at + 16 * j, 16), :]) for j in range(4)]
+        parts = [decoded(tiles_ref[pl.ds(at + 16 * j, 16), :]) for j in range(4)]
         return total + ((parts[0] + parts[1]) + (parts[2] + parts[3]))
 
-    total = lax.fori_loop(0, 32, step, jnp.zeros((16, 128), F32), unroll=4)
+    total = jnp.zeros((16, 128), F32)
+    for i in range(4):
+        copies[i].wait()
+        total = lax.fori_loop(8 * i, 8 * i + 8, step, total, unroll=4)
     total = total[:8] + total[8:]
     used = lanes_of((8, 128)) < USED
     largest = jnp.max(jnp.where(used, jnp.abs(total), 0.0), axis=1, keepdims=True)
@@ -198,9 +217,10 @@
 def summed(received, *others):
     return pl.pallas_call(
         sum_kernel,
-        in_specs=[VMEM, ANY, ANY],
+        in_specs=[ANY, ANY, ANY],
         out_specs=VMEM,
         out_shape=jax.ShapeDtypeStruct((2048, 128), I16),
+        scratch_shapes=[pltpu.VMEM((2048, 128), I16), pltpu.SemaphoreType.DMA((4,))],
         compiler_params=pltpu.CompilerParams(vmem_limit_bytes=LIMIT),
         cost_estimate=pl.CostEstimate(flops=1000000, bytes_accessed=1500000, transcendentals=0),
     )(received, *others)
@@ -301,8 +321,9 @@
     gram_ref[...] = square_ref[...] + squared(p_ref)
     codes, scales = packed(mine_ref[...] + product(p_ref, grad_ref, 1 - core_ref[0]))
     codes = coded(codes)
+    blank = jnp.zeros((7, 128), F32)
     for i in range(8):
-        rest = jnp.concatenate([tagged(expert_ref[i]), scales], axis=0)
+        rest = jnp.concatenate([tagged(expert_ref[i]), scales, blank], axis=0)
         out_ref[i, :RANK, :] = codes
         out_ref[i, RANK:, :] = coded(rest)
 
@@ -338,11 +359,13 @@
 def pass_kernel(in_ref, out_ref):
     raw, rows = collected(in_ref)
     codes, scales = packed(raw)
+    codes = coded(codes)
     rows = tagged(rows)
+    blank = jnp.zeros((7, 128), F32)
     for i in range(8):
         mine = jnp.broadcast_to(rows[i : i + 1], (8, 128))
-        out_ref[i, :RANK, :] = coded(codes)
-        out_ref[i, RANK:, :] = coded(jnp.concatenate([mine, scales], axis=0))
+        out_ref[i, :RANK, :] = codes
+        out_ref[i, RANK:, :] = coded(jnp.concatenate([mine, scales, blank], axis=0))
 
 
 def passed(received):
@@ -399,14 +422,14 @@
     )(jnp.stack([data, core]), inverse, sums, p_mine, p_other, grad)
 
 
-def first_kernel(q_ref, cols_ref, tokens_ref, routes_ref, logits_ref, score_ref, out_ref):
+def first_kernel(
+    q_ref, cols_ref, tokens_ref, routes_ref, logits_ref, score_ref, out_ref, expert_ref
+):
     part = folded(
         lax.dot_general(
             three(q_ref[...]), cols_ref[...], (((1,), (1,)), ((), ())), preferred_element_type=F32
         )
     )
-    for i in range(8):
-        out_ref[i, :RANK, :] = part
     first = 1.0 / (1.0 + jnp.exp(logits_ref[1:2, :] - logits_ref[0:1, :]))
     rows = first * (1.0 - first) * (score_ref[0:1, :] - score_ref[1:2, :])
     rows = jnp.broadcast_to(rows, (8, 128))
@@ -416,7 +439,12 @@
     )
     experts = jnp.dot(spread.astype(BF16), tokens_ref[...], preferred_element_type=F32)
     for t in range(48):
-        out_ref[:, RANK + t, :] = experts[:, t * 128 : t * 128 + 128]
+        expert_ref[:, t, :] = experts[:, t * 128 : t * 128 + 128]
+    blank = jnp.zeros((15, 128), F32)
+    for i in range(8):
+        codes, scales = packed(jnp.concatenate([part, expert_ref[i]], axis=0))
+        out_ref[i, : RANK + 48, :] = coded(codes)
+        out_ref[i, RANK + 48 :, :] = coded(jnp.concatenate([scales, blank], axis=0))
 
 
 def first_of(power_t, out_cols, tokens, routes_t, logits_t, score_t):
@@ -434,8 +462,9 @@
             whole(2, 128),
             whole(2, 128),
         ],
-        out_specs=whole(8, RANK + 48, 128),
-        out_shape=jax.ShapeDtypeStruct((8, RANK + 48, 128), F32),
+        out_specs=whole(8, RANK + 64, 128),
+        out_shape=jax.ShapeDtypeStruct((8, RANK + 64, 128), I16),
+        scratch_shapes=[pltpu.VMEM((8, 48, 128), F32)],
         compiler_params=pltpu.CompilerParams(vmem_limit_bytes=MOST),
     )(power_t, out_cols, tokens, routes_t, logits_t, score_t)
 
@@ -447,12 +476,12 @@
     data = (lax.axis_index("x") * 8 + lax.axis_index("y")) * 2 + lax.axis_index("h")
     power_t = power_q.T
 
-    cq_all = exchange(
-        first_of(power_t, out_cols, tokens, routes.T, route_logits.T, pair_score.T), EXPERT
-    )
-    given, attn_first = error_share(power_t, error, 1 - core, attn_out)
+    first = first_of(power_t, out_cols, tokens, routes.T, route_logits.T, pair_score.T)
+    cq_all = exchange(first, EXPERT)
+
+    given, attn_first = error_share(power_t, error, 1 - core, attn_out, first)
     came = swap_cores(given)
-    kept, attn_here = error_share(power_t, error, core, attn_first)
+    kept, attn_here = error_share(power_t, error, core, attn_first, first)
     shifted = [
         lax.ppermute(attn_here, "l", [(i, (i + k) % 4) for i in range(4)]) for k in (1, 2, 3)
     ]

time: 151 us -> 151 us (level)
  transfers between devices with their start and end apart: 10 -> 10, of which waited for: 4 -> 4; matrix products, arithmetic and copies ran while one was open for 9% -> 8% of each run, Pallas kernels for 6% -> 5%
where the time goes in v7:
time: 151 us; the launch traced here: 149 us
  starting transfers between devices  52.7 us (35%)
  blocking collectives  31.8 us (21%)
  Pallas kernels  21.9 us (15%)
  waiting for transfers between devices  18.8 us (12%)
  other arithmetic  12.3 us (8%)
  local copies, waits for them, and re-layouts  10.7 us (7%)
    all_to_all x4, starting transfers between devices, exchange(): return lax.all_to_all(values, axes, split_axis=0, concat_axis=0, tiled=True)  35.8 us
    all_to_all x1, blocking collectives, exchange(): return lax.all_to_all(values, axes, split_axis=0, concat_axis=0, tiled=True)  31.8 us
    all_to_all x4, waiting for transfers between devices, exchange(): return lax.all_to_all(values, axes, split_axis=0, concat_axis=0, tiled=True)  17.7 us
    ppermute x3, starting transfers between devices, local(): lax.ppermute(attn_here, 'l', [(i, (i + k) % 4) for i in range(4)])  11 us
    unnamed x30, local copies, waits for them, and re-layouts  10.6 us
    another operation x3, other arithmetic, local(): factor = jnp.linalg.cholesky(gram, symmetrize_input=False)  6.52 us
    ppermute x3, starting transfers between devices, swap_cores(): return lax.ppermute(values, 'c', [(0, 1), (1, 0)])  5.92 us
    another operation x2, other arithmetic, local(): lax.linalg.triangular_solve(factor, jnp.eye(RANK, dtype=F32), left_side=T...  5.55 us
  transfers between devices with their start and end apart: 10, of which 4 were waited for; matrix products, arithmetic and copies ran while one was open for 8% of the time, Pallas kernels for 5%

profile of v7, /device:TPU:64, one launch (start us, length us, event | category | flops | bytes accessed | tf_op | source)
XLA Modules:
  0.0 149.4 jit_solution(4817459957448566050)
XLA Ops:
  0.7 0.0 copy-start
  0.7 2.8 %shard_map.111.other_ref = s16[8,128,128]{2,1,0:T(8,128)(2,1)} custom-call(f32[64,128]{1,0:T(8,128)} %bitcast.31, bf16[128,128]{1,0:T(8,128)(2,1)} %cols_ref.3, bf16[128,6144]{1,0:T(8,128)(2,1)} %tokens_ref.1, s32[2,128]{1,0:T(2,128)} %bitcast.39, f32[2,128]{1,0:T(2,128)} %bitcast.40, f32[2,128]{1,0:T(2,128)} %bitcast.41), custom_call_target="tpu_custom_call" | custom-call | tf_op jit(solution)/shard_map/pallas_call | solution.py:454
  3.5 2.1 %shard_map.112 = (f32[64,3072]{1,0:T(8,128)}, bf16[128,768]{1,0:T(8,128)(2,1)S(1)}) custom-call(s32[1]{0:T(128)} %bitcast.8.block_ref, f32[64,128]{1,0:T(8,128)S(1)} %bitcast.32, bf16[6144,128]{1,0:T(8,128)(2,1)S(1)} %bitcast.27, bf16[128,768]{1,0:T(8,128)(2,1)S(1)} %copy-done.10, s16[8,128,128]{2,1,0:T(8,128)(2,1)} %shard_map.111.other_ref), custom_call_target="tpu_custom_call" | custom-call | flops 150994944 | bytes 1572864 | tf_op jit(solution)/shard_map/pallas_call | solution.py:115
  5.6 1.9 %collective-permute-start = (f32[64,3072]{1,0:T(8,128)}, f32[64,3072]{1,0:T(8,128)S(1)}, u32[]{:S(2)}, u32[]{:S(2)}) collective-permute-start(f32[64,3072]{1,0:T(8,128)} %get-tuple-element.22), channel_id=1, source_target_pairs={{0,1},{1,0},{2,3},{3,2},{4,5},{5,4},{6,7},{7,6},{8,9},{9,8},{10,11... | collective-permute-start | bytes 2359304 | tf_op jit(solution)/shard_map/ppermute | solution.py:34
  7.6 8.4 %all-to-all-start = ((s16[8,128,128]{2,1,0:T(8,128)(2,1)}), s16[8,128,128]{2,1,0:T(8,128)(2,1)S(1)}, u32[]{:S(2)}, u32[]{:S(2)}) async-start(s16[8,128,128]{2,1,0:T(8,128)(2,1)} %shard_map.111.other_ref), calls=%async_computation | async-start | bytes 524288 | tf_op jit(solution)/shard_map/all_to_all | solution.py:30
  15.9 1.1 shard_map.113
  17.0 0.9 copy-done.11
  17.9 2.0 %collective-permute-start.3 = (bf16[128,768]{1,0:T(8,128)(2,1)S(1)}, bf16[128,768]{1,0:T(8,128)(2,1)S(1)}, u32[]{:S(2)}, u32[]{:S(2)}) collective-permute-start(bf16[128,768]{1,0:T(8,128)(2,1)S(1)} %get-tuple-element.24), channel_id=1, source_target_pairs={{0,6},{2,0},{4,2},{6,4},{1,7},{3,1},{5,3},{7,5},{8,14},{10,8},{12,... | collective-permute-start | bytes 589832 | tf_op jit(solution)/shard_map/ppermute | solution.py:486
  19.9 4.7 %collective-permute-start.2 = (bf16[128,768]{1,0:T(8,128)(2,1)S(1)}, bf16[128,768]{1,0:T(8,128)(2,1)S(1)}, u32[]{:S(2)}, u32[]{:S(2)}) collective-permute-start(bf16[128,768]{1,0:T(8,128)(2,1)S(1)} %get-tuple-element.24), channel_id=1, source_target_pairs={{0,4},{2,6},{4,0},{6,2},{1,5},{3,7},{5,1},{7,3},{8,12},{10,14},{12... | collective-permute-start | bytes 589832 | tf_op jit(solution)/shard_map/ppermute | solution.py:486
  24.6 4.3 %collective-permute-start.1 = (bf16[128,768]{1,0:T(8,128)(2,1)S(1)}, bf16[128,768]{1,0:T(8,128)(2,1)S(1)}, u32[]{:S(2)}, u32[]{:S(2)}) collective-permute-start(bf16[128,768]{1,0:T(8,128)(2,1)S(1)} %get-tuple-element.24), channel_id=1, source_target_pairs={{0,2},{2,4},{4,6},{6,0},{1,3},{3,5},{5,7},{7,1},{8,10},{10,12},{12... | collective-permute-start | bytes 589832 | tf_op jit(solution)/shard_map/ppermute | solution.py:486
  28.9 0.0 all-to-all-done.cq_ref
  29.0 1.1 copy-done.12
  30.1 1.6 %shard_map.114 = (s16[2048,128]{1,0:T(8,128)(2,1)}, f32[48,128]{1,0:T(8,128)S(1)}) custom-call(s32[1]{0:T(128)} %bitcast.2.place_ref, s16[8,128,128]{2,1,0:T(8,128)(2,1)S(1)} %all-to-all-done.cq_ref, bf16[128,768]{1,0:T(8,128)(2,1)S(1)} %copy-done.10, f32[64,3072]{1,0:T(8,128)S(1)} %copy-done.12, f32[64,3072]{1,0:T(8,128)S(1)} %collective-permute-done.came_ref), custom_call_target="tpu_custom_call" | custom-call | flops 37748736 | bytes 6000000 | tf_op jit(solution)/shard_map/pallas_call | solution.py:175
  31.7 18.5 %all-to-all-start.1 = ((s16[256,8,128]{2,1,0:T(8,128)(2,1)}), s16[256,8,128]{2,1,0:T(8,128)(2,1)}, u32[]{:S(2)}, u32[]{:S(2)}) async-start(s16[256,8,128]{2,1,0:T(8,128)(2,1)} %bitcast.9), calls=%async_computation.1 | async-start | bytes 1048576 | tf_op jit(solution)/shard_map/all_to_all | solution.py:30
  50.3 0.1 pad_maximum_fusion.own_ref
  50.4 1.9 %collective-permute-start.4 = (bf16[4,128,768]{2,1,0:T(8,128)(2,1)S(1)}, bf16[4,128,768]{2,1,0:T(8,128)(2,1)S(1)}, u32[]{:S(2)}, u32[]{:S(2)}) collective-permute-start(bf16[4,128,768]{2,1,0:T(8,128)(2,1)S(1)} %pad_maximum_fusion.own_ref), channel_id=1, source_target_pairs={{0,1},{1,0},{2,3},{3,2},{4,5},{5,4},{6,7},{7,6},{8,9},{9,8},{10,11... | collective-permute-start | bytes 2359304 | tf_op jit(solution)/shard_map/ppermute | solution.py:34
  52.3 0.0 copy-start.2
  52.3 0.9 copy-done.2
  53.2 0.1 pad_add_fusion.1.at_ref
  53.2 0.1 reshape.48
  53.4 1.2 collective-permute-done.4.other_ref
  54.5 0.9 copy-done.8
  55.4 1.4 copy-done.1
  56.8 1.1 copy-done.3
  58.0 1.1 copy-done.9
  59.1 2.9 %shard_map.115.grad_ref = bf16[6144,256]{1,0:T(8,128)(2,1)S(1)} custom-call(s32[2]{0:T(128)S(1)} %pad_add_fusion.1.at_ref, bf16[4,128,768]{2,1,0:T(8,128)(2,1)S(1)} %copy-done.3, bf16[4,128,768]{2,1,0:T(8,128)(2,1)S(1)} %copy-done.9, bf16[128,128]{1,0:T(8,128)(2,1)S(1)} %copy-done.14, bf16[6144,128]{1,0:T(8,128)(2,1)S(1)} %bitcast.29), custom_call_target="tpu_custom_call" | custom-call | flops 201326592 | bytes 6291456 | tf_op jit(solution)/shard_map/pallas_call | solution.py:245
  62.0 7.3 %all-to-all-done.1 = s16[256,8,128]{2,1,0:T(8,128)(2,1)} async-done(((s16[256,8,128]{2,1,0:T(8,128)(2,1)}), s16[256,8,128]{2,1,0:T(8,128)(2,1)}, u32[]{:S(2)}, u32[]{:S(2)}) %all-to-all-start.1) | async-done | bytes 524320 | tf_op jit(solution)/shard_map/all_to_all | solution.py:30
  69.3 2.0 %shard_map.116 = s16[2048,128]{1,0:T(8,128)(2,1)S(1)} custom-call(s16[2048,128]{1,0:T(8,128)(2,1)} %bitcast.10.in_ref, bf16[6144,256]{1,0:T(8,128)(2,1)S(1)} %shard_map.115.grad_ref, f32[8,8,128]{2,1,0:T(8,128)S(1)} %pad.4.expert_ref), custom_call_target="tpu_custom_call" | custom-call | flops 1000000 | bytes 1500000 | tf_op jit(solution)/shard_map/pallas_call | solution.py:218
  71.4 31.8 %all_to_all.25 = s16[256,8,128]{2,1,0:T(8,128)(2,1)} all-to-all(s16[256,8,128]{2,1,0:T(8,128)(2,1)S(1)} %bitcast.30), channel_id=1, replica_groups=mesh['x'=4,'y'=8,'h'=2,'l'=4,'c'=2] {'x','y','h','l'}, dimensions={0} | all-to-all | bytes 1048576 | tf_op jit(solution)/shard_map/all_to_all | solution.py:30
  103.2 2.1 %collective-permute-start.5 = (s16[2048,128]{1,0:T(8,128)(2,1)}, s16[2048,128]{1,0:T(8,128)(2,1)}, u32[]{:S(2)}, u32[]{:S(2)}) collective-permute-start(s16[2048,128]{1,0:T(8,128)(2,1)} %bitcast.18.codes_ref), channel_id=1, source_target_pairs={{0,1},{1,0},{2,3},{3,2},{4,5},{5,4},{6,7},{7,6},{8,9},{9,8},{10,11... | collective-permute-start | bytes 1572872 | tf_op jit(solution)/shard_map/ppermute | solution.py:34
  105.3 2.1 %shard_map.117 = (f32[64,128]{1,0:T(8,128)S(1)}, f32[64,64]{1,0:T(8,128)S(1)}, bf16[12,128,256]{2,1,0:T(8,128)(2,1)S(1)}) custom-call(s32[1]{0:T(128)} %bitcast.1.block_ref.core_ref, s16[2048,128]{1,0:T(8,128)(2,1)} %bitcast.18.codes_ref, bf16[6144,256]{1,0:T(8,128)(2,1)S(1)} %shard_map.115.grad_ref), custom_call_target="tpu_custom_call" | custom-call | flops 201326592 | bytes 3000000 | tf_op jit(solution)/shard_map/pallas_call | solution.py:338
  107.4 0.0 copy-start.4
  107.4 3.1 %shard_map.118 = (s16[8,80,128]{2,1,0:T(8,128)(2,1)}, f32[64,64]{1,0:T(8,128)S(1)}, bf16[12,128,256]{2,1,0:T(8,128)(2,1)S(1)}) custom-call(s32[1]{0:T(128)} %bitcast.1.block_ref.core_ref, s16[2048,128]{1,0:T(8,128)(2,1)} %collective-permute-done.5.codes_ref, bf16[6144,256]{1,0:T(8,128)(2,1)S(1)} %shard_map.115.grad_ref, ...), custom_call_target="tpu_custom_call" | custom-call | flops 201326592 | bytes 3000000 | tf_op jit(solution)/shard_map/pallas_call | solution.py:349
  110.5 0.9 copy-done.6
  111.4 3.8 %all-to-all-start.3 = ((s16[8,80,128]{2,1,0:T(8,128)(2,1)}), s16[8,80,128]{2,1,0:T(8,128)(2,1)S(1)}, u32[]{:S(2)}, u32[]{:S(2)}) async-start(s16[8,80,128]{2,1,0:T(8,128)(2,1)} %get-tuple-element.29), calls=%async_computation.3 | async-start | bytes 327680 | tf_op jit(solution)/shard_map/all_to_all | solution.py:30
  115.2 0.1 pad_add_fusion.at_ref
  115.2 5.8 %cholesky.17 = f32[64,64]{1,0:T(8,128)S(1)} custom-call(f32[64,64]{1,0:T(8,128)S(1)} %get-tuple-element.28), custom_call_target="Cholesky" | custom-call | tf_op jit(solution)/shard_map/jit(cholesky)/cholesky | solution.py:501
  121.1 0.6 compare_reduce_fusion
  121.8 3.8 %all-to-all-done.3.in_ref = s16[8,80,128]{2,1,0:T(8,128)(2,1)S(1)} async-done(((s16[8,80,128]{2,1,0:T(8,128)(2,1)}), s16[8,80,128]{2,1,0:T(8,128)(2,1)S(1)}, u32[]{:S(2)}, u32[]{:S(2)}) %all-to-all-start.3) | async-done | bytes 163872 | tf_op jit(solution)/shard_map/all_to_all | solution.py:30
  125.6 1.0 shard_map.119
  126.6 5.1 %all-to-all-start.4 = ((s16[8,80,128]{2,1,0:T(8,128)(2,1)}), s16[8,80,128]{2,1,0:T(8,128)(2,1)S(1)}, u32[]{:S(2)}, u32[]{:S(2)}) async-start(s16[8,80,128]{2,1,0:T(8,128)(2,1)} %shard_map.119), calls=%async_computation.4 | async-start | bytes 327680 | tf_op jit(solution)/shard_map/all_to_all | solution.py:30
  131.7 0.7 fusion
  132.4 4.9 %custom-call.6 = f32[1,64,64]{1,2,0:T(8,128)S(1)} custom-call(f32[1,64,64]{2,1,0:T(8,128)S(1)} %fusion), custom_call_target="InvertDiagBlocksLowerTriangular" | custom-call | tf_op jit(solution)/shard_map/triangular_solve | solution.py:502
  137.3 0.2 fusion.1.inverse_ref
  137.5 6.5 %all-to-all-done.4.sums_ref = s16[8,80,128]{2,1,0:T(8,128)(2,1)S(1)} async-done(((s16[8,80,128]{2,1,0:T(8,128)(2,1)}), s16[8,80,128]{2,1,0:T(8,128)(2,1)S(1)}, u32[]{:S(2)}, u32[]{:S(2)}) %all-to-all-start.4) | async-done | bytes 163872 | tf_op jit(solution)/shard_map/all_to_all | solution.py:30
  144.0 1.1 copy-done.5
  145.1 1.1 copy-done.7
  146.3 3.2 %shard_map.120 = (bf16[96,128]{1,0:T(8,128)(2,1)}, f32[64,128]{1,0:T(8,128)}, bf16[6144,128]{1,0:T(8,128)(2,1)}, f32[1,96]{1,0:T(1,128)}) custom-call(s32[2]{0:T(128)S(1)} %pad_add_fusion.at_ref, f32[64,64]{1,0:T(8,128)S(1)} %fusion.1.inverse_ref, s16[8,80,128]{2,1,0:T(8,128)(2,1)S(1)} %all-to-all-done.4.sums_ref, bf16[12,128,256]{2,1,0:T(8,128)(2,1)S(1)} %copy-done.5, ...), custom_call_target="tpu_custom_call" | custom-call | tf_op jit(solution)/shard_map/pallas_call | solution.py:410
  (25 shorter events, 0.1 us)
Async XLA Ops:
  0.6 2.9 %copy-start.13 = (f32[128,64]{0,1:T(8,128)S(1)}, f32[128,64]{0,1:T(8,128)}, u32[]{:S(2)}) copy-start(f32[128,64]{0,1:T(8,128)} %param.11) | copy-start | bytes 98308
  0.6 2.9 %copy-start.10 = (bf16[128,768]{1,0:T(8,128)(2,1)S(1)}, bf16[128,768]{1,0:T(8,128)(2,1)}, u32[]{:S(2)}) copy-start(bf16[128,768]{1,0:T(8,128)(2,1)} %attn_ref.3) | copy-start | bytes 589828
  0.7 2.9 %copy-start = (bf16[1,6144,128]{2,1,0:T(8,128)(2,1)S(1)}, bf16[1,6144,128]{2,1,0:T(8,128)(2,1)}, u32[]{:S(2)}) copy-start(bf16[1,6144,128]{2,1,0:T(8,128)(2,1)} %param.10) | copy-start | bytes 4718596
  5.6 23.3 %collective-permute-start = (f32[64,3072]{1,0:T(8,128)}, f32[64,3072]{1,0:T(8,128)S(1)}, u32[]{:S(2)}, u32[]{:S(2)}) collective-permute-start(f32[64,3072]{1,0:T(8,128)} %get-tuple-element.22), channel_id=1, source_target_pairs={{0,1},{1,0},{2,3},{3,2},{4,5},{5,4},{6,7},{7,6},{8,9},{9,8},{10,11... | collective-permute-start | bytes 2359304 | tf_op jit(solution)/shard_map/ppermute | solution.py:34
  7.6 21.4 %all-to-all-start = ((s16[8,128,128]{2,1,0:T(8,128)(2,1)}), s16[8,128,128]{2,1,0:T(8,128)(2,1)S(1)}, u32[]{:S(2)}, u32[]{:S(2)}) async-start(s16[8,128,128]{2,1,0:T(8,128)(2,1)} %shard_map.111.other_ref), calls=%async_computation | async-start | bytes 524288 | tf_op jit(solution)/shard_map/all_to_all | solution.py:30
  17.0 0.9 copy-start.11
  17.9 32.4 %collective-permute-start.3 = (bf16[128,768]{1,0:T(8,128)(2,1)S(1)}, bf16[128,768]{1,0:T(8,128)(2,1)S(1)}, u32[]{:S(2)}, u32[]{:S(2)}) collective-permute-start(bf16[128,768]{1,0:T(8,128)(2,1)S(1)} %get-tuple-element.24), channel_id=1, source_target_pairs={{0,6},{2,0},{4,2},{6,4},{1,7},{3,1},{5,3},{7,5},{8,14},{10,8},{12,... | collective-permute-start | bytes 589832 | tf_op jit(solution)/shard_map/ppermute | solution.py:486
  19.9 30.3 %collective-permute-start.2 = (bf16[128,768]{1,0:T(8,128)(2,1)S(1)}, bf16[128,768]{1,0:T(8,128)(2,1)S(1)}, u32[]{:S(2)}, u32[]{:S(2)}) collective-permute-start(bf16[128,768]{1,0:T(8,128)(2,1)S(1)} %get-tuple-element.24), channel_id=1, source_target_pairs={{0,4},{2,6},{4,0},{6,2},{1,5},{3,7},{5,1},{7,3},{8,12},{10,14},{12... | collective-permute-start | bytes 589832 | tf_op jit(solution)/shard_map/ppermute | solution.py:486
  24.6 25.6 %collective-permute-start.1 = (bf16[128,768]{1,0:T(8,128)(2,1)S(1)}, bf16[128,768]{1,0:T(8,128)(2,1)S(1)}, u32[]{:S(2)}, u32[]{:S(2)}) collective-permute-start(bf16[128,768]{1,0:T(8,128)(2,1)S(1)} %get-tuple-element.24), channel_id=1, source_target_pairs={{0,2},{2,4},{4,6},{6,0},{1,3},{3,5},{5,7},{7,1},{8,10},{10,12},{12... | collective-permute-start | bytes 589832 | tf_op jit(solution)/shard_map/ppermute | solution.py:486
  28.9 1.1 copy-start.12
  31.7 23.7 %copy-start.14 = (bf16[128,128]{1,0:T(8,128)(2,1)S(1)}, bf16[128,128]{1,0:T(8,128)(2,1)}, u32[]{:S(2)}) copy-start(bf16[128,128]{1,0:T(8,128)(2,1)} %cols_ref.3) | copy-start | bytes 98308
  31.7 37.6 %all-to-all-start.1 = ((s16[256,8,128]{2,1,0:T(8,128)(2,1)}), s16[256,8,128]{2,1,0:T(8,128)(2,1)}, u32[]{:S(2)}, u32[]{:S(2)}) async-start(s16[256,8,128]{2,1,0:T(8,128)(2,1)} %bitcast.9), calls=%async_computation.1 | async-start | bytes 1048576 | tf_op jit(solution)/shard_map/all_to_all | solution.py:30
  50.4 4.2 %collective-permute-start.4 = (bf16[4,128,768]{2,1,0:T(8,128)(2,1)S(1)}, bf16[4,128,768]{2,1,0:T(8,128)(2,1)S(1)}, u32[]{:S(2)}, u32[]{:S(2)}) collective-permute-start(bf16[4,128,768]{2,1,0:T(8,128)(2,1)S(1)} %pad_maximum_fusion.own_ref), channel_id=1, source_target_pairs={{0,1},{1,0},{2,3},{3,2},{4,5},{5,4},{6,7},{7,6},{8,9},{9,8},{10,11... | collective-permute-start | bytes 2359304 | tf_op jit(solution)/shard_map/ppermute | solution.py:34
  52.3 0.9 copy-start.2
  54.5 0.9 copy-start.8
  55.4 1.4 copy-start.1
  56.8 1.1 copy-start.3
  58.0 1.1 copy-start.9
  103.2 4.2 %collective-permute-start.5 = (s16[2048,128]{1,0:T(8,128)(2,1)}, s16[2048,128]{1,0:T(8,128)(2,1)}, u32[]{:S(2)}, u32[]{:S(2)}) collective-permute-start(s16[2048,128]{1,0:T(8,128)(2,1)} %bitcast.18.codes_ref), channel_id=1, source_target_pairs={{0,1},{1,0},{2,3},{3,2},{4,5},{5,4},{6,7},{7,6},{8,9},{9,8},{10,11... | collective-permute-start | bytes 1572872 | tf_op jit(solution)/shard_map/ppermute | solution.py:34
  107.4 3.1 %copy-start.4 = (bf16[12,128,256]{2,1,0:T(8,128)(2,1)}, bf16[12,128,256]{2,1,0:T(8,128)(2,1)S(1)}, u32[]{:S(2)}) copy-start(bf16[12,128,256]{2,1,0:T(8,128)(2,1)S(1)} %get-tuple-element.30.mine_ref) | copy-start | bytes 2359300
  110.5 0.9 copy-start.6
  111.4 14.2 %all-to-all-start.3 = ((s16[8,80,128]{2,1,0:T(8,128)(2,1)}), s16[8,80,128]{2,1,0:T(8,128)(2,1)S(1)}, u32[]{:S(2)}, u32[]{:S(2)}) async-start(s16[8,80,128]{2,1,0:T(8,128)(2,1)} %get-tuple-element.29), calls=%async_computation.3 | async-start | bytes 327680 | tf_op jit(solution)/shard_map/all_to_all | solution.py:30
  126.6 17.4 %all-to-all-start.4 = ((s16[8,80,128]{2,1,0:T(8,128)(2,1)}), s16[8,80,128]{2,1,0:T(8,128)(2,1)S(1)}, u32[]{:S(2)}, u32[]{:S(2)}) async-start(s16[8,80,128]{2,1,0:T(8,128)(2,1)} %shard_map.119), calls=%async_computation.4 | async-start | bytes 327680 | tf_op jit(solution)/shard_map/all_to_all | solution.py:30
  144.0 1.1 copy-start.5
  145.1 1.1 copy-start.7

commit v8 on v7

--- a/solution.py
+++ b/solution.py
@@ -139,7 +139,10 @@
     )(core.reshape(1), power_t, error, attn_out, other)
 
 
-def share_kernel(place_ref, cq_ref, attn_ref, kept_ref, came_ref, out_ref, expert_ref, half_ref):
+def share_kernel(
+    place_ref, core_ref, cq_ref, attn_ref, q_ref, error_ref, came_ref,
+    out_ref, expert_ref, half_ref,
+):
     total = jnp.zeros((RANK + 48, 128), F32)
     for i in range(8):
         total += unscaled(
@@ -147,7 +150,14 @@
         )
     expert_ref[...] = total[RANK:]
     from_attn = folded(jnp.dot(three(total[:RANK]), attn_ref[...], preferred_element_type=F32))
-    half_ref[...] = kept_ref[...] + came_ref[...]
+    parts = three(q_ref[...])
+    for i in range(4):
+        rows = pl.ds(pl.multiple_of((2 * i + core_ref[0]) * BLOCK, BLOCK), BLOCK)
+        kept = lax.dot_general(
+            parts, error_ref[rows, :], (((1,), (1,)), ((), ())), preferred_element_type=F32
+        )
+        lanes = slice(i * BLOCK, i * BLOCK + BLOCK)
+        half_ref[:, lanes] = folded(kept) + came_ref[:, lanes]
     here = pl.ds(pl.multiple_of(place_ref[0] * BLOCK, BLOCK), BLOCK)
     half_ref[:, here] += from_attn
     lane = lanes_of((8, 128))
@@ -171,10 +181,10 @@
             out_ref[at + 16 : at + 32, :] = coded(jnp.concatenate([c, tail], axis=0))
 
 
-def share_of(place, cq_all, attn_out, kept, came):
+def share_of(place, core, cq_all, attn_out, power_t, error, came):
     return pl.pallas_call(
         share_kernel,
-        in_specs=[SMEM, VMEM, VMEM, VMEM, VMEM],
+        in_specs=[SMEM, SMEM, VMEM, VMEM, VMEM, VMEM, VMEM],
         out_specs=[VMEM, VMEM],
         out_shape=[
             jax.ShapeDtypeStruct((2048, 128), I16),
@@ -185,7 +195,7 @@
         cost_estimate=pl.CostEstimate(
             flops=2 * 192 * 128 * 768, bytes_accessed=6000000, transcendentals=0
         ),
-    )(place.reshape(1), cq_all, attn_out, kept, came)
+    )(place.reshape(1), core.reshape(1), cq_all, attn_out, power_t, error, came)
 
 
 def sum_kernel(in_ref, grad_ref, expert_ref, out_ref, tiles_ref, sem):
@@ -479,14 +489,13 @@
     first = first_of(power_t, out_cols, tokens, routes.T, route_logits.T, pair_score.T)
     cq_all = exchange(first, EXPERT)
 
-    given, attn_first = error_share(power_t, error, 1 - core, attn_out, first)
+    given, attn_here = error_share(power_t, error, 1 - core, attn_out, first)
     came = swap_cores(given)
-    kept, attn_here = error_share(power_t, error, core, attn_first, first)
     shifted = [
         lax.ppermute(attn_here, "l", [(i, (i + k) % 4) for i in range(4)]) for k in (1, 2, 3)
     ]
     own = jnp.stack([attn_here, *shifted])
-    codes, experts = share_of(place, cq_all, attn_out, kept, came)
+    codes, experts = share_of(place, core, cq_all, attn_out, power_t, error, came)
     by_y = experts.reshape(4, 8, 2, 96).transpose(1, 0, 2, 3).reshape(8, 8, 96)
     by_y = jnp.pad(by_y, ((0, 0), (0, 0), (0, 32)))
     grad = grad_of(place, core, own, swap_cores(own), out_cols, error)

time: 151 us -> 153 us (1.013)
  waiting for transfers between devices: 18.8 us -> 21.7 us
  local copies, waits for them, and re-layouts: 10.7 us -> 8.73 us
    all_to_all x4, waiting for transfers between devices: 17.7 us -> 20.5 us  [exchange(): return lax.all_to_all(values, axes, split_axis=0, concat_axis=0, tiled=True)]
    unnamed x30 -> x26, local copies, waits for them, and re-layouts: 10.6 us -> 8.62 us
    pallas_call x2 -> x1, Pallas kernels: 3.19 us -> 2.13 us  [error_share(): pl.pallas_call(error_kernel, grid_spec=pltpu.PrefetchScalarGridSpec(num_s...]
  transfers between devices with their start and end apart: 10 -> 10, of which waited for: 4 -> 5; matrix products, arithmetic and copies ran while one was open for 8% -> 9% of each run, Pallas kernels for 5% -> 5%
where the time goes in v8:
time: 153 us; the launch traced here: 152 us
  starting transfers between devices  53.9 us (35%)
  blocking collectives  32.3 us (21%)
  waiting for transfers between devices  21.7 us (14%)
  Pallas kernels  21.1 us (14%)
  other arithmetic  13.3 us (9%)
  local copies, waits for them, and re-layouts  8.73 us (6%)
    all_to_all x4, starting transfers between devices, exchange(): return lax.all_to_all(values, axes, split_axis=0, concat_axis=0, tiled=True)  37 us
    all_to_all x1, blocking collectives, exchange(): return lax.all_to_all(values, axes, split_axis=0, concat_axis=0, tiled=True)  32.3 us
    all_to_all x4, waiting for transfers between devices, exchange(): return lax.all_to_all(values, axes, split_axis=0, concat_axis=0, tiled=True)  20.5 us
    ppermute x3, starting transfers between devices, local(): lax.ppermute(attn_here, 'l', [(i, (i + k) % 4) for i in range(4)])  11 us
    unnamed x26, local copies, waits for them, and re-layouts  8.62 us
    another operation x3, other arithmetic, local(): factor = jnp.linalg.cholesky(gram, symmetrize_input=False)  6.52 us
    ppermute x3, starting transfers between devices, swap_cores(): return lax.ppermute(values, 'c', [(0, 1), (1, 0)])  5.92 us
    another operation x2, other arithmetic, local(): lax.linalg.triangular_solve(factor, jnp.eye(RANK, dtype=F32), left_side=T...  5.55 us
  transfers between devices with their start and end apart: 10, of which 5 were waited for; matrix products, arithmetic and copies ran while one was open for 9% of the time, Pallas kernels for 5%

profile of v8, /device:TPU:64, one launch (start us, length us, event | category | flops | bytes accessed | tf_op | source)
XLA Modules:
  0.0 152.2 jit_solution(5435816118277336604)
XLA Ops:
  0.7 0.0 copy-start
  0.7 2.8 %shard_map.111.other_ref = s16[8,128,128]{2,1,0:T(8,128)(2,1)} custom-call(f32[64,128]{1,0:T(8,128)} %bitcast.31, bf16[128,128]{1,0:T(8,128)(2,1)} %cols_ref.3, bf16[128,6144]{1,0:T(8,128)(2,1)} %tokens_ref.1, s32[2,128]{1,0:T(2,128)} %bitcast.37, f32[2,128]{1,0:T(2,128)} %bitcast.38, f32[2,128]{1,0:T(2,128)} %bitcast.39), custom_call_target="tpu_custom_call" | custom-call | tf_op jit(solution)/shard_map/pallas_call | solution.py:464
  3.5 2.1 %shard_map.112 = (f32[64,3072]{1,0:T(8,128)}, bf16[128,768]{1,0:T(8,128)(2,1)S(1)}) custom-call(s32[1]{0:T(128)} %bitcast.8.block_ref, f32[64,128]{1,0:T(8,128)S(1)} %bitcast.32, bf16[6144,128]{1,0:T(8,128)(2,1)S(1)} %bitcast.27, bf16[128,768]{1,0:T(8,128)(2,1)S(1)} %copy-done.10, s16[8,128,128]{2,1,0:T(8,128)(2,1)} %shard_map.111.other_ref), custom_call_target="tpu_custom_call" | custom-call | flops 150994944 | bytes 1572864 | tf_op jit(solution)/shard_map/pallas_call | solution.py:115
  5.6 1.9 %collective-permute-start = (f32[64,3072]{1,0:T(8,128)}, f32[64,3072]{1,0:T(8,128)S(1)}, u32[]{:S(2)}, u32[]{:S(2)}) collective-permute-start(f32[64,3072]{1,0:T(8,128)} %get-tuple-element.18), channel_id=1, source_target_pairs={{0,1},{1,0},{2,3},{3,2},{4,5},{5,4},{6,7},{7,6},{8,9},{9,8},{10,11... | collective-permute-start | bytes 2359304 | tf_op jit(solution)/shard_map/ppermute | solution.py:34
  7.5 8.4 %all-to-all-start = ((s16[8,128,128]{2,1,0:T(8,128)(2,1)}), s16[8,128,128]{2,1,0:T(8,128)(2,1)S(1)}, u32[]{:S(2)}, u32[]{:S(2)}) async-start(s16[8,128,128]{2,1,0:T(8,128)(2,1)} %shard_map.111.other_ref), calls=%async_computation | async-start | bytes 524288 | tf_op jit(solution)/shard_map/all_to_all | solution.py:30
  15.9 2.0 %collective-permute-start.3 = (bf16[128,768]{1,0:T(8,128)(2,1)S(1)}, bf16[128,768]{1,0:T(8,128)(2,1)S(1)}, u32[]{:S(2)}, u32[]{:S(2)}) collective-permute-start(bf16[128,768]{1,0:T(8,128)(2,1)S(1)} %get-tuple-element.20), channel_id=1, source_target_pairs={{0,6},{2,0},{4,2},{6,4},{1,7},{3,1},{5,3},{7,5},{8,14},{10,8},{12,... | collective-permute-start | bytes 589832 | tf_op jit(solution)/shard_map/ppermute | solution.py:495
  17.9 4.7 %collective-permute-start.2 = (bf16[128,768]{1,0:T(8,128)(2,1)S(1)}, bf16[128,768]{1,0:T(8,128)(2,1)}, u32[]{:S(2)}, u32[]{:S(2)}) collective-permute-start(bf16[128,768]{1,0:T(8,128)(2,1)S(1)} %get-tuple-element.20), channel_id=1, source_target_pairs={{0,4},{2,6},{4,0},{6,2},{1,5},{3,7},{5,1},{7,3},{8,12},{10,14},{12... | collective-permute-start | bytes 589832 | tf_op jit(solution)/shard_map/ppermute | solution.py:495
  22.7 4.3 %collective-permute-start.1 = (bf16[128,768]{1,0:T(8,128)(2,1)S(1)}, bf16[128,768]{1,0:T(8,128)(2,1)}, u32[]{:S(2)}, u32[]{:S(2)}) collective-permute-start(bf16[128,768]{1,0:T(8,128)(2,1)S(1)} %get-tuple-element.20), channel_id=1, source_target_pairs={{0,2},{2,4},{4,6},{6,0},{1,3},{3,5},{5,7},{7,1},{8,10},{10,12},{12... | collective-permute-start | bytes 589832 | tf_op jit(solution)/shard_map/ppermute | solution.py:495
  27.0 3.4 %all-to-all-done.cq_ref = s16[8,128,128]{2,1,0:T(8,128)(2,1)S(1)} async-done(((s16[8,128,128]{2,1,0:T(8,128)(2,1)}), s16[8,128,128]{2,1,0:T(8,128)(2,1)S(1)}, u32[]{:S(2)}, u32[]{:S(2)}) %all-to-all-start) | async-done | bytes 262176 | tf_op jit(solution)/shard_map/all_to_all | solution.py:30
  30.3 1.9 %shard_map.113 = (s16[2048,128]{1,0:T(8,128)(2,1)}, f32[48,128]{1,0:T(8,128)S(1)}) custom-call(s32[1]{0:T(128)} %bitcast.2.place_ref, s32[1]{0:T(128)} %bitcast.1.core_ref, s16[8,128,128]{2,1,0:T(8,128)(2,1)S(1)} %all-to-all-done.cq_ref, bf16[128,768]{1,0:T(8,128)(2,1)S(1)} %copy-done.10, f32[64,128]{1,0:T(8,128)S(1)} %bitcast.33, ...), custom_call_target="tpu_custom_call" | custom-call | flops 37748736 | bytes 6000000 | tf_op jit(solution)/shard_map/pallas_call | solution.py:185
  32.3 19.7 %all-to-all-start.1 = ((s16[256,8,128]{2,1,0:T(8,128)(2,1)}), s16[256,8,128]{2,1,0:T(8,128)(2,1)}, u32[]{:S(2)}, u32[]{:S(2)}) async-start(s16[256,8,128]{2,1,0:T(8,128)(2,1)} %bitcast.9), calls=%async_computation.1 | async-start | bytes 1048576 | tf_op jit(solution)/shard_map/all_to_all | solution.py:30
  52.0 0.0 collective-permute-done.2
  52.0 0.0 collective-permute-done.1
  52.0 1.1 pad_maximum_fusion.own_ref
  53.1 1.9 %collective-permute-start.4 = (bf16[4,128,768]{2,1,0:T(8,128)(2,1)S(1)}, bf16[4,128,768]{2,1,0:T(8,128)(2,1)S(1)}, u32[]{:S(2)}, u32[]{:S(2)}) collective-permute-start(bf16[4,128,768]{2,1,0:T(8,128)(2,1)S(1)} %pad_maximum_fusion.own_ref), channel_id=1, source_target_pairs={{0,1},{1,0},{2,3},{3,2},{4,5},{5,4},{6,7},{7,6},{8,9},{9,8},{10,11... | collective-permute-start | bytes 2359304 | tf_op jit(solution)/shard_map/ppermute | solution.py:34
  55.1 0.0 copy-start.2
  55.1 0.9 copy-done.2
  56.0 0.1 pad_add_fusion.1.at_ref
  56.0 0.1 reshape.48
  56.2 1.2 collective-permute-done.4.other_ref
  57.3 0.9 copy-done.8
  58.2 1.4 copy-done.1
  59.6 1.1 copy-done.3
  60.8 1.1 copy-done.9
  61.9 2.9 %shard_map.114.grad_ref = bf16[6144,256]{1,0:T(8,128)(2,1)S(1)} custom-call(s32[2]{0:T(128)S(1)} %pad_add_fusion.1.at_ref, bf16[4,128,768]{2,1,0:T(8,128)(2,1)S(1)} %copy-done.3, bf16[4,128,768]{2,1,0:T(8,128)(2,1)S(1)} %copy-done.9, bf16[128,128]{1,0:T(8,128)(2,1)S(1)} %copy-done.12, bf16[6144,128]{1,0:T(8,128)(2,1)S(1)} %bitcast.29), custom_call_target="tpu_custom_call" | custom-call | flops 201326592 | bytes 6291456 | tf_op jit(solution)/shard_map/pallas_call | solution.py:255
  64.8 6.8 %all-to-all-done.1 = s16[256,8,128]{2,1,0:T(8,128)(2,1)} async-done(((s16[256,8,128]{2,1,0:T(8,128)(2,1)}), s16[256,8,128]{2,1,0:T(8,128)(2,1)}, u32[]{:S(2)}, u32[]{:S(2)}) %all-to-all-start.1) | async-done | bytes 524320 | tf_op jit(solution)/shard_map/all_to_all | solution.py:30
  71.6 2.0 %shard_map.115 = s16[2048,128]{1,0:T(8,128)(2,1)S(1)} custom-call(s16[2048,128]{1,0:T(8,128)(2,1)} %bitcast.10.in_ref, bf16[6144,256]{1,0:T(8,128)(2,1)S(1)} %shard_map.114.grad_ref, f32[8,8,128]{2,1,0:T(8,128)S(1)} %pad.4.expert_ref), custom_call_target="tpu_custom_call" | custom-call | flops 1000000 | bytes 1500000 | tf_op jit(solution)/shard_map/pallas_call | solution.py:228
  73.7 32.3 %all_to_all.25 = s16[256,8,128]{2,1,0:T(8,128)(2,1)} all-to-all(s16[256,8,128]{2,1,0:T(8,128)(2,1)S(1)} %bitcast.30), channel_id=1, replica_groups=mesh['x'=4,'y'=8,'h'=2,'l'=4,'c'=2] {'x','y','h','l'}, dimensions={0} | all-to-all | bytes 1048576 | tf_op jit(solution)/shard_map/all_to_all | solution.py:30
  106.0 2.1 %collective-permute-start.5 = (s16[2048,128]{1,0:T(8,128)(2,1)}, s16[2048,128]{1,0:T(8,128)(2,1)}, u32[]{:S(2)}, u32[]{:S(2)}) collective-permute-start(s16[2048,128]{1,0:T(8,128)(2,1)} %bitcast.18.codes_ref), channel_id=1, source_target_pairs={{0,1},{1,0},{2,3},{3,2},{4,5},{5,4},{6,7},{7,6},{8,9},{9,8},{10,11... | collective-permute-start | bytes 1572872 | tf_op jit(solution)/shard_map/ppermute | solution.py:34
  108.1 2.1 %shard_map.116 = (f32[64,128]{1,0:T(8,128)S(1)}, f32[64,64]{1,0:T(8,128)S(1)}, bf16[12,128,256]{2,1,0:T(8,128)(2,1)S(1)}) custom-call(s32[1]{0:T(128)} %bitcast.1.core_ref, s16[2048,128]{1,0:T(8,128)(2,1)} %bitcast.18.codes_ref, bf16[6144,256]{1,0:T(8,128)(2,1)S(1)} %shard_map.114.grad_ref), custom_call_target="tpu_custom_call" | custom-call | flops 201326592 | bytes 3000000 | tf_op jit(solution)/shard_map/pallas_call | solution.py:348
  110.2 0.0 copy-start.4
  110.2 0.0 collective-permute-done.5.codes_ref
  110.2 3.1 %shard_map.117 = (s16[8,80,128]{2,1,0:T(8,128)(2,1)}, f32[64,64]{1,0:T(8,128)S(1)}, bf16[12,128,256]{2,1,0:T(8,128)(2,1)S(1)}) custom-call(s32[1]{0:T(128)} %bitcast.1.core_ref, s16[2048,128]{1,0:T(8,128)(2,1)} %collective-permute-done.5.codes_ref, bf16[6144,256]{1,0:T(8,128)(2,1)S(1)} %shard_map.114.grad_ref, f32[64,128]{1,0:T(8,128)S(1)} %get-tuple-element.22.mine_ref, ...), custom_call_target="tpu_custom_call" | custom-call | flops 201326592 | bytes 3000000 | tf_op jit(solution)/shard_map/pallas_call | solution.py:359
  113.3 0.9 copy-done.6
  114.2 3.8 %all-to-all-start.3 = ((s16[8,80,128]{2,1,0:T(8,128)(2,1)}), s16[8,80,128]{2,1,0:T(8,128)(2,1)S(1)}, u32[]{:S(2)}, u32[]{:S(2)}) async-start(s16[8,80,128]{2,1,0:T(8,128)(2,1)} %get-tuple-element.25), calls=%async_computation.3 | async-start | bytes 327680 | tf_op jit(solution)/shard_map/all_to_all | solution.py:30
  118.0 0.1 pad_add_fusion.at_ref
  118.0 5.8 %cholesky.17 = f32[64,64]{1,0:T(8,128)S(1)} custom-call(f32[64,64]{1,0:T(8,128)S(1)} %get-tuple-element.24), custom_call_target="Cholesky" | custom-call | tf_op jit(solution)/shard_map/jit(cholesky)/cholesky | solution.py:510
  123.9 0.6 compare_reduce_fusion
  124.6 3.8 %all-to-all-done.3.in_ref = s16[8,80,128]{2,1,0:T(8,128)(2,1)S(1)} async-done(((s16[8,80,128]{2,1,0:T(8,128)(2,1)}), s16[8,80,128]{2,1,0:T(8,128)(2,1)S(1)}, u32[]{:S(2)}, u32[]{:S(2)}) %all-to-all-start.3) | async-done | bytes 163872 | tf_op jit(solution)/shard_map/all_to_all | solution.py:30
  128.4 1.0 shard_map.118
  129.4 5.1 %all-to-all-start.4 = ((s16[8,80,128]{2,1,0:T(8,128)(2,1)}), s16[8,80,128]{2,1,0:T(8,128)(2,1)S(1)}, u32[]{:S(2)}, u32[]{:S(2)}) async-start(s16[8,80,128]{2,1,0:T(8,128)(2,1)} %shard_map.118), calls=%async_computation.4 | async-start | bytes 327680 | tf_op jit(solution)/shard_map/all_to_all | solution.py:30
  134.5 0.7 fusion
  135.2 4.9 %custom-call.6 = f32[1,64,64]{1,2,0:T(8,128)S(1)} custom-call(f32[1,64,64]{2,1,0:T(8,128)S(1)} %fusion), custom_call_target="InvertDiagBlocksLowerTriangular" | custom-call | tf_op jit(solution)/shard_map/triangular_solve | solution.py:511
  140.1 0.2 fusion.1.inverse_ref
  140.3 6.5 %all-to-all-done.4.sums_ref = s16[8,80,128]{2,1,0:T(8,128)(2,1)S(1)} async-done(((s16[8,80,128]{2,1,0:T(8,128)(2,1)}), s16[8,80,128]{2,1,0:T(8,128)(2,1)S(1)}, u32[]{:S(2)}, u32[]{:S(2)}) %all-to-all-start.4) | async-done | bytes 163872 | tf_op jit(solution)/shard_map/all_to_all | solution.py:30
  146.8 1.1 copy-done.5
  147.9 1.1 copy-done.7
  149.1 3.2 %shard_map.119 = (bf16[96,128]{1,0:T(8,128)(2,1)}, f32[64,128]{1,0:T(8,128)}, bf16[6144,128]{1,0:T(8,128)(2,1)}, f32[1,96]{1,0:T(1,128)}) custom-call(s32[2]{0:T(128)S(1)} %pad_add_fusion.at_ref, f32[64,64]{1,0:T(8,128)S(1)} %fusion.1.inverse_ref, s16[8,80,128]{2,1,0:T(8,128)(2,1)S(1)} %all-to-all-done.4.sums_ref, bf16[12,128,256]{2,1,0:T(8,128)(2,1)S(1)} %copy-done.5, ...), custom_call_target="tpu_custom_call" | custom-call | tf_op jit(solution)/shard_map/pallas_call | solution.py:420
  (20 shorter events, 0.1 us)
Async XLA Ops:
  0.6 2.9 %copy-start.11 = (f32[128,64]{0,1:T(8,128)S(1)}, f32[128,64]{0,1:T(8,128)}, u32[]{:S(2)}) copy-start(f32[128,64]{0,1:T(8,128)} %param.11) | copy-start | bytes 98308
  0.6 2.8 %copy-start.10 = (bf16[128,768]{1,0:T(8,128)(2,1)S(1)}, bf16[128,768]{1,0:T(8,128)(2,1)}, u32[]{:S(2)}) copy-start(bf16[128,768]{1,0:T(8,128)(2,1)} %attn_ref.3) | copy-start | bytes 589828
  0.7 2.8 %copy-start = (bf16[1,6144,128]{2,1,0:T(8,128)(2,1)S(1)}, bf16[1,6144,128]{2,1,0:T(8,128)(2,1)}, u32[]{:S(2)}) copy-start(bf16[1,6144,128]{2,1,0:T(8,128)(2,1)} %param.10) | copy-start | bytes 4718596
  5.6 24.7 %collective-permute-start = (f32[64,3072]{1,0:T(8,128)}, f32[64,3072]{1,0:T(8,128)S(1)}, u32[]{:S(2)}, u32[]{:S(2)}) collective-permute-start(f32[64,3072]{1,0:T(8,128)} %get-tuple-element.18), channel_id=1, source_target_pairs={{0,1},{1,0},{2,3},{3,2},{4,5},{5,4},{6,7},{7,6},{8,9},{9,8},{10,11... | collective-permute-start | bytes 2359304 | tf_op jit(solution)/shard_map/ppermute | solution.py:34
  7.5 22.8 %all-to-all-start = ((s16[8,128,128]{2,1,0:T(8,128)(2,1)}), s16[8,128,128]{2,1,0:T(8,128)(2,1)S(1)}, u32[]{:S(2)}, u32[]{:S(2)}) async-start(s16[8,128,128]{2,1,0:T(8,128)(2,1)} %shard_map.111.other_ref), calls=%async_computation | async-start | bytes 524288 | tf_op jit(solution)/shard_map/all_to_all | solution.py:30
  15.9 36.1 %collective-permute-start.3 = (bf16[128,768]{1,0:T(8,128)(2,1)S(1)}, bf16[128,768]{1,0:T(8,128)(2,1)S(1)}, u32[]{:S(2)}, u32[]{:S(2)}) collective-permute-start(bf16[128,768]{1,0:T(8,128)(2,1)S(1)} %get-tuple-element.20), channel_id=1, source_target_pairs={{0,6},{2,0},{4,2},{6,4},{1,7},{3,1},{5,3},{7,5},{8,14},{10,8},{12,... | collective-permute-start | bytes 589832 | tf_op jit(solution)/shard_map/ppermute | solution.py:495
  17.9 34.1 %collective-permute-start.2 = (bf16[128,768]{1,0:T(8,128)(2,1)S(1)}, bf16[128,768]{1,0:T(8,128)(2,1)}, u32[]{:S(2)}, u32[]{:S(2)}) collective-permute-start(bf16[128,768]{1,0:T(8,128)(2,1)S(1)} %get-tuple-element.20), channel_id=1, source_target_pairs={{0,4},{2,6},{4,0},{6,2},{1,5},{3,7},{5,1},{7,3},{8,12},{10,14},{12... | collective-permute-start | bytes 589832 | tf_op jit(solution)/shard_map/ppermute | solution.py:495
  22.7 29.4 %collective-permute-start.1 = (bf16[128,768]{1,0:T(8,128)(2,1)S(1)}, bf16[128,768]{1,0:T(8,128)(2,1)}, u32[]{:S(2)}, u32[]{:S(2)}) collective-permute-start(bf16[128,768]{1,0:T(8,128)(2,1)S(1)} %get-tuple-element.20), channel_id=1, source_target_pairs={{0,2},{2,4},{4,6},{6,0},{1,3},{3,5},{5,7},{7,1},{8,10},{10,12},{12... | collective-permute-start | bytes 589832 | tf_op jit(solution)/shard_map/ppermute | solution.py:495
  32.3 25.9 %copy-start.12 = (bf16[128,128]{1,0:T(8,128)(2,1)S(1)}, bf16[128,128]{1,0:T(8,128)(2,1)}, u32[]{:S(2)}) copy-start(bf16[128,128]{1,0:T(8,128)(2,1)} %cols_ref.3) | copy-start | bytes 98308
  32.3 39.4 %all-to-all-start.1 = ((s16[256,8,128]{2,1,0:T(8,128)(2,1)}), s16[256,8,128]{2,1,0:T(8,128)(2,1)}, u32[]{:S(2)}, u32[]{:S(2)}) async-start(s16[256,8,128]{2,1,0:T(8,128)(2,1)} %bitcast.9), calls=%async_computation.1 | async-start | bytes 1048576 | tf_op jit(solution)/shard_map/all_to_all | solution.py:30
  53.1 4.2 %collective-permute-start.4 = (bf16[4,128,768]{2,1,0:T(8,128)(2,1)S(1)}, bf16[4,128,768]{2,1,0:T(8,128)(2,1)S(1)}, u32[]{:S(2)}, u32[]{:S(2)}) collective-permute-start(bf16[4,128,768]{2,1,0:T(8,128)(2,1)S(1)} %pad_maximum_fusion.own_ref), channel_id=1, source_target_pairs={{0,1},{1,0},{2,3},{3,2},{4,5},{5,4},{6,7},{7,6},{8,9},{9,8},{10,11... | collective-permute-start | bytes 2359304 | tf_op jit(solution)/shard_map/ppermute | solution.py:34
  55.1 0.9 copy-start.2
  57.3 0.9 copy-start.8
  58.2 1.4 copy-start.1
  59.6 1.1 copy-start.3
  60.8 1.1 copy-start.9
  106.0 4.2 %collective-permute-start.5 = (s16[2048,128]{1,0:T(8,128)(2,1)}, s16[2048,128]{1,0:T(8,128)(2,1)}, u32[]{:S(2)}, u32[]{:S(2)}) collective-permute-start(s16[2048,128]{1,0:T(8,128)(2,1)} %bitcast.18.codes_ref), channel_id=1, source_target_pairs={{0,1},{1,0},{2,3},{3,2},{4,5},{5,4},{6,7},{7,6},{8,9},{9,8},{10,11... | collective-permute-start | bytes 1572872 | tf_op jit(solution)/shard_map/ppermute | solution.py:34
  110.2 3.1 %copy-start.4 = (bf16[12,128,256]{2,1,0:T(8,128)(2,1)}, bf16[12,128,256]{2,1,0:T(8,128)(2,1)S(1)}, u32[]{:S(2)}) copy-start(bf16[12,128,256]{2,1,0:T(8,128)(2,1)S(1)} %get-tuple-element.26.mine_ref) | copy-start | bytes 2359300
  113.3 0.9 copy-start.6
  114.2 14.2 %all-to-all-start.3 = ((s16[8,80,128]{2,1,0:T(8,128)(2,1)}), s16[8,80,128]{2,1,0:T(8,128)(2,1)S(1)}, u32[]{:S(2)}, u32[]{:S(2)}) async-start(s16[8,80,128]{2,1,0:T(8,128)(2,1)} %get-tuple-element.25), calls=%async_computation.3 | async-start | bytes 327680 | tf_op jit(solution)/shard_map/all_to_all | solution.py:30
  129.4 17.4 %all-to-all-start.4 = ((s16[8,80,128]{2,1,0:T(8,128)(2,1)}), s16[8,80,128]{2,1,0:T(8,128)(2,1)S(1)}, u32[]{:S(2)}, u32[]{:S(2)}) async-start(s16[8,80,128]{2,1,0:T(8,128)(2,1)} %shard_map.118), calls=%async_computation.4 | async-start | bytes 327680 | tf_op jit(solution)/shard_map/all_to_all | solution.py:30
  146.8 1.1 copy-start.5
  147.9 1.1 copy-start.7

commit v9 on v8

--- a/solution.py
+++ b/solution.py
@@ -250,7 +250,8 @@
 
 def grad_of(place, core, own, other, out_cols, error):
     def slot(i, at):
-        return (lax.rem(at[0] + 4 - i // 2, 4), 0, 0)
+        apart = lax.bitwise_xor(at[0], i // 2)
+        return (lax.rem(apart, 2) * 2 + apart // 2, 0, 0)
 
     return pl.pallas_call(
         grad_kernel,
@@ -491,10 +492,10 @@
 
     given, attn_here = error_share(power_t, error, 1 - core, attn_out, first)
     came = swap_cores(given)
-    shifted = [
-        lax.ppermute(attn_here, "l", [(i, (i + k) % 4) for i in range(4)]) for k in (1, 2, 3)
-    ]
-    own = jnp.stack([attn_here, *shifted])
+    across = lax.ppermute(attn_here, "l", [(i, i ^ 2) for i in range(4)])
+    pair = jnp.stack([attn_here, across])
+    beside = lax.ppermute(pair, "l", [(i, i ^ 1) for i in range(4)])
+    own = jnp.concatenate([pair, beside])
     codes, experts = share_of(place, core, cq_all, attn_out, power_t, error, came)
     by_y = experts.reshape(4, 8, 2, 96).transpose(1, 0, 2, 3).reshape(8, 8, 96)
     by_y = jnp.pad(by_y, ((0, 0), (0, 0), (0, 32)))

time: 153 us -> 154 us (level)
  starting transfers between devices: 53.9 us -> 49.8 us
  waiting for transfers between devices: 21.7 us -> 25.5 us
    ppermute x3 -> x2, waiting for transfers between devices: 0.01 us -> 7.25 us  [the longest x1 7.25 us: local(): across = lax.ppermute(attn_here, 'l', [(i, i ^ 2) for i in range(4)])]
    all_to_all x4, waiting for transfers between devices: 20.5 us -> 17.1 us  [exchange(): return lax.all_to_all(values, axes, split_axis=0, concat_axis=0, tiled=True)]
    ppermute x3 -> x2, starting transfers between devices: 11 us -> 8.08 us  [the longest x1 6.09 us: local(): across = lax.ppermute(attn_here, 'l', [(i, i ^ 2) for i in range(4)])]
  transfers between devices with their start and end apart: 10 -> 9, of which waited for: 5 -> 5; matrix products, arithmetic and copies ran while one was open for 9% -> 9% of each run, Pallas kernels for 5% -> 5%
where the time goes in v9:
time: 154 us; the launch traced here: 153 us
  starting transfers between devices  49.8 us (32%)
  blocking collectives  32.3 us (21%)
  waiting for transfers between devices  25.5 us (17%)
  Pallas kernels  21.1 us (14%)
  other arithmetic  14.1 us (9%)
  local copies, waits for them, and re-layouts  8.7 us (6%)
    all_to_all x4, starting transfers between devices, exchange(): return lax.all_to_all(values, axes, split_axis=0, concat_axis=0, tiled=True)  35.8 us
    all_to_all x1, blocking collectives, exchange(): return lax.all_to_all(values, axes, split_axis=0, concat_axis=0, tiled=True)  32.3 us
    all_to_all x4, waiting for transfers between devices, exchange(): return lax.all_to_all(values, axes, split_axis=0, concat_axis=0, tiled=True)  17.1 us
    unnamed x26, local copies, waits for them, and re-layouts  8.59 us
    ppermute x1, waiting for transfers between devices, local(): across = lax.ppermute(attn_here, 'l', [(i, i ^ 2) for i in range(4)])  7.25 us
    another operation x3, other arithmetic, local(): factor = jnp.linalg.cholesky(gram, symmetrize_input=False)  6.52 us
    ppermute x1, starting transfers between devices, local(): across = lax.ppermute(attn_here, 'l', [(i, i ^ 2) for i in range(4)])  6.09 us
    ppermute x3, starting transfers between devices, swap_cores(): return lax.ppermute(values, 'c', [(0, 1), (1, 0)])  5.92 us
  transfers between devices with their start and end apart: 9, of which 5 were waited for; matrix products, arithmetic and copies ran while one was open for 9% of the time, Pallas kernels for 5%

profile of v9, /device:TPU:64, one launch (start us, length us, event | category | flops | bytes accessed | tf_op | source)
XLA Modules:
  0.0 152.7 jit_solution(14911750521847691924)
XLA Ops:
  0.7 0.0 copy-start
  0.7 2.8 %shard_map.111.other_ref = s16[8,128,128]{2,1,0:T(8,128)(2,1)} custom-call(f32[64,128]{1,0:T(8,128)} %bitcast.31, bf16[128,128]{1,0:T(8,128)(2,1)} %cols_ref.3, bf16[128,6144]{1,0:T(8,128)(2,1)} %tokens_ref.1, s32[2,128]{1,0:T(2,128)} %bitcast.37, f32[2,128]{1,0:T(2,128)} %bitcast.38, f32[2,128]{1,0:T(2,128)} %bitcast.39), custom_call_target="tpu_custom_call" | custom-call | tf_op jit(solution)/shard_map/pallas_call | solution.py:465
  3.5 2.1 %shard_map.112 = (f32[64,3072]{1,0:T(8,128)}, bf16[128,768]{1,0:T(8,128)(2,1)S(1)}) custom-call(s32[1]{0:T(128)} %bitcast.8.block_ref, f32[64,128]{1,0:T(8,128)S(1)} %bitcast.32, bf16[6144,128]{1,0:T(8,128)(2,1)S(1)} %bitcast.25, bf16[128,768]{1,0:T(8,128)(2,1)S(1)} %copy-done.10, s16[8,128,128]{2,1,0:T(8,128)(2,1)} %shard_map.111.other_ref), custom_call_target="tpu_custom_call" | custom-call | flops 150994944 | bytes 1572864 | tf_op jit(solution)/shard_map/pallas_call | solution.py:115
  5.6 1.9 %collective-permute-start = (f32[64,3072]{1,0:T(8,128)}, f32[64,3072]{1,0:T(8,128)S(1)}, u32[]{:S(2)}, u32[]{:S(2)}) collective-permute-start(f32[64,3072]{1,0:T(8,128)} %get-tuple-element.18), channel_id=1, source_target_pairs={{0,1},{1,0},{2,3},{3,2},{4,5},{5,4},{6,7},{7,6},{8,9},{9,8},{10,11... | collective-permute-start | bytes 2359304 | tf_op jit(solution)/shard_map/ppermute | solution.py:34
  7.5 6.1 %collective-permute-start.1 = (bf16[128,768]{1,0:T(8,128)(2,1)S(1)}, bf16[128,768]{1,0:T(8,128)(2,1)S(1)}, u32[]{:S(2)}, u32[]{:S(2)}) collective-permute-start(bf16[128,768]{1,0:T(8,128)(2,1)S(1)} %get-tuple-element.20), channel_id=1, source_target_pairs={{0,4},{2,6},{4,0},{6,2},{1,5},{3,7},{5,1},{7,3},{8,12},{10,14},{12... | collective-permute-start | bytes 589832 | tf_op jit(solution)/shard_map/ppermute | solution.py:495
  13.6 5.1 %all-to-all-start = ((s16[8,128,128]{2,1,0:T(8,128)(2,1)}), s16[8,128,128]{2,1,0:T(8,128)(2,1)S(1)}, u32[]{:S(2)}, u32[]{:S(2)}) async-start(s16[8,128,128]{2,1,0:T(8,128)(2,1)} %shard_map.111.other_ref), calls=%async_computation | async-start | bytes 524288 | tf_op jit(solution)/shard_map/all_to_all | solution.py:30
  18.7 7.2 %collective-permute-done.1 = bf16[128,768]{1,0:T(8,128)(2,1)S(1)} collective-permute-done((bf16[128,768]{1,0:T(8,128)(2,1)S(1)}, bf16[128,768]{1,0:T(8,128)(2,1)S(1)}, u32[]{:S(2)}, u32[]{:S(2)}) %collective-permute-start.1) | collective-permute-done | bytes 196640 | tf_op jit(solution)/shard_map/ppermute | solution.py:495
  26.0 0.8 pad_maximum_fusion.1
  26.7 2.0 %collective-permute-start.2 = (bf16[2,128,768]{2,1,0:T(8,128)(2,1)}, bf16[2,128,768]{2,1,0:T(8,128)(2,1)}, u32[]{:S(2)}, u32[]{:S(2)}) collective-permute-start(bf16[2,128,768]{2,1,0:T(8,128)(2,1)} %pad_maximum_fusion.1), channel_id=1, source_target_pairs={{0,2},{2,0},{4,6},{6,4},{1,3},{3,1},{5,7},{7,5},{8,10},{10,8},{12,... | collective-permute-start | bytes 1179656 | tf_op jit(solution)/shard_map/ppermute | solution.py:497
  28.7 0.0 all-to-all-done.cq_ref
  28.7 0.0 collective-permute-done.came_ref
  28.7 1.9 %shard_map.113 = (s16[2048,128]{1,0:T(8,128)(2,1)}, f32[48,128]{1,0:T(8,128)S(1)}) custom-call(s32[1]{0:T(128)} %bitcast.2.place_ref, s32[1]{0:T(128)} %bitcast.1.core_ref, s16[8,128,128]{2,1,0:T(8,128)(2,1)S(1)} %all-to-all-done.cq_ref, bf16[128,768]{1,0:T(8,128)(2,1)S(1)} %copy-done.10, f32[64,128]{1,0:T(8,128)S(1)} %bitcast.33, ...), custom_call_target="tpu_custom_call" | custom-call | flops 37748736 | bytes 6000000 | tf_op jit(solution)/shard_map/pallas_call | solution.py:185
  30.7 21.8 %all-to-all-start.1 = ((s16[256,8,128]{2,1,0:T(8,128)(2,1)}), s16[256,8,128]{2,1,0:T(8,128)(2,1)}, u32[]{:S(2)}, u32[]{:S(2)}) async-start(s16[256,8,128]{2,1,0:T(8,128)(2,1)} %bitcast.9), calls=%async_computation.1 | async-start | bytes 1048576 | tf_op jit(solution)/shard_map/all_to_all | solution.py:30
  52.5 0.0 collective-permute-done.2
  52.5 1.1 pad_maximum_fusion.own_ref
  53.6 1.9 %collective-permute-start.3 = (bf16[4,128,768]{2,1,0:T(8,128)(2,1)S(1)}, bf16[4,128,768]{2,1,0:T(8,128)(2,1)S(1)}, u32[]{:S(2)}, u32[]{:S(2)}) collective-permute-start(bf16[4,128,768]{2,1,0:T(8,128)(2,1)S(1)} %pad_maximum_fusion.own_ref), channel_id=1, source_target_pairs={{0,1},{1,0},{2,3},{3,2},{4,5},{5,4},{6,7},{7,6},{8,9},{9,8},{10,11... | collective-permute-start | bytes 2359304 | tf_op jit(solution)/shard_map/ppermute | solution.py:34
  55.5 0.0 copy-start.2
  55.5 0.9 copy-done.2
  56.4 0.1 pad_add_fusion.1.at_ref
  56.5 0.1 reshape.48
  56.6 1.2 collective-permute-done.3.other_ref
  57.8 0.9 copy-done.8
  58.7 1.4 copy-done.1
  60.1 1.1 copy-done.3
  61.2 1.1 copy-done.9
  62.3 2.9 %shard_map.114.grad_ref = bf16[6144,256]{1,0:T(8,128)(2,1)S(1)} custom-call(s32[2]{0:T(128)S(1)} %pad_add_fusion.1.at_ref, bf16[4,128,768]{2,1,0:T(8,128)(2,1)S(1)} %copy-done.3, bf16[4,128,768]{2,1,0:T(8,128)(2,1)S(1)} %copy-done.9, bf16[128,128]{1,0:T(8,128)(2,1)S(1)} %copy-done.12, bf16[6144,128]{1,0:T(8,128)(2,1)S(1)} %bitcast.27), custom_call_target="tpu_custom_call" | custom-call | flops 201326592 | bytes 6291456 | tf_op jit(solution)/shard_map/pallas_call | solution.py:256
  65.3 6.8 %all-to-all-done.1 = s16[256,8,128]{2,1,0:T(8,128)(2,1)} async-done(((s16[256,8,128]{2,1,0:T(8,128)(2,1)}), s16[256,8,128]{2,1,0:T(8,128)(2,1)}, u32[]{:S(2)}, u32[]{:S(2)}) %all-to-all-start.1) | async-done | bytes 524320 | tf_op jit(solution)/shard_map/all_to_all | solution.py:30
  72.0 2.0 %shard_map.115 = s16[2048,128]{1,0:T(8,128)(2,1)S(1)} custom-call(s16[2048,128]{1,0:T(8,128)(2,1)} %bitcast.10.in_ref, bf16[6144,256]{1,0:T(8,128)(2,1)S(1)} %shard_map.114.grad_ref, f32[8,8,128]{2,1,0:T(8,128)S(1)} %pad.4.expert_ref), custom_call_target="tpu_custom_call" | custom-call | flops 1000000 | bytes 1500000 | tf_op jit(solution)/shard_map/pallas_call | solution.py:228
  74.1 32.3 %all_to_all.25 = s16[256,8,128]{2,1,0:T(8,128)(2,1)} all-to-all(s16[256,8,128]{2,1,0:T(8,128)(2,1)S(1)} %bitcast.28), channel_id=1, replica_groups=mesh['x'=4,'y'=8,'h'=2,'l'=4,'c'=2] {'x','y','h','l'}, dimensions={0} | all-to-all | bytes 1048576 | tf_op jit(solution)/shard_map/all_to_all | solution.py:30
  106.4 2.1 %collective-permute-start.4 = (s16[2048,128]{1,0:T(8,128)(2,1)}, s16[2048,128]{1,0:T(8,128)(2,1)}, u32[]{:S(2)}, u32[]{:S(2)}) collective-permute-start(s16[2048,128]{1,0:T(8,128)(2,1)} %bitcast.16.codes_ref), channel_id=1, source_target_pairs={{0,1},{1,0},{2,3},{3,2},{4,5},{5,4},{6,7},{7,6},{8,9},{9,8},{10,11... | collective-permute-start | bytes 1572872 | tf_op jit(solution)/shard_map/ppermute | solution.py:34
  108.5 2.1 %shard_map.116 = (f32[64,128]{1,0:T(8,128)S(1)}, f32[64,64]{1,0:T(8,128)S(1)}, bf16[12,128,256]{2,1,0:T(8,128)(2,1)S(1)}) custom-call(s32[1]{0:T(128)} %bitcast.1.core_ref, s16[2048,128]{1,0:T(8,128)(2,1)} %bitcast.16.codes_ref, bf16[6144,256]{1,0:T(8,128)(2,1)S(1)} %shard_map.114.grad_ref), custom_call_target="tpu_custom_call" | custom-call | flops 201326592 | bytes 3000000 | tf_op jit(solution)/shard_map/pallas_call | solution.py:349
  110.6 0.0 copy-start.4
  110.7 3.1 %shard_map.117 = (s16[8,80,128]{2,1,0:T(8,128)(2,1)}, f32[64,64]{1,0:T(8,128)S(1)}, bf16[12,128,256]{2,1,0:T(8,128)(2,1)S(1)}) custom-call(s32[1]{0:T(128)} %bitcast.1.core_ref, s16[2048,128]{1,0:T(8,128)(2,1)} %collective-permute-done.4.codes_ref, bf16[6144,256]{1,0:T(8,128)(2,1)S(1)} %shard_map.114.grad_ref, f32[64,128]{1,0:T(8,128)S(1)} %get-tuple-element.22.mine_ref, ...), custom_call_target="tpu_custom_call" | custom-call | flops 201326592 | bytes 3000000 | tf_op jit(solution)/shard_map/pallas_call | solution.py:360
  113.8 0.9 copy-done.6
  114.6 3.8 %all-to-all-start.3 = ((s16[8,80,128]{2,1,0:T(8,128)(2,1)}), s16[8,80,128]{2,1,0:T(8,128)(2,1)S(1)}, u32[]{:S(2)}, u32[]{:S(2)}) async-start(s16[8,80,128]{2,1,0:T(8,128)(2,1)} %get-tuple-element.25), calls=%async_computation.3 | async-start | bytes 327680 | tf_op jit(solution)/shard_map/all_to_all | solution.py:30
  118.4 0.1 pad_add_fusion.at_ref
  118.5 5.8 %cholesky.17 = f32[64,64]{1,0:T(8,128)S(1)} custom-call(f32[64,64]{1,0:T(8,128)S(1)} %get-tuple-element.24), custom_call_target="Cholesky" | custom-call | tf_op jit(solution)/shard_map/jit(cholesky)/cholesky | solution.py:511
  124.4 0.6 compare_reduce_fusion
  125.0 3.8 %all-to-all-done.3.in_ref = s16[8,80,128]{2,1,0:T(8,128)(2,1)S(1)} async-done(((s16[8,80,128]{2,1,0:T(8,128)(2,1)}), s16[8,80,128]{2,1,0:T(8,128)(2,1)S(1)}, u32[]{:S(2)}, u32[]{:S(2)}) %all-to-all-start.3) | async-done | bytes 163872 | tf_op jit(solution)/shard_map/all_to_all | solution.py:30
  128.8 1.0 shard_map.118
  129.8 5.1 %all-to-all-start.4 = ((s16[8,80,128]{2,1,0:T(8,128)(2,1)}), s16[8,80,128]{2,1,0:T(8,128)(2,1)S(1)}, u32[]{:S(2)}, u32[]{:S(2)}) async-start(s16[8,80,128]{2,1,0:T(8,128)(2,1)} %shard_map.118), calls=%async_computation.4 | async-start | bytes 327680 | tf_op jit(solution)/shard_map/all_to_all | solution.py:30
  134.9 0.7 fusion
  135.6 4.9 %custom-call.6 = f32[1,64,64]{1,2,0:T(8,128)S(1)} custom-call(f32[1,64,64]{2,1,0:T(8,128)S(1)} %fusion), custom_call_target="InvertDiagBlocksLowerTriangular" | custom-call | tf_op jit(solution)/shard_map/triangular_solve | solution.py:512
  140.5 0.2 fusion.1.inverse_ref
  140.7 6.5 %all-to-all-done.4.sums_ref = s16[8,80,128]{2,1,0:T(8,128)(2,1)S(1)} async-done(((s16[8,80,128]{2,1,0:T(8,128)(2,1)}), s16[8,80,128]{2,1,0:T(8,128)(2,1)S(1)}, u32[]{:S(2)}, u32[]{:S(2)}) %all-to-all-start.4) | async-done | bytes 163872 | tf_op jit(solution)/shard_map/all_to_all | solution.py:30
  147.2 1.1 copy-done.5
  148.4 1.1 copy-done.7
  149.5 3.2 %shard_map.119 = (bf16[96,128]{1,0:T(8,128)(2,1)}, f32[64,128]{1,0:T(8,128)}, bf16[6144,128]{1,0:T(8,128)(2,1)}, f32[1,96]{1,0:T(1,128)}) custom-call(s32[2]{0:T(128)S(1)} %pad_add_fusion.at_ref, f32[64,64]{1,0:T(8,128)S(1)} %fusion.1.inverse_ref, s16[8,80,128]{2,1,0:T(8,128)(2,1)S(1)} %all-to-all-done.4.sums_ref, bf16[12,128,256]{2,1,0:T(8,128)(2,1)S(1)} %copy-done.5, ...), custom_call_target="tpu_custom_call" | custom-call | tf_op jit(solution)/shard_map/pallas_call | solution.py:421
  (19 shorter events, 0.1 us)
Async XLA Ops:
  0.6 2.9 %copy-start.11 = (f32[128,64]{0,1:T(8,128)S(1)}, f32[128,64]{0,1:T(8,128)}, u32[]{:S(2)}) copy-start(f32[128,64]{0,1:T(8,128)} %param.11) | copy-start | bytes 98308
  0.6 2.8 %copy-start.10 = (bf16[128,768]{1,0:T(8,128)(2,1)S(1)}, bf16[128,768]{1,0:T(8,128)(2,1)}, u32[]{:S(2)}) copy-start(bf16[128,768]{1,0:T(8,128)(2,1)} %attn_ref.3) | copy-start | bytes 589828
  0.7 2.8 %copy-start = (bf16[1,6144,128]{2,1,0:T(8,128)(2,1)S(1)}, bf16[1,6144,128]{2,1,0:T(8,128)(2,1)}, u32[]{:S(2)}) copy-start(bf16[1,6144,128]{2,1,0:T(8,128)(2,1)} %param.10) | copy-start | bytes 4718596
  5.6 23.1 %collective-permute-start = (f32[64,3072]{1,0:T(8,128)}, f32[64,3072]{1,0:T(8,128)S(1)}, u32[]{:S(2)}, u32[]{:S(2)}) collective-permute-start(f32[64,3072]{1,0:T(8,128)} %get-tuple-element.18), channel_id=1, source_target_pairs={{0,1},{1,0},{2,3},{3,2},{4,5},{5,4},{6,7},{7,6},{8,9},{9,8},{10,11... | collective-permute-start | bytes 2359304 | tf_op jit(solution)/shard_map/ppermute | solution.py:34
  7.5 18.4 %collective-permute-start.1 = (bf16[128,768]{1,0:T(8,128)(2,1)S(1)}, bf16[128,768]{1,0:T(8,128)(2,1)S(1)}, u32[]{:S(2)}, u32[]{:S(2)}) collective-permute-start(bf16[128,768]{1,0:T(8,128)(2,1)S(1)} %get-tuple-element.20), channel_id=1, source_target_pairs={{0,4},{2,6},{4,0},{6,2},{1,5},{3,7},{5,1},{7,3},{8,12},{10,14},{12... | collective-permute-start | bytes 589832 | tf_op jit(solution)/shard_map/ppermute | solution.py:495
  13.6 15.1 %all-to-all-start = ((s16[8,128,128]{2,1,0:T(8,128)(2,1)}), s16[8,128,128]{2,1,0:T(8,128)(2,1)S(1)}, u32[]{:S(2)}, u32[]{:S(2)}) async-start(s16[8,128,128]{2,1,0:T(8,128)(2,1)} %shard_map.111.other_ref), calls=%async_computation | async-start | bytes 524288 | tf_op jit(solution)/shard_map/all_to_all | solution.py:30
  26.7 25.8 %collective-permute-start.2 = (bf16[2,128,768]{2,1,0:T(8,128)(2,1)}, bf16[2,128,768]{2,1,0:T(8,128)(2,1)}, u32[]{:S(2)}, u32[]{:S(2)}) collective-permute-start(bf16[2,128,768]{2,1,0:T(8,128)(2,1)} %pad_maximum_fusion.1), channel_id=1, source_target_pairs={{0,2},{2,0},{4,6},{6,4},{1,3},{3,1},{5,7},{7,5},{8,10},{10,8},{12,... | collective-permute-start | bytes 1179656 | tf_op jit(solution)/shard_map/ppermute | solution.py:497
  30.7 28.0 %copy-start.12 = (bf16[128,128]{1,0:T(8,128)(2,1)S(1)}, bf16[128,128]{1,0:T(8,128)(2,1)}, u32[]{:S(2)}) copy-start(bf16[128,128]{1,0:T(8,128)(2,1)} %cols_ref.3) | copy-start | bytes 98308
  30.7 41.4 %all-to-all-start.1 = ((s16[256,8,128]{2,1,0:T(8,128)(2,1)}), s16[256,8,128]{2,1,0:T(8,128)(2,1)}, u32[]{:S(2)}, u32[]{:S(2)}) async-start(s16[256,8,128]{2,1,0:T(8,128)(2,1)} %bitcast.9), calls=%async_computation.1 | async-start | bytes 1048576 | tf_op jit(solution)/shard_map/all_to_all | solution.py:30
  53.6 4.2 %collective-permute-start.3 = (bf16[4,128,768]{2,1,0:T(8,128)(2,1)S(1)}, bf16[4,128,768]{2,1,0:T(8,128)(2,1)S(1)}, u32[]{:S(2)}, u32[]{:S(2)}) collective-permute-start(bf16[4,128,768]{2,1,0:T(8,128)(2,1)S(1)} %pad_maximum_fusion.own_ref), channel_id=1, source_target_pairs={{0,1},{1,0},{2,3},{3,2},{4,5},{5,4},{6,7},{7,6},{8,9},{9,8},{10,11... | collective-permute-start | bytes 2359304 | tf_op jit(solution)/shard_map/ppermute | solution.py:34
  55.5 0.9 copy-start.2
  57.8 0.9 copy-start.8
  58.7 1.4 copy-start.1
  60.1 1.1 copy-start.3
  61.2 1.1 copy-start.9
  106.4 4.2 %collective-permute-start.4 = (s16[2048,128]{1,0:T(8,128)(2,1)}, s16[2048,128]{1,0:T(8,128)(2,1)}, u32[]{:S(2)}, u32[]{:S(2)}) collective-permute-start(s16[2048,128]{1,0:T(8,128)(2,1)} %bitcast.16.codes_ref), channel_id=1, source_target_pairs={{0,1},{1,0},{2,3},{3,2},{4,5},{5,4},{6,7},{7,6},{8,9},{9,8},{10,11... | collective-permute-start | bytes 1572872 | tf_op jit(solution)/shard_map/ppermute | solution.py:34
  110.6 3.1 %copy-start.4 = (bf16[12,128,256]{2,1,0:T(8,128)(2,1)}, bf16[12,128,256]{2,1,0:T(8,128)(2,1)S(1)}, u32[]{:S(2)}) copy-start(bf16[12,128,256]{2,1,0:T(8,128)(2,1)S(1)} %get-tuple-element.26.mine_ref) | copy-start | bytes 2359300
  113.8 0.9 copy-start.6
  114.6 14.2 %all-to-all-start.3 = ((s16[8,80,128]{2,1,0:T(8,128)(2,1)}), s16[8,80,128]{2,1,0:T(8,128)(2,1)S(1)}, u32[]{:S(2)}, u32[]{:S(2)}) async-start(s16[8,80,128]{2,1,0:T(8,128)(2,1)} %get-tuple-element.25), calls=%async_computation.3 | async-start | bytes 327680 | tf_op jit(solution)/shard_map/all_to_all | solution.py:30
  129.8 17.4 %all-to-all-start.4 = ((s16[8,80,128]{2,1,0:T(8,128)(2,1)}), s16[8,80,128]{2,1,0:T(8,128)(2,1)S(1)}, u32[]{:S(2)}, u32[]{:S(2)}) async-start(s16[8,80,128]{2,1,0:T(8,128)(2,1)} %shard_map.118), calls=%async_computation.4 | async-start | bytes 327680 | tf_op jit(solution)/shard_map/all_to_all | solution.py:30
  147.2 1.1 copy-start.5
  148.4 1.1 copy-start.7

commit v10 on v7

--- a/solution.py
+++ b/solution.py
@@ -356,6 +356,21 @@
     )(core.reshape(1), codes, grad, raw, square, by_y)
 
 
+def after_kernel(in_ref, other_ref, out_ref):
+    del in_ref, other_ref, out_ref
+
+
+def after(values, other):
+    return pl.pallas_call(
+        after_kernel,
+        in_specs=[ANY, ANY],
+        out_specs=ANY,
+        out_shape=jax.ShapeDtypeStruct(values.shape, values.dtype),
+        input_output_aliases={0: 0},
+        compiler_params=pltpu.CompilerParams(vmem_limit_bytes=1024 * 1024),
+    )(values, other)
+
+
 def pass_kernel(in_ref, out_ref):
     raw, rows = collected(in_ref)
     codes, scales = packed(raw)
@@ -489,9 +504,11 @@
     codes, experts = share_of(place, cq_all, attn_out, kept, came)
     by_y = experts.reshape(4, 8, 2, 96).transpose(1, 0, 2, 3).reshape(8, 8, 96)
     by_y = jnp.pad(by_y, ((0, 0), (0, 0), (0, 32)))
-    grad = grad_of(place, core, own, swap_cores(own), out_cols, error)
-    piece = summed(exchange(codes.reshape(256, 8, 128), FLAT).reshape(2048, 128), grad, by_y)
+    beside = swap_cores(own)
+    piece = summed(exchange(codes.reshape(256, 8, 128), FLAT).reshape(2048, 128), beside, by_y)
+    grad = grad_of(place, core, own, beside, out_cols, error)
     mine = exchange(piece.reshape(256, 8, 128), FLAT).reshape(2048, 128)
+    mine = after(mine, grad)
     other = swap_cores(mine)
     raw, square, p_mine = mine_of(core, mine, grad)
     send, gram, p_other = other_of(core, other, grad, raw, square, by_y)

time: 151 us -> 148 us (0.980)
  blocking collectives: 31.8 us -> 0 us
  waiting for transfers between devices: 18.8 us -> 39.8 us
  starting transfers between devices: 52.7 us -> 61.9 us
    all_to_all x1 -> x0, blocking collectives: 31.8 us -> none  [exchange(): return lax.all_to_all(values, axes, split_axis=0, concat_axis=0, tiled=True)]
    all_to_all x4 -> x5, waiting for transfers between devices: 17.7 us -> 37.6 us  [exchange(): return lax.all_to_all(values, axes, split_axis=0, concat_axis=0, tiled=True)]
    all_to_all x4 -> x5, starting transfers between devices: 35.8 us -> 44.8 us  [exchange(): return lax.all_to_all(values, axes, split_axis=0, concat_axis=0, tiled=True)]
  transfers between devices with their start and end apart: 10 -> 11, of which waited for: 4 -> 5; matrix products, arithmetic and copies ran while one was open for 8% -> 9% of each run, Pallas kernels for 5% -> 5%
where the time goes in v10:
time: 148 us; the launch traced here: 147 us
  starting transfers between devices  61.9 us (42%)
  waiting for transfers between devices  39.8 us (27%)
  Pallas kernels  22.2 us (15%)
  other arithmetic  12.3 us (8%)
  local copies, waits for them, and re-layouts  9.87 us (7%)
    all_to_all x5, starting transfers between devices, exchange(): return lax.all_to_all(values, axes, split_axis=0, concat_axis=0, tiled=True)  44.8 us
    all_to_all x5, waiting for transfers between devices, exchange(): return lax.all_to_all(values, axes, split_axis=0, concat_axis=0, tiled=True)  37.6 us
    ppermute x3, starting transfers between devices, local(): lax.ppermute(attn_here, 'l', [(i, (i + k) % 4) for i in range(4)])  11 us
    unnamed x30, local copies, waits for them, and re-layouts  9.76 us
    another operation x3, other arithmetic, local(): factor = jnp.linalg.cholesky(gram, symmetrize_input=False)  6.52 us
    ppermute x3, starting transfers between devices, swap_cores(): return lax.ppermute(values, 'c', [(0, 1), (1, 0)])  6.05 us
    another operation x2, other arithmetic, local(): lax.linalg.triangular_solve(factor, jnp.eye(RANK, dtype=F32), left_side=T...  5.55 us
    pallas_call x2, Pallas kernels, error_share(): pl.pallas_call(error_kernel, grid_spec=pltpu.PrefetchScalarGridSpec(num_s...  3.19 us
  transfers between devices with their start and end apart: 11, of which 5 were waited for; matrix products, arithmetic and copies ran while one was open for 9% of the time, Pallas kernels for 5%

profile of v10, /device:TPU:64, one launch (start us, length us, event | category | flops | bytes accessed | tf_op | source)
XLA Modules:
  0.0 147.3 jit_solution(7439850619028463612)
XLA Ops:
  0.7 0.0 copy-start
  0.7 2.8 %shard_map.111.other_ref = s16[8,128,128]{2,1,0:T(8,128)(2,1)} custom-call(f32[64,128]{1,0:T(8,128)} %bitcast.31, bf16[128,128]{1,0:T(8,128)(2,1)} %cols_ref.3, bf16[128,6144]{1,0:T(8,128)(2,1)} %tokens_ref.1, s32[2,128]{1,0:T(2,128)} %bitcast.39, f32[2,128]{1,0:T(2,128)} %bitcast.40, f32[2,128]{1,0:T(2,128)} %bitcast.41), custom_call_target="tpu_custom_call" | custom-call | tf_op jit(solution)/shard_map/pallas_call | solution.py:469
  3.5 2.1 %shard_map.112 = (f32[64,3072]{1,0:T(8,128)}, bf16[128,768]{1,0:T(8,128)(2,1)S(1)}) custom-call(s32[1]{0:T(128)} %bitcast.8.block_ref, f32[64,128]{1,0:T(8,128)S(1)} %bitcast.32, bf16[6144,128]{1,0:T(8,128)(2,1)S(1)} %bitcast.27, bf16[128,768]{1,0:T(8,128)(2,1)S(1)} %copy-done.10, s16[8,128,128]{2,1,0:T(8,128)(2,1)} %shard_map.111.other_ref), custom_call_target="tpu_custom_call" | custom-call | flops 150994944 | bytes 1572864 | tf_op jit(solution)/shard_map/pallas_call | solution.py:115
  5.6 1.9 %collective-permute-start = (f32[64,3072]{1,0:T(8,128)}, f32[64,3072]{1,0:T(8,128)S(1)}, u32[]{:S(2)}, u32[]{:S(2)}) collective-permute-start(f32[64,3072]{1,0:T(8,128)} %get-tuple-element.22), channel_id=1, source_target_pairs={{0,1},{1,0},{2,3},{3,2},{4,5},{5,4},{6,7},{7,6},{8,9},{9,8},{10,11... | collective-permute-start | bytes 2359304 | tf_op jit(solution)/shard_map/ppermute | solution.py:34
  7.6 8.4 %all-to-all-start = ((s16[8,128,128]{2,1,0:T(8,128)(2,1)}), s16[8,128,128]{2,1,0:T(8,128)(2,1)S(1)}, u32[]{:S(2)}, u32[]{:S(2)}) async-start(s16[8,128,128]{2,1,0:T(8,128)(2,1)} %shard_map.111.other_ref), calls=%async_computation | async-start | bytes 524288 | tf_op jit(solution)/shard_map/all_to_all | solution.py:30
  15.9 1.1 shard_map.113
  17.0 0.9 copy-done.11
  17.9 2.0 %collective-permute-start.3 = (bf16[128,768]{1,0:T(8,128)(2,1)S(1)}, bf16[128,768]{1,0:T(8,128)(2,1)S(1)}, u32[]{:S(2)}, u32[]{:S(2)}) collective-permute-start(bf16[128,768]{1,0:T(8,128)(2,1)S(1)} %get-tuple-element.24), channel_id=1, source_target_pairs={{0,6},{2,0},{4,2},{6,4},{1,7},{3,1},{5,3},{7,5},{8,14},{10,8},{12,... | collective-permute-start | bytes 589832 | tf_op jit(solution)/shard_map/ppermute | solution.py:501
  19.9 4.7 %collective-permute-start.2 = (bf16[128,768]{1,0:T(8,128)(2,1)S(1)}, bf16[128,768]{1,0:T(8,128)(2,1)S(1)}, u32[]{:S(2)}, u32[]{:S(2)}) collective-permute-start(bf16[128,768]{1,0:T(8,128)(2,1)S(1)} %get-tuple-element.24), channel_id=1, source_target_pairs={{0,4},{2,6},{4,0},{6,2},{1,5},{3,7},{5,1},{7,3},{8,12},{10,14},{12... | collective-permute-start | bytes 589832 | tf_op jit(solution)/shard_map/ppermute | solution.py:501
  24.6 4.3 %collective-permute-start.1 = (bf16[128,768]{1,0:T(8,128)(2,1)S(1)}, bf16[128,768]{1,0:T(8,128)(2,1)S(1)}, u32[]{:S(2)}, u32[]{:S(2)}) collective-permute-start(bf16[128,768]{1,0:T(8,128)(2,1)S(1)} %get-tuple-element.24), channel_id=1, source_target_pairs={{0,2},{2,4},{4,6},{6,0},{1,3},{3,5},{5,7},{7,1},{8,10},{10,12},{12... | collective-permute-start | bytes 589832 | tf_op jit(solution)/shard_map/ppermute | solution.py:501
  29.0 1.1 copy-done.12
  30.1 1.7 %shard_map.114 = (s16[2048,128]{1,0:T(8,128)(2,1)}, f32[48,128]{1,0:T(8,128)S(1)}) custom-call(s32[1]{0:T(128)} %bitcast.2.place_ref, s16[8,128,128]{2,1,0:T(8,128)(2,1)S(1)} %all-to-all-done.cq_ref, bf16[128,768]{1,0:T(8,128)(2,1)S(1)} %copy-done.10, f32[64,3072]{1,0:T(8,128)S(1)} %copy-done.12, f32[64,3072]{1,0:T(8,128)S(1)} %collective-permute-done.came_ref), custom_call_target="tpu_custom_call" | custom-call | flops 37748736 | bytes 6000000 | tf_op jit(solution)/shard_map/pallas_call | solution.py:175
  31.7 17.4 %all-to-all-start.1 = ((s16[256,8,128]{2,1,0:T(8,128)(2,1)}), s16[256,8,128]{2,1,0:T(8,128)(2,1)S(1)}, u32[]{:S(2)}, u32[]{:S(2)}) async-start(s16[256,8,128]{2,1,0:T(8,128)(2,1)} %bitcast.9), calls=%async_computation.1 | async-start | bytes 1048576 | tf_op jit(solution)/shard_map/all_to_all | solution.py:30
  49.2 0.1 pad_maximum_fusion.own_ref
  49.3 0.0 copy-start.4
  49.3 0.0 copy-start.14
  49.3 2.1 %collective-permute-start.4 = (bf16[4,128,768]{2,1,0:T(8,128)(2,1)S(1)}, bf16[4,128,768]{2,1,0:T(8,128)(2,1)S(1)}, u32[]{:S(2)}, u32[]{:S(2)}) collective-permute-start(bf16[4,128,768]{2,1,0:T(8,128)(2,1)S(1)} %pad_maximum_fusion.own_ref), channel_id=1, source_target_pairs={{0,1},{1,0},{2,3},{3,2},{4,5},{5,4},{6,7},{7,6},{8,9},{9,8},{10,11... | collective-permute-start | bytes 2359304 | tf_op jit(solution)/shard_map/ppermute | solution.py:34
  51.3 0.1 reshape.48
  51.5 2.1 %collective-permute-done.4.grad_ref.other_ref = bf16[4,128,768]{2,1,0:T(8,128)(2,1)S(1)} collective-permute-done((bf16[4,128,768]{2,1,0:T(8,128)(2,1)S(1)}, bf16[4,128,768]{2,1,0:T(8,128)(2,1)S(1)}, u32[]{:S(2)}, u32[]{:S(2)}) %collective-permute-start.4) | collective-permute-done | bytes 786464 | tf_op jit(solution)/shard_map/ppermute | solution.py:34
  53.6 15.5 %all-to-all-done.1 = s16[256,8,128]{2,1,0:T(8,128)(2,1)S(1)} async-done(((s16[256,8,128]{2,1,0:T(8,128)(2,1)}), s16[256,8,128]{2,1,0:T(8,128)(2,1)S(1)}, u32[]{:S(2)}, u32[]{:S(2)}) %all-to-all-start.1) | async-done | bytes 524320 | tf_op jit(solution)/shard_map/all_to_all | solution.py:30
  69.1 2.6 %shard_map.115 = s16[2048,128]{1,0:T(8,128)(2,1)} custom-call(s16[2048,128]{1,0:T(8,128)(2,1)S(1)} %bitcast.30, bf16[4,128,768]{2,1,0:T(8,128)(2,1)S(1)} %collective-permute-done.4.grad_ref.other_ref, f32[8,8,128]{2,1,0:T(8,128)S(1)} %pad.4.expert_ref), custom_call_target="tpu_custom_call" | custom-call | flops 1000000 | bytes 1500000 | tf_op jit(solution)/shard_map/pallas_call | solution.py:218
  71.7 10.2 %all-to-all-start.2 = ((s16[256,8,128]{2,1,0:T(8,128)(2,1)}), s16[256,8,128]{2,1,0:T(8,128)(2,1)}, u32[]{:S(2)}, u32[]{:S(2)}) async-start(s16[256,8,128]{2,1,0:T(8,128)(2,1)} %bitcast.17), calls=%async_computation.2 | async-start | bytes 1048576 | tf_op jit(solution)/shard_map/all_to_all | solution.py:30
  82.0 0.1 pad_add_fusion.1.at_ref
  82.1 1.4 copy-done.1
  83.5 1.1 copy-done.3
  84.6 1.1 copy-done.5
  85.7 2.9 %shard_map.116.other_ref.grad_ref = bf16[6144,256]{1,0:T(8,128)(2,1)S(1)} custom-call(s32[2]{0:T(128)S(1)} %pad_add_fusion.1.at_ref, bf16[4,128,768]{2,1,0:T(8,128)(2,1)S(1)} %copy-done.5, bf16[4,128,768]{2,1,0:T(8,128)(2,1)S(1)} %copy-done.3, bf16[128,128]{1,0:T(8,128)(2,1)S(1)} %copy-done.14, bf16[6144,128]{1,0:T(8,128)(2,1)S(1)} %bitcast.29), custom_call_target="tpu_custom_call" | custom-call | flops 201326592 | bytes 6291456 | tf_op jit(solution)/shard_map/pallas_call | solution.py:245
  88.7 11.8 %all-to-all-done.2 = s16[256,8,128]{2,1,0:T(8,128)(2,1)} async-done(((s16[256,8,128]{2,1,0:T(8,128)(2,1)}), s16[256,8,128]{2,1,0:T(8,128)(2,1)}, u32[]{:S(2)}, u32[]{:S(2)}) %all-to-all-start.2) | async-done | bytes 524320 | tf_op jit(solution)/shard_map/all_to_all | solution.py:30
  100.4 2.1 %collective-permute-start.5 = (s16[2048,128]{1,0:T(8,128)(2,1)}, s16[2048,128]{1,0:T(8,128)(2,1)}, u32[]{:S(2)}, u32[]{:S(2)}) collective-permute-start(s16[2048,128]{1,0:T(8,128)(2,1)} %shard_map.117.codes_ref), channel_id=1, source_target_pairs={{0,1},{1,0},{2,3},{3,2},{4,5},{5,4},{6,7},{7,6},{8,9},{9,8},{10,11... | collective-permute-start | bytes 1572872 | tf_op jit(solution)/shard_map/ppermute | solution.py:34
  102.5 2.1 %shard_map.118 = (f32[64,128]{1,0:T(8,128)S(1)}, f32[64,64]{1,0:T(8,128)S(1)}, bf16[12,128,256]{2,1,0:T(8,128)(2,1)S(1)}) custom-call(s32[1]{0:T(128)} %bitcast.1.block_ref.core_ref, s16[2048,128]{1,0:T(8,128)(2,1)} %shard_map.117.codes_ref, bf16[6144,256]{1,0:T(8,128)(2,1)S(1)} %shard_map.116.other_ref.grad_ref), custom_call_target="tpu_custom_call" | custom-call | flops 201326592 | bytes 3000000 | tf_op jit(solution)/shard_map/pallas_call | solution.py:338
  104.7 0.0 copy-start.6
  104.7 0.9 copy-done.6
  105.5 2.8 %shard_map.119 = (s16[8,80,128]{2,1,0:T(8,128)(2,1)}, f32[64,64]{1,0:T(8,128)S(1)}, bf16[12,128,256]{2,1,0:T(8,128)(2,1)S(1)}) custom-call(s32[1]{0:T(128)} %bitcast.1.block_ref.core_ref, s16[2048,128]{1,0:T(8,128)(2,1)} %collective-permute-done.5.codes_ref, bf16[6144,256]{1,0:T(8,128)(2,1)S(1)} %shard_map.116.other_ref.grad_ref, ...), custom_call_target="tpu_custom_call" | custom-call | flops 201326592 | bytes 3000000 | tf_op jit(solution)/shard_map/pallas_call | solution.py:349
  108.4 0.9 copy-done.8
  109.3 3.7 %all-to-all-start.3 = ((s16[8,80,128]{2,1,0:T(8,128)(2,1)}), s16[8,80,128]{2,1,0:T(8,128)(2,1)S(1)}, u32[]{:S(2)}, u32[]{:S(2)}) async-start(s16[8,80,128]{2,1,0:T(8,128)(2,1)} %get-tuple-element.29), calls=%async_computation.3 | async-start | bytes 327680 | tf_op jit(solution)/shard_map/all_to_all | solution.py:30
  113.0 0.1 pad_add_fusion.at_ref
  113.1 5.8 %cholesky.17 = f32[64,64]{1,0:T(8,128)S(1)} custom-call(f32[64,64]{1,0:T(8,128)S(1)} %get-tuple-element.28), custom_call_target="Cholesky" | custom-call | tf_op jit(solution)/shard_map/jit(cholesky)/cholesky | solution.py:518
  118.9 0.6 compare_reduce_fusion
  119.6 3.8 %all-to-all-done.3.in_ref = s16[8,80,128]{2,1,0:T(8,128)(2,1)S(1)} async-done(((s16[8,80,128]{2,1,0:T(8,128)(2,1)}), s16[8,80,128]{2,1,0:T(8,128)(2,1)S(1)}, u32[]{:S(2)}, u32[]{:S(2)}) %all-to-all-start.3) | async-done | bytes 163872 | tf_op jit(solution)/shard_map/all_to_all | solution.py:30
  123.4 1.0 shard_map.120
  124.4 5.1 %all-to-all-start.4 = ((s16[8,80,128]{2,1,0:T(8,128)(2,1)}), s16[8,80,128]{2,1,0:T(8,128)(2,1)S(1)}, u32[]{:S(2)}, u32[]{:S(2)}) async-start(s16[8,80,128]{2,1,0:T(8,128)(2,1)} %shard_map.120), calls=%async_computation.4 | async-start | bytes 327680 | tf_op jit(solution)/shard_map/all_to_all | solution.py:30
  129.5 0.7 fusion
  130.2 4.9 %custom-call.6 = f32[1,64,64]{1,2,0:T(8,128)S(1)} custom-call(f32[1,64,64]{2,1,0:T(8,128)S(1)} %fusion), custom_call_target="InvertDiagBlocksLowerTriangular" | custom-call | tf_op jit(solution)/shard_map/triangular_solve | solution.py:519
  135.1 0.2 fusion.1.inverse_ref
  135.3 6.5 %all-to-all-done.4.sums_ref = s16[8,80,128]{2,1,0:T(8,128)(2,1)S(1)} async-done(((s16[8,80,128]{2,1,0:T(8,128)(2,1)}), s16[8,80,128]{2,1,0:T(8,128)(2,1)S(1)}, u32[]{:S(2)}, u32[]{:S(2)}) %all-to-all-start.4) | async-done | bytes 163872 | tf_op jit(solution)/shard_map/all_to_all | solution.py:30
  141.8 1.1 copy-done.7
  143.0 1.1 copy-done.9
  144.1 3.2 %shard_map.121 = (bf16[96,128]{1,0:T(8,128)(2,1)}, f32[64,128]{1,0:T(8,128)}, bf16[6144,128]{1,0:T(8,128)(2,1)}, f32[1,96]{1,0:T(1,128)}) custom-call(s32[2]{0:T(128)S(1)} %pad_add_fusion.at_ref, f32[64,64]{1,0:T(8,128)S(1)} %fusion.1.inverse_ref, s16[8,80,128]{2,1,0:T(8,128)(2,1)S(1)} %all-to-all-done.4.sums_ref, bf16[12,128,256]{2,1,0:T(8,128)(2,1)S(1)} %copy-done.7, ...), custom_call_target="tpu_custom_call" | custom-call | tf_op jit(solution)/shard_map/pallas_call | solution.py:425
  (27 shorter events, 0.1 us)
Async XLA Ops:
  0.6 2.9 %copy-start.13 = (f32[128,64]{0,1:T(8,128)S(1)}, f32[128,64]{0,1:T(8,128)}, u32[]{:S(2)}) copy-start(f32[128,64]{0,1:T(8,128)} %param.11) | copy-start | bytes 98308
  0.6 2.9 %copy-start.10 = (bf16[128,768]{1,0:T(8,128)(2,1)S(1)}, bf16[128,768]{1,0:T(8,128)(2,1)}, u32[]{:S(2)}) copy-start(bf16[128,768]{1,0:T(8,128)(2,1)} %attn_ref.3) | copy-start | bytes 589828
  0.7 2.9 %copy-start = (bf16[1,6144,128]{2,1,0:T(8,128)(2,1)S(1)}, bf16[1,6144,128]{2,1,0:T(8,128)(2,1)}, u32[]{:S(2)}) copy-start(bf16[1,6144,128]{2,1,0:T(8,128)(2,1)} %param.10) | copy-start | bytes 4718596
  5.6 23.3 %collective-permute-start = (f32[64,3072]{1,0:T(8,128)}, f32[64,3072]{1,0:T(8,128)S(1)}, u32[]{:S(2)}, u32[]{:S(2)}) collective-permute-start(f32[64,3072]{1,0:T(8,128)} %get-tuple-element.22), channel_id=1, source_target_pairs={{0,1},{1,0},{2,3},{3,2},{4,5},{5,4},{6,7},{7,6},{8,9},{9,8},{10,11... | collective-permute-start | bytes 2359304 | tf_op jit(solution)/shard_map/ppermute | solution.py:34
  7.6 21.4 %all-to-all-start = ((s16[8,128,128]{2,1,0:T(8,128)(2,1)}), s16[8,128,128]{2,1,0:T(8,128)(2,1)S(1)}, u32[]{:S(2)}, u32[]{:S(2)}) async-start(s16[8,128,128]{2,1,0:T(8,128)(2,1)} %shard_map.111.other_ref), calls=%async_computation | async-start | bytes 524288 | tf_op jit(solution)/shard_map/all_to_all | solution.py:30
  17.0 0.9 copy-start.11
  17.9 31.3 %collective-permute-start.3 = (bf16[128,768]{1,0:T(8,128)(2,1)S(1)}, bf16[128,768]{1,0:T(8,128)(2,1)S(1)}, u32[]{:S(2)}, u32[]{:S(2)}) collective-permute-start(bf16[128,768]{1,0:T(8,128)(2,1)S(1)} %get-tuple-element.24), channel_id=1, source_target_pairs={{0,6},{2,0},{4,2},{6,4},{1,7},{3,1},{5,3},{7,5},{8,14},{10,8},{12,... | collective-permute-start | bytes 589832 | tf_op jit(solution)/shard_map/ppermute | solution.py:501
  19.9 29.2 %collective-permute-start.2 = (bf16[128,768]{1,0:T(8,128)(2,1)S(1)}, bf16[128,768]{1,0:T(8,128)(2,1)S(1)}, u32[]{:S(2)}, u32[]{:S(2)}) collective-permute-start(bf16[128,768]{1,0:T(8,128)(2,1)S(1)} %get-tuple-element.24), channel_id=1, source_target_pairs={{0,4},{2,6},{4,0},{6,2},{1,5},{3,7},{5,1},{7,3},{8,12},{10,14},{12... | collective-permute-start | bytes 589832 | tf_op jit(solution)/shard_map/ppermute | solution.py:501
  24.6 24.5 %collective-permute-start.1 = (bf16[128,768]{1,0:T(8,128)(2,1)S(1)}, bf16[128,768]{1,0:T(8,128)(2,1)S(1)}, u32[]{:S(2)}, u32[]{:S(2)}) collective-permute-start(bf16[128,768]{1,0:T(8,128)(2,1)S(1)} %get-tuple-element.24), channel_id=1, source_target_pairs={{0,2},{2,4},{4,6},{6,0},{1,3},{3,5},{5,7},{7,1},{8,10},{10,12},{12... | collective-permute-start | bytes 589832 | tf_op jit(solution)/shard_map/ppermute | solution.py:501
  28.9 1.1 copy-start.12
  31.7 37.4 %all-to-all-start.1 = ((s16[256,8,128]{2,1,0:T(8,128)(2,1)}), s16[256,8,128]{2,1,0:T(8,128)(2,1)S(1)}, u32[]{:S(2)}, u32[]{:S(2)}) async-start(s16[256,8,128]{2,1,0:T(8,128)(2,1)} %bitcast.9), calls=%async_computation.1 | async-start | bytes 1048576 | tf_op jit(solution)/shard_map/all_to_all | solution.py:30
  49.3 32.7 %copy-start.4 = (bf16[4,128,768]{2,1,0:T(8,128)(2,1)}, bf16[4,128,768]{2,1,0:T(8,128)(2,1)S(1)}, u32[]{:S(2)}) copy-start(bf16[4,128,768]{2,1,0:T(8,128)(2,1)S(1)} %pad_maximum_fusion.own_ref) | copy-start | bytes 2359300
  49.3 32.8 %copy-start.14 = (bf16[128,128]{1,0:T(8,128)(2,1)S(1)}, bf16[128,128]{1,0:T(8,128)(2,1)}, u32[]{:S(2)}) copy-start(bf16[128,128]{1,0:T(8,128)(2,1)} %cols_ref.3) | copy-start | bytes 98308
  49.3 4.3 %collective-permute-start.4 = (bf16[4,128,768]{2,1,0:T(8,128)(2,1)S(1)}, bf16[4,128,768]{2,1,0:T(8,128)(2,1)S(1)}, u32[]{:S(2)}, u32[]{:S(2)}) collective-permute-start(bf16[4,128,768]{2,1,0:T(8,128)(2,1)S(1)} %pad_maximum_fusion.own_ref), channel_id=1, source_target_pairs={{0,1},{1,0},{2,3},{3,2},{4,5},{5,4},{6,7},{7,6},{8,9},{9,8},{10,11... | collective-permute-start | bytes 2359304 | tf_op jit(solution)/shard_map/ppermute | solution.py:34
  53.6 28.4 %copy-start.2 = (bf16[4,128,768]{2,1,0:T(8,128)(2,1)}, bf16[4,128,768]{2,1,0:T(8,128)(2,1)S(1)}, u32[]{:S(2)}) copy-start(bf16[4,128,768]{2,1,0:T(8,128)(2,1)S(1)} %collective-permute-done.4.grad_ref.other_ref) | copy-start | bytes 2359300
  71.7 28.7 %all-to-all-start.2 = ((s16[256,8,128]{2,1,0:T(8,128)(2,1)}), s16[256,8,128]{2,1,0:T(8,128)(2,1)}, u32[]{:S(2)}, u32[]{:S(2)}) async-start(s16[256,8,128]{2,1,0:T(8,128)(2,1)} %bitcast.17), calls=%async_computation.2 | async-start | bytes 1048576 | tf_op jit(solution)/shard_map/all_to_all | solution.py:30
  82.1 1.4 copy-start.1
  83.5 1.1 copy-start.3
  84.6 1.1 copy-start.5
  100.4 5.1 %collective-permute-start.5 = (s16[2048,128]{1,0:T(8,128)(2,1)}, s16[2048,128]{1,0:T(8,128)(2,1)}, u32[]{:S(2)}, u32[]{:S(2)}) collective-permute-start(s16[2048,128]{1,0:T(8,128)(2,1)} %shard_map.117.codes_ref), channel_id=1, source_target_pairs={{0,1},{1,0},{2,3},{3,2},{4,5},{5,4},{6,7},{7,6},{8,9},{9,8},{10,11... | collective-permute-start | bytes 1572872 | tf_op jit(solution)/shard_map/ppermute | solution.py:34
  104.7 0.9 copy-start.6
  108.4 0.9 copy-start.8
  109.3 14.2 %all-to-all-start.3 = ((s16[8,80,128]{2,1,0:T(8,128)(2,1)}), s16[8,80,128]{2,1,0:T(8,128)(2,1)S(1)}, u32[]{:S(2)}, u32[]{:S(2)}) async-start(s16[8,80,128]{2,1,0:T(8,128)(2,1)} %get-tuple-element.29), calls=%async_computation.3 | async-start | bytes 327680 | tf_op jit(solution)/shard_map/all_to_all | solution.py:30
  124.4 17.4 %all-to-all-start.4 = ((s16[8,80,128]{2,1,0:T(8,128)(2,1)}), s16[8,80,128]{2,1,0:T(8,128)(2,1)S(1)}, u32[]{:S(2)}, u32[]{:S(2)}) async-start(s16[8,80,128]{2,1,0:T(8,128)(2,1)} %shard_map.120), calls=%async_computation.4 | async-start | bytes 327680 | tf_op jit(solution)/shard_map/all_to_all | solution.py:30
  141.8 1.1 copy-start.7
  143.0 1.1 copy-start.9
